TPU v7x, 32 devices: a whole 2x2x4 slice. The times are simulated.
32 devices in a mesh: dp: 4 (over x, core), space: 8 (over z, y).
Axes of the slice: x: 2, y: 2, z: 4, core: 2. Of those that a mesh axis runs over, the one named last changes fastest.
Arguments:
- features: bfloat16 [4, 96, 72, 2048], P('dp', 'space'), may hold values from -0.14355469 to 0.14355469
- grad_out: bfloat16 [4, 96, 72, 256], P('dp', 'space'), may hold values from -6 to 6
- weight: bfloat16 [18432, 256], replicated, may hold values from -0.125 to 0.125
- alive: int32 [4], P('dp'), may hold values from 0 to 1, as said below
Outputs:
- weight_grad: float32 [18432, 256], P(('dp', 'space'))
- grad_features: bfloat16 [4, 96, 72, 2048], P('dp', 'space')
Inputs may be any that keep to these rules, and one draw needn't show every extreme that they name: `alive`: at least one member survives and at least one does not.
All inputs are finite; a program needn't handle non-finite values.
Results may differ from a plain program's by a relative error of at most 0.001.
Values may be sent and summed in bfloat16 or wider, within the bound.
No kernel may reach another device: no remote copies, remote signals or barrier semaphores. Data moves between devices by JAX's collectives and lax.ppermute only.
A program may use at most 320 MiB of HBM per device.

v0:
```python
import jax
import jax.numpy as jnp
from jax import lax
from jax.sharding import PartitionSpec as P

KERNEL_DILATION = 18


def from_behind(value, axis, steps):
    count = lax.axis_size(axis)
    leading, last = (max(0, -steps), min(count, count - steps))
    return lax.ppermute(value, axis, [(source, source + steps) for source in range(leading, last)])


def widen_cols(climate_field):
    return jnp.pad(climate_field, ((0, 0), (0, 0), (KERNEL_DILATION, KERNEL_DILATION), (0, 0)))


def grad_rows(tile):
    rows_per_tile = tile.shape[1]
    halo_tile_count = -(-KERNEL_DILATION // rows_per_tile)
    above_rows = []
    below_rows = []
    for tap_displacement in range(1, halo_tile_count + 1):
        required_rows = min(rows_per_tile, KERNEL_DILATION - (tap_displacement - 1) * rows_per_tile)
        above_rows.insert(
            0, from_behind(tile[:, rows_per_tile - required_rows :], "space", tap_displacement)
        )
        below_rows.append(from_behind(tile[:, :required_rows], "space", -tap_displacement))
    return jnp.concatenate(above_rows + [tile] + below_rows, axis=1)


def feature_rows(tile):
    rows_per_tile = tile.shape[1]
    halo_tile_count = -(-KERNEL_DILATION // rows_per_tile)
    above_rows = []
    below_rows = []
    for tap_displacement in range(1, halo_tile_count + 1):
        required_rows = min(rows_per_tile, KERNEL_DILATION - (tap_displacement - 1) * rows_per_tile)
        above_rows.insert(
            0, from_behind(tile[:, rows_per_tile - required_rows :], "space", tap_displacement)
        )
        below_rows.append(from_behind(tile[:, :required_rows], "space", -tap_displacement))
    return jnp.concatenate(above_rows + [tile] + below_rows, axis=1)


def tap_stack(padded, row_count, col_count, forward):
    views = []
    for tap_index in range(9):
        kernel_tap_row = tap_index // 3
        kernel_tap_column = tap_index % 3
        if forward:
            row_position = kernel_tap_row * KERNEL_DILATION
            column_position = kernel_tap_column * KERNEL_DILATION
        else:
            row_position = (2 - kernel_tap_row) * KERNEL_DILATION
            column_position = (2 - kernel_tap_column) * KERNEL_DILATION
        views.append(
            padded[
                :,
                row_position : row_position + row_count,
                column_position : column_position + col_count,
            ]
        )
    return jnp.stack(views, axis=3)


def shards(features, grad_out, weight, alive):
    members, rows_per_tile, map_width, in_channels = features.shape
    out_channels = grad_out.shape[-1]
    surviving_count = lax.psum(jnp.sum(alive).astype(jnp.float32), "dp")
    member_weighting = alive.astype(jnp.float32) / surviving_count
    pixels = rows_per_tile * map_width
    tap_weights = weight.reshape(in_channels, 9, out_channels)
    gradient_padded = widen_cols(grad_rows(grad_out))
    shifted = tap_stack(gradient_padded, rows_per_tile, map_width, False).reshape(
        members, pixels, 9, out_channels
    )
    input_grad = jnp.einsum(
        "mpto,cto->mpc", shifted, tap_weights, preferred_element_type=jnp.float32
    )
    grad_features = (
        (input_grad * member_weighting[:, None, None]).astype(jnp.bfloat16).reshape(features.shape)
    )
    image_padded = widen_cols(feature_rows(features))
    flat_grad = grad_out.reshape(members, pixels, out_channels)
    rows_total = 9 * in_channels
    chan_count = rows_total // lax.axis_size(("dp", "space")) * lax.axis_size(("dp", "space")) // 9
    stacked = tap_stack(image_padded, rows_per_tile, map_width, True).reshape(
        members, pixels, 9, chan_count
    )
    term = jnp.einsum("mptc,mpo->mcto", stacked, flat_grad, preferred_element_type=jnp.float32)
    weighted = jnp.einsum("mcto,m->cto", term, member_weighting)
    weight_grad = lax.psum_scatter(
        weighted.reshape(chan_count * 9, out_channels),
        ("dp", "space"),
        scatter_dimension=0,
        tiled=True,
    )
    return (weight_grad, grad_features)


def solution(mesh):
    in_specs = (P("dp", "space", None, None), P("dp", "space", None, None), P(), P("dp"))
    out_specs = (P(("dp", "space"), None), P("dp", "space", None, None))
    return jax.shard_map(shards, mesh=mesh, in_specs=in_specs, out_specs=out_specs, check_vma=False)
```

profile of v0, /device:TPU:0, one launch (start us, length us, event | category | flops | bytes accessed | tf_op | source)
XLA Modules:
  0.0 493.7 jit_solution(7642230143571853899)
XLA Ops:
  7.2 6.7 %collective-permute-start.1 = (bf16[1,12,72,2048]{3,2,1,0:T(8,128)(2,1)}, bf16[1,12,72,2048]{3,2,1,0:T(8,128)(2,1)}, u32[]{:S(2)}, u32[]{:S(2)}) collective-permute-start(bf16[1,12,72,2048]{3,2,1,0:T(8,128)(2,1)} %param.4), channel_id=1, source_target_pairs={{0,1},{1,2},{2,3},{3,4},{4,5},{5,6},{6,7},{8,9},{9,10},{10,11},{11... | collective-permute-start | bytes 10616840 | tf_op jit(solution)/shard_map/ppermute | solution.py:12
  15.2 3.6 fusion.12
  18.8 5.0 %collective-permute-start = (bf16[1,6,72,2048]{3,2,1,0:T(8,128)(2,1)S(1)}, bf16[1,6,72,2048]{3,2,1,0:T(8,128)(2,1)}, u32[]{:S(2)}, u32[]{:S(2)}) collective-permute-start(bf16[1,6,72,2048]{3,2,1,0:T(8,128)(2,1)S(1)} %get-tuple-element.13), channel_id=1, source_target_pairs={{0,2},{1,3},{2,4},{3,5},{4,6},{5,7},{8,10},{9,11},{10,12},{11,13},... | collective-permute-start | bytes 5308424 | tf_op jit(solution)/shard_map/ppermute | solution.py:12
  25.7 6.6 %psum.7 = f32[1]{0:T(128)} all-reduce(f32[1]{0:T(128)S(6)} %convert_element_type.15), channel_id=1, replica_groups=mesh['dp'=4,'space'=8] {'dp'}, use_global_device_ids=true, to_apply=%region_0.0 | all-reduce | flops 1 | bytes 8 | tf_op jit(solution)/shard_map/psum | solution.py:71
  33.0 26.8 %collective-permute-done = bf16[1,6,72,2048]{3,2,1,0:T(8,128)(2,1)} collective-permute-done((bf16[1,6,72,2048]{3,2,1,0:T(8,128)(2,1)S(1)}, bf16[1,6,72,2048]{3,2,1,0:T(8,128)(2,1)}, u32[]{:S(2)}, u32[]{:S(2)}) %collective-permute-start) | collective-permute-done | bytes 1769504 | tf_op jit(solution)/shard_map/ppermute | solution.py:12
  61.4 102.6 %collective-permute-done.1 = bf16[1,12,72,2048]{3,2,1,0:T(8,128)(2,1)} collective-permute-done((bf16[1,12,72,2048]{3,2,1,0:T(8,128)(2,1)}, bf16[1,12,72,2048]{3,2,1,0:T(8,128)(2,1)}, u32[]{:S(2)}, u32[]{:S(2)}) %collective-permute-start.1) | collective-permute-done | bytes 3538976 | tf_op jit(solution)/shard_map/ppermute | solution.py:12
  164.0 4.6 pad_maximum_fusion.1
  169.2 4.8 pad_maximum_fusion
  175.5 8.5 %pad_slice_fusion = (bf16[1,12,72,2048]{3,2,1,0:T(8,128)(2,1)S(1)}, bf16[1,12,72,2048]{3,2,1,0:T(8,128)(2,1)}, bf16[1,12,72,2048]{3,2,1,0:T(8,128)(2,1)}, bf16[1...) fusion(bf16[1,48,72,2048]{3,2,1,0:T(8,128)(2,1)S(1)} %constant_dynamic-update, ...), kind=kLoop, calls=%fused_computation.2 | loop fusion | bytes 35389440 | tf_op jit(solution)/shard_map/slice | solution.py:59
  184.1 4.4 constant_dynamic-update-slice_fusion.13
  188.5 2.2 constant_dynamic-update-slice_fusion.12
  191.7 2.3 constant_dynamic-update-slice_fusion.11
  194.0 2.3 constant_dynamic-update-slice_fusion.10
  199.6 2.2 constant_dynamic-update-slice_fusion.8
  205.1 2.1 constant_dynamic-update-slice_fusion.6
  207.2 2.1 constant_dynamic-update-slice_fusion.5
  209.3 19.6 %multiply_bitcast_fusion = f32[1,2048,9,256]{3,1,2,0:T(8,128)} fusion(f32[]{:T(128)} %bitcast.12, bf16[864,256,1]{1,0,2:T(8,128)(2,1)S(1)} %bitcast.53, bf16[1,864,9,2048]{3,1,2,0:T(8,128)(2,1)} %constant_dynamic-update-slice_fusion.5), kind=kOutput, calls=%fused_computation.8 | convolution fusion | flops 8158445568 | bytes 51167236 | tf_op jit(solution)/shard_map/mptc,mpo->mcto/dot_general | solution.py:92
  228.9 23.3 %copy.7 = f32[1,2048,9,256]{3,2,1,0:T(8,128)} copy(f32[1,2048,9,256]{3,1,2,0:T(8,128)} %multiply_bitcast_fusion) | data formatting | bytes 37748736 | tf_op jit(solution)/shard_map/mcto,m->cto/dot_general | solution.py:93
  252.2 26.4 %dot_general.25 = f32[18432,256]{1,0:T(8,128)} reshape(f32[1,2048,9,256]{3,2,1,0:T(8,128)} %copy.7) | data formatting | bytes 37748736 | tf_op jit(solution)/shard_map/mcto,m->cto/dot_general | solution.py:93
  278.7 5.2 %collective-permute-start.5 = (bf16[1,12,72,256]{3,2,1,0:T(8,128)(2,1)S(1)}, bf16[1,12,72,256]{3,2,1,0:T(8,128)(2,1)}, u32[]{:S(2)}, u32[]{:S(2)}) collective-permute-start(bf16[1,12,72,256]{3,2,1,0:T(8,128)(2,1)S(1)} %copy-done.7), channel_id=1, source_target_pairs={{0,1},{1,2},{2,3},{3,4},{4,5},{5,6},{6,7},{8,9},{9,10},{10,11},{11... | collective-permute-start | bytes 1327112 | tf_op jit(solution)/shard_map/ppermute | solution.py:12
  284.5 2.7 collective-permute-start.4
  289.9 19.0 %reshape.84 = bf16[2048,9,256]{2,1,0:T(8,128)(2,1)} reshape(bf16[18432,256]{1,0:T(8,128)(2,1)} %param.6) | data formatting | bytes 18874368 | tf_op jit(solution)/shard_map/reshape | solution.py:74
  320.8 16.3 %fusion.4 = bf16[864,2048]{1,0:T(8,128)(2,1)} fusion(bf16[2048,9,256]{2,1,0:T(8,128)(2,1)S(1)} %copy-done.1, bf16[1,864,9,256]{3,1,2,0:T(8,128)(2,1)} %constant_dynamic-update-slice_fusion.19, f32[]{:T(128)} %bitcast.12), kind=kOutput, calls=%fused_computation.12 | convolution fusion | flops 8157265920 | bytes 16957444 | tf_op jit(solution)/shard_map/mpto,cto->mpc/dot_general | solution.py:79
  337.1 149.7 %reduce-scatter.2.cloned.1.call-done = f32[576,256]{1,0:T(8,128)} async-done(((f32[18432,256]{1,0:T(8,128)}), f32[576,256]{1,0:T(8,128)}) %reduce-scatter.2.cloned.1.call-update) | async-done | bytes 589840 | tf_op jit(solution)/shard_map/reduce_scatter | solution.py:94
  (49 shorter events, 29.0 us)
Async XLA Ops:
  7.2 479.6 %reduce-scatter.2.cloned.1.call-start = ((), (), s32[]{:S(2)}) async-start(), calls=%async_computation.1 | async-start | bytes 19464192 | tf_op jit(solution)/shard_map/reduce_scatter | solution.py:94
  7.2 156.8 %collective-permute-start.1 = (bf16[1,12,72,2048]{3,2,1,0:T(8,128)(2,1)}, bf16[1,12,72,2048]{3,2,1,0:T(8,128)(2,1)}, u32[]{:S(2)}, u32[]{:S(2)}) collective-permute-start(bf16[1,12,72,2048]{3,2,1,0:T(8,128)(2,1)} %param.4), channel_id=1, source_target_pairs={{0,1},{1,2},{2,3},{3,4},{4,5},{5,6},{6,7},{8,9},{9,10},{10,11},{11... | collective-permute-start | bytes 10616840 | tf_op jit(solution)/shard_map/ppermute | solution.py:12
  13.9 155.3 %collective-permute-start.2 = (bf16[1,12,72,2048]{3,2,1,0:T(8,128)(2,1)}, bf16[1,12,72,2048]{3,2,1,0:T(8,128)(2,1)}, u32[]{:S(2)}, u32[]{:S(2)}) collective-permute-start(bf16[1,12,72,2048]{3,2,1,0:T(8,128)(2,1)} %param.4), channel_id=1, source_target_pairs={{1,0},{2,1},{3,2},{4,3},{5,4},{6,5},{7,6},{9,8},{10,9},{11,10},{12... | collective-permute-start | bytes 10616840 | tf_op jit(solution)/shard_map/ppermute | solution.py:12
  18.8 41.0 %collective-permute-start = (bf16[1,6,72,2048]{3,2,1,0:T(8,128)(2,1)S(1)}, bf16[1,6,72,2048]{3,2,1,0:T(8,128)(2,1)}, u32[]{:S(2)}, u32[]{:S(2)}) collective-permute-start(bf16[1,6,72,2048]{3,2,1,0:T(8,128)(2,1)S(1)} %get-tuple-element.13), channel_id=1, source_target_pairs={{0,2},{1,3},{2,4},{3,5},{4,6},{5,7},{8,10},{9,11},{10,12},{11,13},... | collective-permute-start | bytes 5308424 | tf_op jit(solution)/shard_map/ppermute | solution.py:12
  23.7 145.4 %collective-permute-start.3 = (bf16[1,6,72,2048]{3,2,1,0:T(8,128)(2,1)}, bf16[1,6,72,2048]{3,2,1,0:T(8,128)(2,1)}, u32[]{:S(2)}, u32[]{:S(2)}) collective-permute-start(bf16[1,6,72,2048]{3,2,1,0:T(8,128)(2,1)} %get-tuple-element.12), channel_id=1, source_target_pairs={{2,0},{3,1},{4,2},{5,3},{6,4},{7,5},{10,8},{11,9},{12,10},{13,11},... | collective-permute-start | bytes 5308424 | tf_op jit(solution)/shard_map/ppermute | solution.py:12
  61.4 107.3 %copy-start = (bf16[1,12,72,2048]{3,2,1,0:T(8,128)(2,1)S(1)}, bf16[1,12,72,2048]{3,2,1,0:T(8,128)(2,1)}, u32[]{:S(2)}) copy-start(bf16[1,12,72,2048]{3,2,1,0:T(8,128)(2,1)} %param.4) | copy-start | bytes 10616836
  184.1 4.4 copy-start.6
  188.5 3.3 copy-start.4
  190.7 3.3 copy-start.3
  196.3 3.3 copy-start.2
  201.8 3.3 copy-start.5
  207.2 2.1 copy-start.7
  278.7 30.3 %collective-permute-start.5 = (bf16[1,12,72,256]{3,2,1,0:T(8,128)(2,1)S(1)}, bf16[1,12,72,256]{3,2,1,0:T(8,128)(2,1)}, u32[]{:S(2)}, u32[]{:S(2)}) collective-permute-start(bf16[1,12,72,256]{3,2,1,0:T(8,128)(2,1)S(1)} %copy-done.7), channel_id=1, source_target_pairs={{0,1},{1,2},{2,3},{3,4},{4,5},{5,6},{6,7},{8,9},{9,10},{10,11},{11... | collective-permute-start | bytes 1327112 | tf_op jit(solution)/shard_map/ppermute | solution.py:12
  284.5 24.4 %collective-permute-start.4 = (bf16[1,6,72,256]{3,2,1,0:T(8,128)(2,1)S(1)}, bf16[1,6,72,256]{3,2,1,0:T(8,128)(2,1)S(1)}, u32[]{:S(2)}, u32[]{:S(2)}) collective-permute-start(bf16[1,6,72,256]{3,2,1,0:T(8,128)(2,1)S(1)} %get-tuple-element.25), channel_id=1, source_target_pairs={{0,2},{1,3},{2,4},{3,5},{4,6},{5,7},{8,10},{9,11},{10,12},{11,13},... | collective-permute-start | bytes 663560 | tf_op jit(solution)/shard_map/ppermute | solution.py:12
  287.3 23.2 %collective-permute-start.6 = (bf16[1,12,72,256]{3,2,1,0:T(8,128)(2,1)S(1)}, bf16[1,12,72,256]{3,2,1,0:T(8,128)(2,1)}, u32[]{:S(2)}, u32[]{:S(2)}) collective-permute-start(bf16[1,12,72,256]{3,2,1,0:T(8,128)(2,1)S(1)} %copy-done.7), channel_id=1, source_target_pairs={{1,0},{2,1},{3,2},{4,3},{5,4},{6,5},{7,6},{9,8},{10,9},{11,10},{12... | collective-permute-start | bytes 1327112 | tf_op jit(solution)/shard_map/ppermute | solution.py:12
  288.6 21.8 %collective-permute-start.7 = (bf16[1,6,72,256]{3,2,1,0:T(8,128)(2,1)}, bf16[1,6,72,256]{3,2,1,0:T(8,128)(2,1)S(1)}, u32[]{:S(2)}, u32[]{:S(2)}) collective-permute-start(bf16[1,6,72,256]{3,2,1,0:T(8,128)(2,1)} %get-tuple-element.24), channel_id=1, source_target_pairs={{2,0},{3,1},{4,2},{5,3},{6,4},{7,5},{10,8},{11,9},{12,10},{13,11},... | collective-permute-start | bytes 663560 | tf_op jit(solution)/shard_map/ppermute | solution.py:12
  308.9 11.9 %copy-start.1 = (bf16[2048,9,256]{2,1,0:T(8,128)(2,1)S(1)}, bf16[2048,9,256]{2,1,0:T(8,128)(2,1)}, u32[]{:S(2)}) copy-start(bf16[2048,9,256]{2,1,0:T(8,128)(2,1)} %reshape.84) | copy-start | bytes 28311556
Sparse Core Ops, SparseCore 0:
  278.8 207.9 reduce-scatter.1
where the time goes:
time: 495 us; the launch traced here: 494 us
  waiting for transfers between devices  279 us (56%)
  local copies, waits for them, and re-layouts  119 us (24%)
  matrix products  35.9 us (7%)
  starting transfers between devices  24.7 us (5%)
  between operations  15.5 us (3%)
  other arithmetic  12.7 us (3%)
  blocking collectives  6.65 us (1%)
    reduce_scatter x1, waiting for transfers between devices, shards(): lax.psum_scatter(weighted.reshape(chan_count * 9, out_channels), ('dp', '...  150 us
    ppermute x8, waiting for transfers between devices, from_behind(): lax.ppermute(value, axis, [(source, source + steps) for source in range(l...  129 us
    dot_general x2, local copies, waits for them, and re-layouts, shards(): weighted = jnp.einsum('mcto,m->cto', term, member_weighting)  49.7 us
    unnamed x36, local copies, waits for them, and re-layouts  31.6 us
    ppermute x8, starting transfers between devices, from_behind(): lax.ppermute(value, axis, [(source, source + steps) for source in range(l...  24.7 us
    dot_general x1, matrix products, shards(): jnp.einsum('mptc,mpo->mcto', stacked, flat_grad, preferred_element_type=j...  19.6 us
    reshape x1, local copies, waits for them, and re-layouts, shards(): tap_weights = weight.reshape(in_channels, 9, out_channels)  19 us
    dot_general x1, matrix products, shards(): jnp.einsum('mpto,cto->mpc', shifted, tap_weights, preferred_element_type=...  16.3 us
  transfers between devices with their start and end apart: 9, of which 3 were waited for; matrix products, arithmetic and copies ran while one was open for 12% of the time, Pallas kernels for 0%

commit v1 on v0

v1 whole, which is shorter than its diff:
```python
import functools

import jax
import jax.numpy as jnp
from jax import lax
from jax.experimental import pallas as pl
from jax.experimental.pallas import tpu as pltpu
from jax.sharding import PartitionSpec as P

KERNEL_DILATION = 18
CHANNELS_PER_STEP = 256
F32, F16, BF16 = jnp.float32, jnp.float16, jnp.bfloat16


def from_behind(value, axis, steps):
    count = lax.axis_size(axis)
    leading, last = (max(0, -steps), min(count, count - steps))
    return lax.ppermute(value, axis, [(source, source + steps) for source in range(leading, last)])


def exchange(value, axis, bit):
    return lax.ppermute(value, axis, [(i, i ^ bit) for i in range(lax.axis_size(axis))])


def halo_rows(tile):
    rows = tile.shape[0]
    away, rest = divmod(KERNEL_DILATION, rows)
    below = [from_behind(tile[rest:], "space", -away)]
    above = [from_behind(tile[: rows - rest], "space", away)]
    if rest:
        below.append(from_behind(tile[:rest], "space", -away - 1))
        above.insert(0, from_behind(tile[rows - rest :], "space", away + 1))
    return jnp.concatenate(below), jnp.concatenate(above)


def shift_kernel(columns, *refs):
    out_ref = refs[-1]
    for j, ref in enumerate(refs[:-1]):
        value = ref[...].astype(F32)
        pixels, width = value.shape
        place = lax.broadcasted_iota(jnp.int32, (pixels, width), 0).astype(F32)
        column = place - jnp.floor((place + 0.5) * (1.0 / columns)) * columns
        ahead = pltpu.roll(value, pixels - KERNEL_DILATION, 0)
        behind = pltpu.roll(value, KERNEL_DILATION, 0)
        ahead = jnp.where(column < columns - KERNEL_DILATION, ahead, 0.0)
        behind = jnp.where(column >= KERNEL_DILATION, behind, 0.0)
        base = 3 * j * width
        out_ref[:, base : base + width] = ahead.astype(BF16)
        out_ref[:, base + width : base + 2 * width] = ref[...]
        out_ref[:, base + 2 * width : base + 3 * width] = behind.astype(BF16)


def column_taps(columns, *maps):
    pixels, width = maps[0].shape
    return pl.pallas_call(
        functools.partial(shift_kernel, columns),
        out_shape=jax.ShapeDtypeStruct((pixels, 3 * len(maps) * width), BF16),
        compiler_params=pltpu.CompilerParams(vmem_limit_bytes=40 << 20),
        cost_estimate=pl.CostEstimate(
            flops=0, bytes_accessed=8 * len(maps) * pixels * width, transcendentals=0
        ),
        name="column_taps",
    )(*maps)


def input_grad_kernel(scale_ref, middle_ref, outer_ref, weight_ref, out_ref, wide_ref, taps_ref):
    step = out_ref.shape[1]
    width = weight_ref.shape[1]
    halves = width // 128
    for h in range(halves):
        wide_ref[h] = weight_ref[:, h * 128 : (h + 1) * 128].astype(F32)
    for t in range(9):
        for h in range(halves):
            base = t * width + h * 128
            taps_ref[:, base : base + 128] = wide_ref[h, pl.ds(t, step, stride=9), :].astype(BF16)
    third = 3 * width

    def product(shifted, taps):
        return lax.dot_general(shifted, taps, (((1,), (1,)), ((), ())), preferred_element_type=F32)

    total = product(outer_ref[:, :third], taps_ref[:, :third])
    total += product(middle_ref[...], taps_ref[:, third : 2 * third])
    total += product(outer_ref[:, third:], taps_ref[:, 2 * third :])
    out_ref[...] = (total * scale_ref[0]).astype(BF16)


def input_grad(scale, middle, outer, weight):
    pixels = middle.shape[0]
    rows, width = weight.shape
    channels = rows // 9
    step = CHANNELS_PER_STEP
    return pl.pallas_call(
        input_grad_kernel,
        grid=(channels // step,),
        in_specs=[
            pl.BlockSpec(memory_space=pltpu.SMEM),
            pl.BlockSpec(middle.shape, lambda i: (0, 0)),
            pl.BlockSpec(outer.shape, lambda i: (0, 0)),
            pl.BlockSpec((9 * step, width), lambda i: (i, 0)),
        ],
        out_specs=pl.BlockSpec((pixels, step), lambda i: (0, i)),
        out_shape=jax.ShapeDtypeStruct((pixels, channels), BF16),
        scratch_shapes=[
            pltpu.VMEM((width // 128, 9 * step, 128), F32),
            pltpu.VMEM((step, 9 * width), BF16),
        ],
        compiler_params=pltpu.CompilerParams(vmem_limit_bytes=48 << 20),
        cost_estimate=pl.CostEstimate(
            flops=2 * pixels * rows * width,
            bytes_accessed=2 * (rows * width + pixels * channels + 9 * pixels * width),
            transcendentals=0,
        ),
        name="input_grad",
    )(scale, middle, outer, weight)


def bits_of(axis):
    return [(axis, 1 << k) for k in reversed(range(lax.axis_size(axis).bit_length() - 1))]


def my_bit(axis, bit):
    return (lax.axis_index(axis) // bit) % 2


def pick(value, position, index):
    return lax.dynamic_index_in_dim(value, index, position, keepdims=False)


def scatter_sum(part, names, order):
    names = list(names)
    for name in order:
        position = names.index(name)
        mine = my_bit(*name)
        sent = exchange(pick(part, position, 1 - mine).astype(F16), *name)
        part = pick(part, position, mine).astype(F32) + sent.astype(F32)
        names.pop(position)
    return part


def shards(features, grad_out, weight, alive):
    _, rows, columns, in_channels = features.shape
    out_channels = grad_out.shape[-1]
    pixels = rows * columns
    member_count = lax.axis_size("dp")
    names = bits_of("dp") + bits_of("space")
    core = ("dp", 1)
    others = [name for name in names if name != core]
    dp_high = [name for name in others if name[0] == "dp"]
    space_low = [name for name in others if name[0] == "space"][::-1]

    own_alive = jnp.sum(alive).astype(F32)
    tile = grad_out.reshape(rows, columns, out_channels)
    below, above = halo_rows(tile)
    survivors = own_alive.reshape(1)
    for name in bits_of("dp"):
        survivors = survivors + exchange(survivors, *name)

    term_scale = own_alive * (4.0 / member_count)
    middle = column_taps(columns, tile.reshape(pixels, out_channels))
    outer = column_taps(
        columns, below.reshape(pixels, out_channels), above.reshape(pixels, out_channels)
    )

    cut = features.reshape(pixels, member_count // 2, 2, in_channels // member_count)
    mine = my_bit(*core)
    kept = pick(cut, 2, mine).reshape(pixels, in_channels // 2)
    given = pick(cut, 2, 1 - mine).reshape(pixels, in_channels // 2)

    def term(image, shifted):
        product = lax.dot_general(
            image, shifted, (((0,), (0,)), ((), ())), preferred_element_type=F32
        )
        return product * term_scale

    def pair_sum(shifted):
        sent = exchange(term(given, shifted).astype(F16), *core)
        total = term(kept, shifted) + sent.astype(F32)
        return total.reshape((2,) * len(others) + (-1, shifted.shape[1]))

    y_first = space_low[:1] + space_low[1:] + dp_high
    z_first = space_low[1:] + dp_high + space_low[:1]
    x_first = dp_high + space_low
    width = out_channels
    centre = scatter_sum(pair_sum(middle), others, x_first)
    ring = pair_sum(outer)
    upper = scatter_sum(ring[..., : 3 * width], others, x_first)
    lower = scatter_sum(ring[..., 3 * width : 5 * width], others, y_first)
    last = scatter_sum(ring[..., 5 * width :], others, z_first)
    final = jnp.concatenate([upper, centre, lower, last], axis=1)
    final = final * (member_count * 0.25 / survivors)
    weight_grad = final.reshape(-1, out_channels)

    grad_features = input_grad(own_alive / survivors, middle, outer, weight).reshape(features.shape)
    return (weight_grad, grad_features)


def solution(mesh):
    in_specs = (P("dp", "space", None, None), P("dp", "space", None, None), P(), P("dp"))
    out_specs = (P(("dp", "space"), None), P("dp", "space", None, None))
    return jax.shard_map(shards, mesh=mesh, in_specs=in_specs, out_specs=out_specs, check_vma=False)
```

time: 495 us -> 170 us (0.34)
  waiting for transfers between devices: 279 us -> 36.6 us
  local copies, waits for them, and re-layouts: 119 us -> 39.3 us
  starting transfers between devices: 24.7 us -> 54.2 us
  matrix products: 35.9 us -> 16.4 us
  Pallas kernels: 0 us -> 15.3 us
  between operations: 15.5 us -> 3.09 us
  other arithmetic: 12.7 us -> 3.77 us
  blocking collectives: 6.65 us -> 0 us
    reduce_scatter x1 -> x0, waiting for transfers between devices: 150 us -> none  [shards(): lax.psum_scatter(weighted.reshape(chan_count * 9, out_channels), ('dp', '...]
    ppermute x8 -> x4, waiting for transfers between devices: 129 us -> 0.01 us  [from_behind(): lax.ppermute(value, axis, [(source, source + steps) for source in range(l...]
    dot_general x2 -> x0, local copies, waits for them, and re-layouts: 49.7 us -> none  [shards(): weighted = jnp.einsum('mcto,m->cto', term, member_weighting)]
    ppermute x0 -> x20, starting transfers between devices: none -> 41.8 us  [exchange(): lax.ppermute(value, axis, [(i, i ^ bit) for i in range(lax.axis_size(axis...]
    ppermute x0 -> x20, waiting for transfers between devices: none -> 36.6 us  [exchange(): lax.ppermute(value, axis, [(i, i ^ bit) for i in range(lax.axis_size(axis...]
    dot_general x2 -> x4, matrix products: 35.9 us -> 16.4 us  [term(): lax.dot_general(image, shifted, (((0,), (0,)), ((), ())), preferred_eleme...]
    pallas_call x0 -> x3, Pallas kernels: none -> 15.3 us  [the longest x1 14.2 us: input_grad(): pl.pallas_call(input_grad_kernel, grid=(channels // step,), in_specs=[pl....]
    slice x4, local copies, waits for them, and re-layouts: 14.1 us -> 0.59 us  [the longest x1 0.28 us: shards(): upper = scatter_sum(ring[..., :3 * width], others, x_first)]
  transfers between devices with their start and end apart: 9 -> 24, of which waited for: 3 -> 11; matrix products, arithmetic and copies ran while one was open for 12% -> 17% of each run, Pallas kernels for 0% -> 9%
where the time goes in v1:
time: 170 us; the launch traced here: 169 us
  starting transfers between devices  54.2 us (32%)
  local copies, waits for them, and re-layouts  39.3 us (23%)
  waiting for transfers between devices  36.6 us (22%)
  matrix products  16.4 us (10%)
  Pallas kernels  15.3 us (9%)
  other arithmetic  3.77 us (2%)
  between operations  3.09 us (2%)
    ppermute x20, starting transfers between devices, exchange(): lax.ppermute(value, axis, [(i, i ^ bit) for i in range(lax.axis_size(axis...  41.8 us
    ppermute x20, waiting for transfers between devices, exchange(): lax.ppermute(value, axis, [(i, i ^ bit) for i in range(lax.axis_size(axis...  36.6 us
    unnamed x18, local copies, waits for them, and re-layouts  18.3 us
    dot_general x4, matrix products, term(): lax.dot_general(image, shifted, (((0,), (0,)), ((), ())), preferred_eleme...  16.4 us
    pallas_call x1, Pallas kernels, input_grad(): pl.pallas_call(input_grad_kernel, grid=(channels // step,), in_specs=[pl....  14.2 us
    ppermute x4, starting transfers between devices, from_behind(): lax.ppermute(value, axis, [(source, source + steps) for source in range(l...  12.4 us
    dynamic_slice x2, local copies, waits for them, and re-layouts, pick(): return lax.dynamic_index_in_dim(value, index, position, keepdims=False)  11.6 us
    reshape x1, local copies, waits for them, and re-layouts, shards(): features.reshape(pixels, member_count // 2, 2, in_channels // member_count)  7.87 us
  transfers between devices with their start and end apart: 24, of which 11 were waited for; matrix products, arithmetic and copies ran while one was open for 17% of the time, Pallas kernels for 9%

profile of v1, /device:TPU:0, one launch (start us, length us, event | category | flops | bytes accessed | tf_op | source)
XLA Modules:
  0.0 168.7 jit_solution(1022776004679756545)
XLA Ops:
  0.6 7.9 %reshape.58 = bf16[864,2,2,512]{3,2,1,0:T(2,128)(2,1)S(1)} reshape(bf16[1,12,72,2048]{3,2,1,0:T(8,128)(2,1)} %param.4) | data formatting | bytes 7077888 | tf_op jit(solution)/shard_map/reshape | solution.py:164
  8.5 10.2 %constant_dynamic-slice_fusion.3 = (bf16[864,2,1,512]{3,2,1,0:T(2,128)(2,1)}, bf16[864,2,1,512]{3,2,1,0:T(2,128)(2,1)}) fusion(bf16[864,2,2,512]{3,2,1,0:T(2,128)(2,1)S(1)} %reshape.58, s32[]{:T(128)S(6)} %select_n.139, s32[]{:T(128)S(6)} %select_n.140), kind=kLoop, calls=%fused_computation.60 | loop fusion | bytes 7077896 | tf_op jit(solution)/shard_map/jit(dynamic_index_in_dim)/dynamic_slice | solution.py:126
  18.7 8.1 %copy.13 = bf16[864,2,1,512]{0,3,1,2:T(8,128)(2,1)S(1)} copy(bf16[864,2,1,512]{3,2,1,0:T(2,128)(2,1)} %get-tuple-element.3) | data formatting | bytes 3538944
  28.0 3.0 %multiply_convert_fusion.1 = f16[1024,768]{1,0:T(8,128)(2,1)} fusion(bf16[864,1024]{0,1:T(8,128)(2,1)S(1)} %bitcast.97, bf16[864,768]{1,0:T(8,128)(2,1)S(1)} %column_taps.3.middle_ref, f32[]{:T(128)} %bitcast.5), kind=kOutput, calls=%fused_computation.3 | convolution fusion | flops 1360527360 | bytes 4669444 | tf_op jit(solution)/shard_map/dot_general | solution.py:170
  34.1 5.1 %collective-permute-start.3 = (bf16[6,72,256]{2,1,0:T(8,128)(2,1)S(1)}, bf16[6,72,256]{2,1,0:T(8,128)(2,1)S(1)}, u32[]{:S(2)}, u32[]{:S(2)}) collective-permute-start(bf16[6,72,256]{2,1,0:T(8,128)(2,1)S(1)} %get-tuple-element.7), channel_id=1, source_target_pairs={{0,1},{1,2},{2,3},{3,4},{4,5},{5,6},{6,7},{8,9},{9,10},{10,11},{11... | collective-permute-start | bytes 663560 | tf_op jit(solution)/shard_map/ppermute | solution.py:18
  39.1 4.8 %collective-permute-start.2 = (bf16[6,72,256]{2,1,0:T(8,128)(2,1)S(1)}, bf16[6,72,256]{2,1,0:T(8,128)(2,1)S(1)}, u32[]{:S(2)}, u32[]{:S(2)}) collective-permute-start(bf16[6,72,256]{2,1,0:T(8,128)(2,1)S(1)} %get-tuple-element.6), channel_id=1, source_target_pairs={{0,2},{1,3},{2,4},{3,5},{4,6},{5,7},{8,10},{9,11},{10,12},{11,13},... | collective-permute-start | bytes 663560 | tf_op jit(solution)/shard_map/ppermute | solution.py:18
  44.0 9.5 %copy.12 = bf16[864,2,1,512]{0,3,1,2:T(8,128)(2,1)} copy(bf16[864,2,1,512]{3,2,1,0:T(2,128)(2,1)} %get-tuple-element.2) | data formatting | bytes 3538944
  55.0 4.8 %multiply_convert_fusion = f16[1024,1536]{1,0:T(8,128)(2,1)} fusion(bf16[864,1024]{0,1:T(8,128)(2,1)S(1)} %bitcast.98, bf16[864,1536]{1,0:T(8,128)(2,1)S(1)} %column_taps.2.outer_ref, f32[]{:T(128)} %bitcast.5), kind=kOutput, calls=%fused_computation.1 | convolution fusion | flops 2721054720 | bytes 7569412 | tf_op jit(solution)/shard_map/dot_general | solution.py:170
  59.9 3.2 %convert_add_fusion.1 = f32[1024,768]{1,0:T(8,128)S(1)} fusion(f16[1024,768]{1,0:T(8,128)(2,1)} %collective-permute-done.9, bf16[864,1024]{0,1:T(8,128)(2,1)S(1)} %bitcast.95, bf16[864,768]{1,0:T(8,128)(2,1)S(1)} %copy-done.2, f32[]{:T(128)} %bitcast.5), kind=kOutput, calls=%fused_computation.2 | convolution fusion | flops 1361313792 | bytes 7815172 | tf_op jit(solution)/shard_map/dot_general | solution.py:170
  64.6 2.0 %collective-permute-start.10 = (f16[2,2,2,64,768]{4,3,0,1,2:T(8,128)(2,1)S(1)}, f16[2,2,2,64,768]{4,3,0,1,2:T(8,128)(2,1)}, u32[]{:S(2)}, u32[]{:S(2)}) collective-permute-start(f16[2,2,2,64,768]{4,3,0,1,2:T(8,128)(2,1)S(1)} %fusion.1), channel_id=1, source_target_pairs={{0,16},{8,24},{16,0},{24,8},{1,17},{9,25},{17,1},{25,9},{2,18},{10... | collective-permute-start | bytes 2359304 | tf_op jit(solution)/shard_map/ppermute | solution.py:22
  66.5 17.5 %collective-permute-start.22 = (f32[1]{0:T(128)}, f32[1]{0:T(128)}, u32[]{:S(2)}, u32[]{:S(2)}) collective-permute-start(f32[1]{0:T(128)} %convert_element_type.162), channel_id=1, source_target_pairs={{0,16},{8,24},{16,0},{24,8},{1,17},{9,25},{17,1},{25,9},{2,18},{10... | collective-permute-start | bytes 20 | tf_op jit(solution)/shard_map/ppermute | solution.py:22
  87.4 1.9 %bitcast_add_fusion = f32[2,2,2,64,768]{4,3,0,1,2:T(8,128)S(1)} fusion(f32[1,2,2,2,64,768]{5,4,3,2,1,0:T(8,128)} %get-tuple-element.5, f16[2,2,2,64,768]{4,3,0,1,2:T(8,128)(2,1)} %collective-permute-done.10), kind=kLoop, calls=%fused_computation.5 | loop fusion | flops 786432 | bytes 3932160 | tf_op jit(solution)/shard_map/add | solution.py:135
  89.3 2.7 %collective-permute-start.11 = (f16[2,2,64,768]{3,2,0,1:T(8,128)(2,1)S(1)}, f16[2,2,64,768]{3,2,0,1:T(8,128)(2,1)S(1)}, u32[]{:S(2)}, u32[]{:S(2)}) collective-permute-start(f16[2,2,64,768]{3,2,0,1:T(8,128)(2,1)S(1)} %fusion.4), channel_id=1, source_target_pairs={{0,1},{1,0},{2,3},{3,2},{4,5},{5,4},{6,7},{7,6},{8,9},{9,8},{10,11... | collective-permute-start | bytes 1179656 | tf_op jit(solution)/shard_map/ppermute | solution.py:22
  92.1 14.2 %input_grad.1 = bf16[864,2048]{1,0:T(8,128)(2,1)} custom-call(f32[1]{0:T(128)S(6)} %div.53.scale_ref, bf16[864,768]{1,0:T(8,128)(2,1)S(1)} %copy-done.3, bf16[864,1536]{1,0:T(8,128)(2,1)S(1)} %column_taps.2.outer_ref, bf16[18432,256]{1,0:T(8,128)(2,1)} %weight_ref.1), custom_call_target="tpu_custom_call" | custom-call | flops 8153726976 | bytes 16957440 | tf_op jit(solution)/shard_map/input_grad/pallas_call | solution.py:92
  108.1 5.3 %convert_add_fusion = f32[1024,1536]{1,0:T(8,128)S(1)} fusion(f16[1024,1536]{1,0:T(8,128)(2,1)} %collective-permute-done.4, bf16[864,1024]{0,1:T(8,128)(2,1)S(1)} %bitcast.96, bf16[864,1536]{1,0:T(8,128)(2,1)S(1)} %column_taps.2.outer_ref, f32[]{:T(128)} %bitcast.5), kind=kOutput, calls=%fused_computation | convolution fusion | flops 2722627584 | bytes 13860868 | tf_op jit(solution)/shard_map/dot_general | solution.py:170
  117.1 6.5 %collective-permute-done.18 = f16[2,2,2,64,256]{4,3,2,1,0:T(8,128)(2,1)S(1)} collective-permute-done((f16[2,2,2,64,256]{4,3,2,1,0:T(8,128)(2,1)S(1)}, f16[2,2,2,64,256]{4,3,2,1,0:T(8,128)(2,1)S(1)}, u32[]{:S(2)}, u32[]{:S(2)}) %collective-permute-start.18) | collective-permute-done | bytes 262176 | tf_op jit(solution)/shard_map/ppermute | solution.py:22
  125.5 5.5 %collective-permute-done.19 = f16[2,2,64,256]{3,2,1,0:T(8,128)(2,1)S(1)} collective-permute-done((f16[2,2,64,256]{3,2,1,0:T(8,128)(2,1)S(1)}, f16[2,2,64,256]{3,2,1,0:T(8,128)(2,1)S(1)}, u32[]{:S(2)}, u32[]{:S(2)}) %collective-permute-start.19) | collective-permute-done | bytes 131104 | tf_op jit(solution)/shard_map/ppermute | solution.py:22
  132.6 11.0 %collective-permute-done.20 = f16[2,64,256]{2,1,0:T(8,128)(2,1)S(1)} collective-permute-done((f16[2,64,256]{2,1,0:T(8,128)(2,1)S(1)}, f16[2,64,256]{2,1,0:T(8,128)(2,1)S(1)}, u32[]{:S(2)}, u32[]{:S(2)}) %collective-permute-start.20) | collective-permute-done | bytes 65568 | tf_op jit(solution)/shard_map/ppermute | solution.py:22
  144.6 1.8 %collective-permute-start.15 = (f16[2,2,64,512]{3,2,1,0:T(8,128)(2,1)S(1)}, f16[2,2,64,512]{3,2,1,0:T(8,128)(2,1)S(1)}, u32[]{:S(2)}, u32[]{:S(2)}) collective-permute-start(f16[2,2,64,512]{3,2,1,0:T(8,128)(2,1)S(1)} %fusion.5), channel_id=1, source_target_pairs={{0,2},{1,3},{2,0},{3,1},{4,6},{5,7},{6,4},{7,5},{8,10},{9,11},{10,... | collective-permute-start | bytes 786440 | tf_op jit(solution)/shard_map/ppermute | solution.py:22
  148.0 3.1 %collective-permute-done.15 = f16[2,2,64,512]{3,2,1,0:T(8,128)(2,1)S(1)} collective-permute-done((f16[2,2,64,512]{3,2,1,0:T(8,128)(2,1)S(1)}, f16[2,2,64,512]{3,2,1,0:T(8,128)(2,1)S(1)}, u32[]{:S(2)}, u32[]{:S(2)}) %collective-permute-start.15) | collective-permute-done | bytes 262176 | tf_op jit(solution)/shard_map/ppermute | solution.py:22
  151.2 3.4 %collective-permute-start.16 = (f16[2,64,512]{2,1,0:T(8,128)(2,1)S(1)}, f16[2,64,512]{2,1,0:T(8,128)(2,1)S(1)}, u32[]{:S(2)}, u32[]{:S(2)}) collective-permute-start(f16[2,64,512]{2,1,0:T(8,128)(2,1)S(1)} %fusion.9), channel_id=1, source_target_pairs={{0,4},{1,5},{2,6},{3,7},{4,0},{5,1},{6,2},{7,3},{8,12},{9,13},{10,... | collective-permute-start | bytes 393224 | tf_op jit(solution)/shard_map/ppermute | solution.py:22
  155.7 2.6 %collective-permute-done.16 = f16[2,64,512]{2,1,0:T(8,128)(2,1)S(1)} collective-permute-done((f16[2,64,512]{2,1,0:T(8,128)(2,1)S(1)}, f16[2,64,512]{2,1,0:T(8,128)(2,1)S(1)}, u32[]{:S(2)}, u32[]{:S(2)}) %collective-permute-start.16) | collective-permute-done | bytes 131104 | tf_op jit(solution)/shard_map/ppermute | solution.py:22
  161.1 1.8 %collective-permute-start.8 = (f16[64,768]{1,0:T(8,128)(2,1)S(1)}, f16[64,768]{1,0:T(8,128)(2,1)S(1)}, u32[]{:S(2)}, u32[]{:S(2)}) collective-permute-start(f16[64,768]{1,0:T(8,128)(2,1)S(1)} %fusion.11), channel_id=1, source_target_pairs={{0,4},{1,5},{2,6},{3,7},{4,0},{5,1},{6,2},{7,3},{8,12},{9,13},{10,... | collective-permute-start | bytes 294920 | tf_op jit(solution)/shard_map/ppermute | solution.py:22
  162.9 4.8 %collective-permute-done.8 = f16[64,768]{1,0:T(8,128)(2,1)S(1)} collective-permute-done((f16[64,768]{1,0:T(8,128)(2,1)S(1)}, f16[64,768]{1,0:T(8,128)(2,1)S(1)}, u32[]{:S(2)}, u32[]{:S(2)}) %collective-permute-start.8) | collective-permute-done | bytes 98336 | tf_op jit(solution)/shard_map/ppermute | solution.py:22
  (92 shorter events, 24.9 us)
Async XLA Ops:
  31.0 28.9 %collective-permute-start.9 = (f16[1024,768]{1,0:T(8,128)(2,1)}, f16[1024,768]{1,0:T(8,128)(2,1)}, u32[]{:S(2)}, u32[]{:S(2)}) collective-permute-start(f16[1024,768]{1,0:T(8,128)(2,1)} %multiply_convert_fusion.1), channel_id=1, source_target_pairs={{0,8},{8,0},{16,24},{24,16},{1,9},{9,1},{17,25},{25,17},{2,10},{10... | collective-permute-start | bytes 4718600 | tf_op jit(solution)/shard_map/ppermute | solution.py:22
  31.5 22.0 %collective-permute-start.1 = (bf16[6,72,256]{2,1,0:T(8,128)(2,1)S(1)}, bf16[6,72,256]{2,1,0:T(8,128)(2,1)S(1)}, u32[]{:S(2)}, u32[]{:S(2)}) collective-permute-start(bf16[6,72,256]{2,1,0:T(8,128)(2,1)S(1)} %get-tuple-element.7), channel_id=1, source_target_pairs={{2,0},{3,1},{4,2},{5,3},{6,4},{7,5},{10,8},{11,9},{12,10},{13,11},... | collective-permute-start | bytes 663560 | tf_op jit(solution)/shard_map/ppermute | solution.py:18
  32.8 20.7 %collective-permute-start = (bf16[6,72,256]{2,1,0:T(8,128)(2,1)S(1)}, bf16[6,72,256]{2,1,0:T(8,128)(2,1)S(1)}, u32[]{:S(2)}, u32[]{:S(2)}) collective-permute-start(bf16[6,72,256]{2,1,0:T(8,128)(2,1)S(1)} %get-tuple-element.6), channel_id=1, source_target_pairs={{1,0},{2,1},{3,2},{4,3},{5,4},{6,5},{7,6},{9,8},{10,9},{11,10},{12... | collective-permute-start | bytes 663560 | tf_op jit(solution)/shard_map/ppermute | solution.py:18
  34.1 19.4 %collective-permute-start.3 = (bf16[6,72,256]{2,1,0:T(8,128)(2,1)S(1)}, bf16[6,72,256]{2,1,0:T(8,128)(2,1)S(1)}, u32[]{:S(2)}, u32[]{:S(2)}) collective-permute-start(bf16[6,72,256]{2,1,0:T(8,128)(2,1)S(1)} %get-tuple-element.7), channel_id=1, source_target_pairs={{0,1},{1,2},{2,3},{3,4},{4,5},{5,6},{6,7},{8,9},{9,10},{10,11},{11... | collective-permute-start | bytes 663560 | tf_op jit(solution)/shard_map/ppermute | solution.py:18
  39.1 14.4 %collective-permute-start.2 = (bf16[6,72,256]{2,1,0:T(8,128)(2,1)S(1)}, bf16[6,72,256]{2,1,0:T(8,128)(2,1)S(1)}, u32[]{:S(2)}, u32[]{:S(2)}) collective-permute-start(bf16[6,72,256]{2,1,0:T(8,128)(2,1)S(1)} %get-tuple-element.6), channel_id=1, source_target_pairs={{0,2},{1,3},{2,4},{3,5},{4,6},{5,7},{8,10},{9,11},{10,12},{11,13},... | collective-permute-start | bytes 663560 | tf_op jit(solution)/shard_map/ppermute | solution.py:18
  59.8 48.2 %collective-permute-start.4 = (f16[1024,1536]{1,0:T(8,128)(2,1)}, f16[1024,1536]{1,0:T(8,128)(2,1)}, u32[]{:S(2)}, u32[]{:S(2)}) collective-permute-start(f16[1024,1536]{1,0:T(8,128)(2,1)} %multiply_convert_fusion), channel_id=1, source_target_pairs={{0,8},{8,0},{16,24},{24,16},{1,9},{9,1},{17,25},{25,17},{2,10},{10... | collective-permute-start | bytes 9437192 | tf_op jit(solution)/shard_map/ppermute | solution.py:22
  64.6 22.8 %collective-permute-start.10 = (f16[2,2,2,64,768]{4,3,0,1,2:T(8,128)(2,1)S(1)}, f16[2,2,2,64,768]{4,3,0,1,2:T(8,128)(2,1)}, u32[]{:S(2)}, u32[]{:S(2)}) collective-permute-start(f16[2,2,2,64,768]{4,3,0,1,2:T(8,128)(2,1)S(1)} %fusion.1), channel_id=1, source_target_pairs={{0,16},{8,24},{16,0},{24,8},{1,17},{9,25},{17,1},{25,9},{2,18},{10... | collective-permute-start | bytes 2359304 | tf_op jit(solution)/shard_map/ppermute | solution.py:22
  66.5 18.3 %collective-permute-start.22 = (f32[1]{0:T(128)}, f32[1]{0:T(128)}, u32[]{:S(2)}, u32[]{:S(2)}) collective-permute-start(f32[1]{0:T(128)} %convert_element_type.162), channel_id=1, source_target_pairs={{0,16},{8,24},{16,0},{24,8},{1,17},{9,25},{17,1},{25,9},{2,18},{10... | collective-permute-start | bytes 20 | tf_op jit(solution)/shard_map/ppermute | solution.py:22
  85.5 1.2 collective-permute-start.23
  89.3 17.0 %collective-permute-start.11 = (f16[2,2,64,768]{3,2,0,1:T(8,128)(2,1)S(1)}, f16[2,2,64,768]{3,2,0,1:T(8,128)(2,1)S(1)}, u32[]{:S(2)}, u32[]{:S(2)}) collective-permute-start(f16[2,2,64,768]{3,2,0,1:T(8,128)(2,1)S(1)} %fusion.4), channel_id=1, source_target_pairs={{0,1},{1,0},{2,3},{3,2},{4,5},{5,4},{6,7},{7,6},{8,9},{9,8},{10,11... | collective-permute-start | bytes 1179656 | tf_op jit(solution)/shard_map/ppermute | solution.py:22
  106.4 8.5 %collective-permute-start.12 = (f16[2,64,768]{2,1,0:T(8,128)(2,1)S(1)}, f16[2,64,768]{2,1,0:T(8,128)(2,1)S(1)}, u32[]{:S(2)}, u32[]{:S(2)}) collective-permute-start(f16[2,64,768]{2,1,0:T(8,128)(2,1)S(1)} %fusion.8), channel_id=1, source_target_pairs={{0,2},{1,3},{2,0},{3,1},{4,6},{5,7},{6,4},{7,5},{8,10},{9,11},{10,... | collective-permute-start | bytes 589832 | tf_op jit(solution)/shard_map/ppermute | solution.py:22
  113.6 10.1 %collective-permute-start.18 = (f16[2,2,2,64,256]{4,3,2,1,0:T(8,128)(2,1)S(1)}, f16[2,2,2,64,256]{4,3,2,1,0:T(8,128)(2,1)S(1)}, u32[]{:S(2)}, u32[]{:S(2)}) collective-permute-start(f16[2,2,2,64,256]{4,3,2,1,0:T(8,128)(2,1)S(1)} %fusion.6), channel_id=1, source_target_pairs={{0,2},{1,3},{2,0},{3,1},{4,6},{5,7},{6,4},{7,5},{8,10},{9,11},{10,... | collective-permute-start | bytes 786440 | tf_op jit(solution)/shard_map/ppermute | solution.py:22
  115.0 17.6 %collective-permute-start.13 = (f16[64,768]{1,0:T(8,128)(2,1)S(1)}, f16[64,768]{1,0:T(8,128)(2,1)S(1)}, u32[]{:S(2)}, u32[]{:S(2)}) collective-permute-start(f16[64,768]{1,0:T(8,128)(2,1)S(1)} %fusion.12), channel_id=1, source_target_pairs={{0,4},{1,5},{2,6},{3,7},{4,0},{5,1},{6,2},{7,3},{8,12},{9,13},{10,... | collective-permute-start | bytes 294920 | tf_op jit(solution)/shard_map/ppermute | solution.py:22
  115.9 28.5 %collective-permute-start.14 = (f16[2,2,2,64,512]{4,3,2,1,0:T(8,128)(2,1)S(1)}, f16[2,2,2,64,512]{4,3,2,1,0:T(8,128)(2,1)S(1)}, u32[]{:S(2)}, u32[]{:S(2)}) collective-permute-start(f16[2,2,2,64,512]{4,3,2,1,0:T(8,128)(2,1)S(1)} %fusion.2), channel_id=1, source_target_pairs={{0,1},{1,0},{2,3},{3,2},{4,5},{5,4},{6,7},{7,6},{8,9},{9,8},{10,11... | collective-permute-start | bytes 1572872 | tf_op jit(solution)/shard_map/ppermute | solution.py:22
  123.7 7.2 %collective-permute-start.19 = (f16[2,2,64,256]{3,2,1,0:T(8,128)(2,1)S(1)}, f16[2,2,64,256]{3,2,1,0:T(8,128)(2,1)S(1)}, u32[]{:S(2)}, u32[]{:S(2)}) collective-permute-start(f16[2,2,64,256]{3,2,1,0:T(8,128)(2,1)S(1)} %fusion.10), channel_id=1, source_target_pairs={{0,4},{1,5},{2,6},{3,7},{4,0},{5,1},{6,2},{7,3},{8,12},{9,13},{10,... | collective-permute-start | bytes 393224 | tf_op jit(solution)/shard_map/ppermute | solution.py:22
  123.9 22.5 %collective-permute-start.5 = (f16[2,2,2,64,768]{4,3,2,1,0:T(8,128)(2,1)S(1)}, f16[2,2,2,64,768]{4,3,2,1,0:T(8,128)(2,1)S(1)}, u32[]{:S(2)}, u32[]{:S(2)}) collective-permute-start(f16[2,2,2,64,768]{4,3,2,1,0:T(8,128)(2,1)S(1)} %fusion), channel_id=1, source_target_pairs={{0,16},{8,24},{16,0},{24,8},{1,17},{9,25},{17,1},{25,9},{2,18},{10... | collective-permute-start | bytes 2359304 | tf_op jit(solution)/shard_map/ppermute | solution.py:22
  131.0 12.6 %collective-permute-start.20 = (f16[2,64,256]{2,1,0:T(8,128)(2,1)S(1)}, f16[2,64,256]{2,1,0:T(8,128)(2,1)S(1)}, u32[]{:S(2)}, u32[]{:S(2)}) collective-permute-start(f16[2,64,256]{2,1,0:T(8,128)(2,1)S(1)} %fusion.14), channel_id=1, source_target_pairs={{0,16},{8,24},{16,0},{24,8},{1,17},{9,25},{17,1},{25,9},{2,18},{10... | collective-permute-start | bytes 196616 | tf_op jit(solution)/shard_map/ppermute | solution.py:22
  143.7 4.3 %collective-permute-start.21 = (f16[64,256]{1,0:T(8,128)(2,1)S(1)}, f16[64,256]{1,0:T(8,128)(2,1)S(1)}, u32[]{:S(2)}, u32[]{:S(2)}) collective-permute-start(f16[64,256]{1,0:T(8,128)(2,1)S(1)} %fusion.15), channel_id=1, source_target_pairs={{0,1},{1,0},{2,3},{3,2},{4,5},{5,4},{6,7},{7,6},{8,9},{9,8},{10,11... | collective-permute-start | bytes 98312 | tf_op jit(solution)/shard_map/ppermute | solution.py:22
  144.6 6.4 %collective-permute-start.15 = (f16[2,2,64,512]{3,2,1,0:T(8,128)(2,1)S(1)}, f16[2,2,64,512]{3,2,1,0:T(8,128)(2,1)S(1)}, u32[]{:S(2)}, u32[]{:S(2)}) collective-permute-start(f16[2,2,64,512]{3,2,1,0:T(8,128)(2,1)S(1)} %fusion.5), channel_id=1, source_target_pairs={{0,2},{1,3},{2,0},{3,1},{4,6},{5,7},{6,4},{7,5},{8,10},{9,11},{10,... | collective-permute-start | bytes 786440 | tf_op jit(solution)/shard_map/ppermute | solution.py:22
  146.7 8.4 %collective-permute-start.6 = (f16[2,2,64,768]{3,2,1,0:T(8,128)(2,1)S(1)}, f16[2,2,64,768]{3,2,1,0:T(8,128)(2,1)S(1)}, u32[]{:S(2)}, u32[]{:S(2)}) collective-permute-start(f16[2,2,64,768]{3,2,1,0:T(8,128)(2,1)S(1)} %fusion.3), channel_id=1, source_target_pairs={{0,1},{1,0},{2,3},{3,2},{4,5},{5,4},{6,7},{7,6},{8,9},{9,8},{10,11... | collective-permute-start | bytes 1179656 | tf_op jit(solution)/shard_map/ppermute | solution.py:22
  151.2 7.0 %collective-permute-start.16 = (f16[2,64,512]{2,1,0:T(8,128)(2,1)S(1)}, f16[2,64,512]{2,1,0:T(8,128)(2,1)S(1)}, u32[]{:S(2)}, u32[]{:S(2)}) collective-permute-start(f16[2,64,512]{2,1,0:T(8,128)(2,1)S(1)} %fusion.9), channel_id=1, source_target_pairs={{0,4},{1,5},{2,6},{3,7},{4,0},{5,1},{6,2},{7,3},{8,12},{9,13},{10,... | collective-permute-start | bytes 393224 | tf_op jit(solution)/shard_map/ppermute | solution.py:22
  155.3 5.7 %collective-permute-start.7 = (f16[2,64,768]{2,1,0:T(8,128)(2,1)S(1)}, f16[2,64,768]{2,1,0:T(8,128)(2,1)S(1)}, u32[]{:S(2)}, u32[]{:S(2)}) collective-permute-start(f16[2,64,768]{2,1,0:T(8,128)(2,1)S(1)} %fusion.7), channel_id=1, source_target_pairs={{0,2},{1,3},{2,0},{3,1},{4,6},{5,7},{6,4},{7,5},{8,10},{9,11},{10,... | collective-permute-start | bytes 589832 | tf_op jit(solution)/shard_map/ppermute | solution.py:22
  158.3 4.6 %collective-permute-start.17 = (f16[64,512]{1,0:T(8,128)(2,1)S(1)}, f16[64,512]{1,0:T(8,128)(2,1)S(1)}, u32[]{:S(2)}, u32[]{:S(2)}) collective-permute-start(f16[64,512]{1,0:T(8,128)(2,1)S(1)} %fusion.13), channel_id=1, source_target_pairs={{0,16},{8,24},{16,0},{24,8},{1,17},{9,25},{17,1},{25,9},{2,18},{10... | collective-permute-start | bytes 196616 | tf_op jit(solution)/shard_map/ppermute | solution.py:22
  161.1 6.6 %collective-permute-start.8 = (f16[64,768]{1,0:T(8,128)(2,1)S(1)}, f16[64,768]{1,0:T(8,128)(2,1)S(1)}, u32[]{:S(2)}, u32[]{:S(2)}) collective-permute-start(f16[64,768]{1,0:T(8,128)(2,1)S(1)} %fusion.11), channel_id=1, source_target_pairs={{0,4},{1,5},{2,6},{3,7},{4,0},{5,1},{6,2},{7,3},{8,12},{9,13},{10,... | collective-permute-start | bytes 294920 | tf_op jit(solution)/shard_map/ppermute | solution.py:22
  (8 other events, 33.6 us)

commit v2 on v1

v2 whole, which is shorter than its diff:
```python
import functools

import jax
import jax.numpy as jnp
from jax import lax
from jax.experimental import pallas as pl
from jax.experimental.pallas import tpu as pltpu
from jax.sharding import PartitionSpec as P

KERNEL_DILATION = 18
CHANNELS_PER_STEP = 256
F32, F16, BF16 = jnp.float32, jnp.float16, jnp.bfloat16


def from_behind(value, axis, steps):
    count = lax.axis_size(axis)
    leading, last = (max(0, -steps), min(count, count - steps))
    return lax.ppermute(value, axis, [(source, source + steps) for source in range(leading, last)])


def exchange(value, axis, bit):
    return lax.ppermute(value, axis, [(i, i ^ bit) for i in range(lax.axis_size(axis))])


def near_rows(tile):
    away, rest = divmod(KERNEL_DILATION, tile.shape[0])
    below = from_behind(tile[rest:], "space", -away)
    above = from_behind(tile[: tile.shape[0] - rest], "space", away)
    return below, above


def far_rows(tile):
    away, rest = divmod(KERNEL_DILATION, tile.shape[0])
    below = from_behind(tile[:rest], "space", -away - 1)
    above = from_behind(tile[tile.shape[0] - rest :], "space", away + 1)
    return below, above


def flat(piece):
    return piece.reshape(-1, piece.shape[-1])


def shift_columns(columns, pieces, out_ref, base):
    value = jnp.concatenate([ref[...].astype(F32) for ref in pieces])
    pixels, width = value.shape
    place = lax.broadcasted_iota(jnp.int32, (pixels, width), 0).astype(F32)
    column = place - jnp.floor((place + 0.5) * (1.0 / columns)) * columns
    ahead = pltpu.roll(value, pixels - KERNEL_DILATION, 0)
    behind = pltpu.roll(value, KERNEL_DILATION, 0)
    ahead = jnp.where(column < columns - KERNEL_DILATION, ahead, 0.0)
    behind = jnp.where(column >= KERNEL_DILATION, behind, 0.0)
    out_ref[:, base : base + width] = ahead.astype(BF16)
    out_ref[:, base + width : base + 2 * width] = value.astype(BF16)
    out_ref[:, base + 2 * width : base + 3 * width] = behind.astype(BF16)


def shift_rows(columns, cuts, pieces, out_ref):
    at = 0
    for row, cut in enumerate(cuts):
        width = pieces[at].shape[1]
        shift_columns(columns, pieces[at : at + cut], out_ref, 3 * row * width)
        at += cut


def place_in(order, block):
    spot = 0
    for _, bit in order:
        spot = 2 * spot + (block // bit) % 2
    return spot


def relative_member(step, steps):
    half = steps // 2
    return jnp.where(step < half, 2 * step + 1, 2 * (step - half))


def kernel_term_kernel(columns, cuts, order, place_ref, scale_ref, image_ref, *refs):
    pieces, given_ref, kept_ref, shifted_ref = refs[:-3], *refs[-3:]
    step, steps = pl.program_id(0), pl.num_programs(0)

    @pl.when(step == 0)
    def _():
        shift_rows(columns, cuts, pieces, shifted_ref)

    product = jnp.dot(image_ref[...].T, shifted_ref[...], preferred_element_type=F32)
    product = product * scale_ref[0]

    def store(out_ref):
        _, blocks, channels, _ = out_ref.shape
        for j in range(blocks):
            spot = place_in(order, jnp.bitwise_xor(j, place_ref[1]))
            out_ref[0, spot] = product[j * channels : (j + 1) * channels]

    @pl.when(step < steps // 2)
    def _():
        store(given_ref)

    @pl.when(step >= steps // 2)
    def _():
        store(kept_ref)


def kernel_term(columns, place, scale, image, rows_of, order):
    pixels, channels = image.shape
    members, blocks = lax.axis_size("dp"), lax.axis_size("space")
    step, half = channels // members, members // 2
    pieces = [flat(piece) for row in rows_of for piece in row]
    cuts = tuple(len(row) for row in rows_of)
    width = 3 * len(cuts) * pieces[0].shape[1]
    block = (1, blocks, step // blocks, width)
    return pl.pallas_call(
        functools.partial(kernel_term_kernel, columns, cuts, order),
        grid_spec=pltpu.PrefetchScalarGridSpec(
            num_scalar_prefetch=1,
            grid=(members,),
            in_specs=[
                pl.BlockSpec(memory_space=pltpu.SMEM),
                pl.BlockSpec(
                    (pixels, step),
                    lambda i, place: (0, jnp.bitwise_xor(relative_member(i, members), place[0])),
                ),
                *[pl.BlockSpec(piece.shape, lambda i, place: (0, 0)) for piece in pieces],
            ],
            out_specs=[
                pl.BlockSpec(block, lambda i, place: (jnp.minimum(i, half - 1), 0, 0, 0)),
                pl.BlockSpec(block, lambda i, place: (jnp.maximum(i - half, 0), 0, 0, 0)),
            ],
            scratch_shapes=[pltpu.VMEM((pixels, width), BF16)],
        ),
        out_shape=[jax.ShapeDtypeStruct((half, *block[1:]), F32)] * 2,
        compiler_params=pltpu.CompilerParams(vmem_limit_bytes=14 << 20),
        cost_estimate=pl.CostEstimate(
            flops=2 * pixels * channels * width,
            bytes_accessed=2 * pixels * channels + 4 * channels * width,
            transcendentals=0,
        ),
        name="kernel_term",
    )(place, scale, image, *pieces)


def input_grad_kernel(columns, cuts, scale_ref, *refs):
    pieces, weight_ref, out_ref, wide_ref, taps_ref, shifted_ref = refs[:-5], *refs[-5:]
    step = out_ref.shape[1]
    width = weight_ref.shape[1]
    halves = width // 128

    @pl.when(pl.program_id(0) == 0)
    def _():
        shift_rows(columns, cuts, pieces, shifted_ref)

    for h in range(halves):
        wide_ref[h] = weight_ref[:, h * 128 : (h + 1) * 128].astype(F32)
    for t in range(9):
        for h in range(halves):
            base = t * width + h * 128
            taps_ref[:, base : base + 128] = wide_ref[h, pl.ds(t, step, stride=9), :].astype(BF16)
    total = lax.dot_general(
        shifted_ref[...], taps_ref[...], (((1,), (1,)), ((), ())), preferred_element_type=F32
    )
    out_ref[...] = (total * scale_ref[0]).astype(BF16)


def input_grad(columns, scale, rows_of, weight):
    pieces = [flat(piece) for row in rows_of for piece in row]
    cuts = tuple(len(row) for row in rows_of)
    pixels = sum(piece.shape[0] for piece in pieces) // 3
    rows, width = weight.shape
    channels = rows // 9
    step = CHANNELS_PER_STEP
    return pl.pallas_call(
        functools.partial(input_grad_kernel, columns, cuts),
        grid=(channels // step,),
        in_specs=[
            pl.BlockSpec(memory_space=pltpu.SMEM),
            *[pl.BlockSpec(piece.shape, lambda i: (0, 0)) for piece in pieces],
            pl.BlockSpec((9 * step, width), lambda i: (i, 0)),
        ],
        out_specs=pl.BlockSpec((pixels, step), lambda i: (0, i)),
        out_shape=jax.ShapeDtypeStruct((pixels, channels), BF16),
        scratch_shapes=[
            pltpu.VMEM((width // 128, 9 * step, 128), F32),
            pltpu.VMEM((step, 9 * width), BF16),
            pltpu.VMEM((pixels, 9 * width), BF16),
        ],
        compiler_params=pltpu.CompilerParams(vmem_limit_bytes=18 << 20),
        cost_estimate=pl.CostEstimate(
            flops=2 * pixels * rows * width,
            bytes_accessed=2 * (rows * width + pixels * channels),
            transcendentals=0,
        ),
        name="input_grad",
    )(scale, *pieces, pltpu.with_memory_space_constraint(weight, pltpu.HBM))


def bits_of(axis):
    return [(axis, 1 << k) for k in reversed(range(lax.axis_size(axis).bit_length() - 1))]


def after(value, *others):
    return lax.optimization_barrier((value, others))[0]


def exchange_by_role(value, orders, step):
    members, blocks = lax.axis_size("dp"), lax.axis_size("space")
    pairs = []
    for member in range(members):
        for block in range(blocks):
            axis, bit = orders[member % 2][step]
            target = (member ^ bit, block) if axis == "dp" else (member, block ^ bit)
            pairs.append((member * blocks + block, target[0] * blocks + target[1]))
    return lax.ppermute(value, ("dp", "space"), pairs)


class Sums:
    def __init__(self, value, names, orders):
        self.value, self.names, self.orders = value, [list(names), list(names)], orders
        self.even = lax.axis_index("dp") % 2 == 0

    def part(self, index):
        spots = [names.index(order[0]) for names, order in zip(self.names, self.orders)]
        parts = [lax.index_in_dim(self.value, index, spot, keepdims=False) for spot in spots]
        return parts[0] if spots[0] == spots[1] else jnp.where(self.even, *parts)

    def sent(self):
        return self.part(1).astype(F16)

    def add(self, back):
        self.value = self.part(0) + back.astype(F32)
        self.names = [[n for n in names if n != order[0]] for names, order in zip(self.names, self.orders)]
        self.orders = [order[1:] for order in self.orders]


def shards(features, grad_out, weight, alive):
    _, rows, columns, in_channels = features.shape
    out_channels = grad_out.shape[-1]
    pixels = rows * columns
    member_count = lax.axis_size("dp")
    core = ("dp", 1)
    across = [name for name in bits_of("dp") if name != core]
    along = bits_of("space")[::-1]
    first, inner, final_bit = along[:1], along[1:-1], along[-1:]
    orders = (across + first + inner + final_bit, first + inner + across + final_bit)
    centre_order = inner + across + first + final_bit

    own_alive = jnp.sum(alive).astype(F32)
    term_scale = (own_alive * (4.0 / member_count)).reshape(1)
    tile = grad_out.reshape(rows, columns, out_channels)
    image = features.reshape(pixels, in_channels)
    place = jnp.stack([lax.axis_index("dp"), lax.axis_index("space")]).astype(jnp.int32)

    def term(rows_of):
        return kernel_term(columns, place, term_scale, image, rows_of, along)

    def sums(kept, back, *orders):
        value = kept.astype(F32) + back.astype(F32)
        names = across + along
        return Sums(value.reshape((2,) * len(names) + value.shape[2:]), names, orders)

    near_below, near_above = near_rows(tile)
    far_below, far_above = far_rows(tile)
    centre = term([[tile]])
    survivors = own_alive.reshape(1)
    survivors = survivors + exchange(survivors, *core)
    below, above, centre, survivors = lax.optimization_barrier(
        ((near_below, far_below), (far_above, near_above), centre, survivors)
    )

    sent, kept = (half.astype(F16) for half in centre)
    back = exchange(sent, *core)
    for name in across:
        survivors = survivors + exchange(survivors, *name)
    lower = term([after(below, sent, kept)])
    lower, kept, back, survivors = lax.optimization_barrier((lower, kept, back, survivors))
    centre = sums(kept, back, centre_order, centre_order)
    sent, kept = (half.astype(F16) for half in lower)
    back = exchange(sent, *core)
    upper = term([after(above, sent, kept, centre.value)])
    upper, kept, back = lax.optimization_barrier((upper, kept, back))
    sent = upper[0].astype(F16)
    lower = sums(kept, after(back, sent), *orders)
    upper = sums(upper[1], exchange(sent, *core), *orders)

    width = 3 * out_channels
    grad_features = None
    for step, name in enumerate(centre_order):
        ring_sent = [lower.sent(), upper.sent()]
        centre_sent = centre.sent()
        if step + 1 < len(centre_order):
            ring_sent = jnp.concatenate(ring_sent, axis=-1)
            ring_back = exchange_by_role(ring_sent, orders, step)
            centre_back = exchange(centre_sent, *name)
        else:
            ring_back = exchange(jnp.concatenate([*ring_sent, centre_sent], axis=-1), *name)
            centre_back = ring_back[..., 2 * width :]
        if step == 0:
            grad_features = input_grad(
                columns,
                (own_alive / survivors).reshape(1),
                [below, [tile], after(above, ring_sent, centre_sent)],
                weight,
            )
        ring_back, centre_back, grad_features = lax.optimization_barrier(
            (ring_back, centre_back, grad_features)
        )
        lower.add(ring_back[..., :width])
        upper.add(ring_back[..., width : 2 * width])
        centre.add(centre_back)
    final = jnp.concatenate([lower.value, centre.value, upper.value], axis=-1)
    final = final * (member_count * 0.25 / survivors)
    return (final.reshape(-1, out_channels), grad_features.reshape(features.shape))


def solution(mesh):
    in_specs = (P("dp", "space", None, None), P("dp", "space", None, None), P(), P("dp"))
    out_specs = (P(("dp", "space"), None), P("dp", "space", None, None))
    return jax.shard_map(shards, mesh=mesh, in_specs=in_specs, out_specs=out_specs, check_vma=False)
```

time: 170 us -> 116 us (0.68)
  local copies, waits for them, and re-layouts: 39.3 us -> 7.68 us
  starting transfers between devices: 54.2 us -> 28.4 us
  Pallas kernels: 15.3 us -> 33.2 us
  matrix products: 16.4 us -> 0 us
  other arithmetic: 3.77 us -> 13.2 us
  waiting for transfers between devices: 36.6 us -> 30 us
    ppermute x20 -> x9, starting transfers between devices: 41.8 us -> 12.1 us  [exchange(): lax.ppermute(value, axis, [(i, i ^ bit) for i in range(lax.axis_size(axis...]
    pallas_call x3 -> x4, Pallas kernels: 15.3 us -> 33.2 us  [the longest x3 18 us: kernel_term(): pl.pallas_call(functools.partial(kernel_term_kernel, columns, cuts, order...]
    dot_general x4 -> x0, matrix products: 16.4 us -> none  [term(): lax.dot_general(image, shifted, (((0,), (0,)), ((), ())), preferred_eleme...]
    unnamed x18 -> x28, local copies, waits for them, and re-layouts: 18.3 us -> 4.5 us
    dynamic_slice x2 -> x0, local copies, waits for them, and re-layouts: 11.6 us -> none  [pick(): return lax.dynamic_index_in_dim(value, index, position, keepdims=False)]
    reshape x1 -> x0, local copies, waits for them, and re-layouts: 7.87 us -> none  [shards(): features.reshape(pixels, member_count // 2, 2, in_channels // member_count)]
    ppermute x20 -> x9, waiting for transfers between devices: 36.6 us -> 29 us  [exchange(): lax.ppermute(value, axis, [(i, i ^ bit) for i in range(lax.axis_size(axis...]
    add x16 -> x12, other arithmetic: 2.93 us -> 7.59 us  [the longest x3 6.31 us: sums(): value = kept.astype(F32) + back.astype(F32)]
  transfers between devices with their start and end apart: 24 -> 16, of which waited for: 11 -> 6; matrix products, arithmetic and copies ran while one was open for 17% -> 6% of each run, Pallas kernels for 9% -> 29%
where the time goes in v2:
time: 116 us
  Pallas kernels  33.2 us (29%)
  waiting for transfers between devices  30 us (26%)
  starting transfers between devices  28.4 us (24%)
  other arithmetic  13.2 us (11%)
  local copies, waits for them, and re-layouts  7.68 us (7%)
  between operations  3.14 us (3%)
    ppermute x9, waiting for transfers between devices, exchange(): lax.ppermute(value, axis, [(i, i ^ bit) for i in range(lax.axis_size(axis...  29 us
    pallas_call x3, Pallas kernels, kernel_term(): pl.pallas_call(functools.partial(kernel_term_kernel, columns, cuts, order...  18 us
    pallas_call x1, Pallas kernels, input_grad(): pl.pallas_call(functools.partial(input_grad_kernel, columns, cuts), grid=...  15.2 us
    ppermute x4, starting transfers between devices, from_behind(): lax.ppermute(value, axis, [(source, source + steps) for source in range(l...  12.1 us
    ppermute x9, starting transfers between devices, exchange(): lax.ppermute(value, axis, [(i, i ^ bit) for i in range(lax.axis_size(axis...  12.1 us
    add x3, other arithmetic, sums(): value = kept.astype(F32) + back.astype(F32)  6.31 us
    unnamed x28, local copies, waits for them, and re-layouts  4.5 us
    ppermute x3, starting transfers between devices, exchange_by_role(): return lax.ppermute(value, ('dp', 'space'), pairs)  4.26 us
  transfers between devices with their start and end apart: 16, of which 6 were waited for; matrix products, arithmetic and copies ran while one was open for 6% of the time, Pallas kernels for 29%

profile of v2, /device:TPU:0, one launch (start us, length us, event | category | flops | bytes accessed | tf_op | source)
XLA Modules:
  0.0 115.6 jit_solution(7379055154059045619)
XLA Ops:
  0.6 1.1 slice_bitcast_fusion.13
  1.7 1.3 %collective-permute-start = (bf16[6,72,256]{2,1,0:T(8,128)(2,1)S(1)}, bf16[6,72,256]{2,1,0:T(8,128)(2,1)S(1)}, u32[]{:S(2)}, u32[]{:S(2)}) collective-permute-start(bf16[6,72,256]{2,1,0:T(8,128)(2,1)S(1)} %get-tuple-element.95), channel_id=1, source_target_pairs={{1,0},{2,1},{3,2},{4,3},{5,4},{6,5},{7,6},{9,8},{10,9},{11,10},{12... | collective-permute-start | bytes 663560 | tf_op jit(solution)/shard_map/ppermute | solution.py:18
  3.0 7.0 %collective-permute-start.2 = (bf16[6,72,256]{2,1,0:T(8,128)(2,1)S(1)}, bf16[6,72,256]{2,1,0:T(8,128)(2,1)S(1)}, u32[]{:S(2)}, u32[]{:S(2)}) collective-permute-start(bf16[6,72,256]{2,1,0:T(8,128)(2,1)S(1)} %get-tuple-element.95), channel_id=1, source_target_pairs={{0,2},{1,3},{2,4},{3,5},{4,6},{5,7},{8,10},{9,11},{10,12},{11,13},... | collective-permute-start | bytes 663560 | tf_op jit(solution)/shard_map/ppermute | solution.py:18
  10.0 1.3 %collective-permute-start.1 = (bf16[6,72,256]{2,1,0:T(8,128)(2,1)S(1)}, bf16[6,72,256]{2,1,0:T(8,128)(2,1)S(1)}, u32[]{:S(2)}, u32[]{:S(2)}) collective-permute-start(bf16[6,72,256]{2,1,0:T(8,128)(2,1)S(1)} %get-tuple-element.94), channel_id=1, source_target_pairs={{2,0},{3,1},{4,2},{5,3},{6,4},{7,5},{10,8},{11,9},{12,10},{13,11},... | collective-permute-start | bytes 663560 | tf_op jit(solution)/shard_map/ppermute | solution.py:18
  11.3 2.5 %collective-permute-start.3 = (bf16[6,72,256]{2,1,0:T(8,128)(2,1)S(1)}, bf16[6,72,256]{2,1,0:T(8,128)(2,1)S(1)}, u32[]{:S(2)}, u32[]{:S(2)}) collective-permute-start(bf16[6,72,256]{2,1,0:T(8,128)(2,1)S(1)} %get-tuple-element.94), channel_id=1, source_target_pairs={{0,1},{1,2},{2,3},{3,4},{4,5},{5,6},{6,7},{8,9},{9,10},{10,11},{11... | collective-permute-start | bytes 663560 | tf_op jit(solution)/shard_map/ppermute | solution.py:18
  16.6 2.0 %copy-done.2 = bf16[1,12,72,2048]{3,2,1,0:T(8,128)(2,1)S(1)} copy-done((bf16[1,12,72,2048]{3,2,1,0:T(8,128)(2,1)S(1)}, bf16[1,12,72,2048]{3,2,1,0:T(8,128)(2,1)}, u32[]{:S(2)}) %copy-start.2) | copy-done | bytes 3538968
  18.6 6.0 %kernel_term.3 = (f32[2,8,64,768]{3,2,1,0:T(8,128)S(1)}, f32[2,8,64,768]{3,2,1,0:T(8,128)S(1)}) custom-call(s32[2]{0:T(128)S(1)} %pad_add_fusion.place_ref, f32[1]{0:T(128)} %convert_element_type.114.scale_ref, bf16[864,2048]{1,0:T(8,128)(2,1)S(1)} %bitcast.145, bf16[864,256]{1,0:T(8,128)(2,1)S(1)} %bitcast.143), custom_call_target="tpu_custom_call" | custom-call | flops 2717908992 | bytes 9830400 | tf_op jit(solution)/shard_map/kernel_term/pallas_call | solution.py:111
  26.8 2.9 %collective-permute-start.6 = (f32[1]{0:T(128)}, f32[1]{0:T(128)}, u32[]{:S(2)}, u32[]{:S(2)}) collective-permute-start(f32[1]{0:T(128)} %add.57), channel_id=1, source_target_pairs={{0,16},{8,24},{16,0},{24,8},{1,17},{9,25},{17,1},{25,9},{2,18},{10... | collective-permute-start | bytes 20 | tf_op jit(solution)/shard_map/ppermute | solution.py:22
  29.7 6.0 %kernel_term.4 = (f32[2,8,64,768]{3,2,1,0:T(8,128)S(1)}, f32[2,8,64,768]{3,2,1,0:T(8,128)S(1)}) custom-call(s32[2]{0:T(128)S(1)} %pad_add_fusion.place_ref, f32[1]{0:T(128)} %convert_element_type.114.scale_ref, bf16[864,2048]{1,0:T(8,128)(2,1)S(1)} %bitcast.146, bf16[432,256]{1,0:T(8,128)(2,1)S(1)} %bitcast.148, bf16[432,256]{1,0:T(8,128)(2,1)S(1)} %bitcast.152), custom_call_target="tpu_custom_call" | custom-call | flops 2717908992 | bytes 9830400 | tf_op jit(solution)/shard_map/kernel_term/pallas_call | solution.py:111
  36.7 1.4 %convert_element_type.118 = f16[2,8,64,768]{3,2,1,0:T(8,128)(2,1)} convert(f32[2,8,64,768]{3,2,1,0:T(8,128)S(1)} %get-tuple-element.57) | non-fusion elementwise | flops 786432 | bytes 4718592 | tf_op jit(solution)/shard_map/convert_element_type | solution.py:275
  38.1 2.1 %convert_add_fusion.2 = f32[2,8,64,768]{3,2,1,0:T(8,128)} fusion(f16[2,8,64,768]{3,2,1,0:T(8,128)(2,1)S(1)} %collective-permute-done.5, f16[2,8,64,768]{3,2,1,0:T(8,128)(2,1)S(1)} %convert_element_type.116), kind=kLoop, calls=%fused_computation.2 | loop fusion | flops 2359296 | bytes 6291456 | tf_op jit(solution)/shard_map/add | solution.py:255
  40.2 6.0 %kernel_term.5 = (f32[2,8,64,768]{3,2,1,0:T(8,128)S(1)}, f32[2,8,64,768]{3,2,1,0:T(8,128)S(1)}) custom-call(s32[2]{0:T(128)S(1)} %pad_add_fusion.place_ref, f32[1]{0:T(128)} %convert_element_type.114.scale_ref, bf16[864,2048]{1,0:T(8,128)(2,1)S(1)} %bitcast.147, bf16[432,256]{1,0:T(8,128)(2,1)S(1)} %bitcast.150, bf16[432,256]{1,0:T(8,128)(2,1)S(1)} %bitcast.154), custom_call_target="tpu_custom_call" | custom-call | flops 2717908992 | bytes 9830400 | tf_op jit(solution)/shard_map/kernel_term/pallas_call | solution.py:111
  46.2 1.7 %convert_element_type.122 = f16[2,8,64,768]{3,2,1,0:T(8,128)(2,1)} convert(f32[2,8,64,768]{3,2,1,0:T(8,128)S(1)} %get-tuple-element.66) | non-fusion elementwise | flops 786432 | bytes 4718592 | tf_op jit(solution)/shard_map/convert_element_type | solution.py:279
  48.4 2.3 %convert_add_fusion.1 = f32[2,8,64,768]{3,2,1,0:T(8,128)S(1)} fusion(f16[2,8,64,768]{3,2,1,0:T(8,128)(2,1)} %copy-done.13, f16[2,8,64,768]{3,2,1,0:T(8,128)(2,1)} %convert_element_type.118), kind=kLoop, calls=%fused_computation.1 | loop fusion | flops 2359296 | bytes 6291456 | tf_op jit(solution)/shard_map/add | solution.py:255
  51.8 1.9 %convert_add_fusion = f32[2,8,64,768]{3,2,1,0:T(8,128)S(1)} fusion(f32[2,8,64,768]{3,2,1,0:T(8,128)S(1)} %get-tuple-element.68, f16[2,8,64,768]{3,2,1,0:T(8,128)(2,1)} %collective-permute-done.8), kind=kLoop, calls=%fused_computation | loop fusion | flops 1572864 | bytes 7864320 | tf_op jit(solution)/shard_map/add | solution.py:255
  56.9 2.7 %collective-permute-start.10 = (f16[2,2,2,64,768]{4,3,2,1,0:T(8,128)(2,1)S(1)}, f16[2,2,2,64,768]{4,3,2,1,0:T(8,128)(2,1)S(1)}, u32[]{:S(2)}, u32[]{:S(2)}) collective-permute-start(f16[2,2,2,64,768]{4,3,2,1,0:T(8,128)(2,1)S(1)} %fusion.9), channel_id=1, source_target_pairs={{0,2},{1,3},{2,0},{3,1},{4,6},{5,7},{6,4},{7,5},{8,10},{9,11},{10,... | collective-permute-start | bytes 2359304 | tf_op jit(solution)/shard_map/ppermute | solution.py:22
  59.7 15.2 %input_grad.1 = bf16[864,2048]{1,0:T(8,128)(2,1)} custom-call(f32[1]{0:T(128)S(6)} %div.7.scale_ref, bf16[432,256]{1,0:T(8,128)(2,1)S(1)} %bitcast.149, bf16[432,256]{1,0:T(8,128)(2,1)S(1)} %bitcast.153, bf16[864,256]{1,0:T(8,128)(2,1)S(1)} %bitcast.144, bf16[432,256]{1,0:T(8,128)(2,1)S(1)} %bitcast.151, bf16[432,256]{1,0:T(8,128)(2,1)S(1)} %bitcast.155, ...), custom_call_target="tpu_custom_call" | custom-call | flops 8153726976 | bytes 12976128 | tf_op jit(solution)/shard_map/input_grad/pallas_call | solution.py:170
  74.9 2.6 %collective-permute-done.10 = f16[2,2,2,64,768]{4,3,2,1,0:T(8,128)(2,1)S(1)} collective-permute-done((f16[2,2,2,64,768]{4,3,2,1,0:T(8,128)(2,1)S(1)}, f16[2,2,2,64,768]{4,3,2,1,0:T(8,128)(2,1)S(1)}, u32[]{:S(2)}, u32[]{:S(2)}) %collective-permute-start.10) | collective-permute-done | bytes 786464 | tf_op jit(solution)/shard_map/ppermute | solution.py:22
  78.4 2.8 %collective-permute-start.11 = (f16[2,2,64,1536]{3,2,1,0:T(8,128)(2,1)S(1)}, f16[2,2,64,1536]{3,2,1,0:T(8,128)(2,1)S(1)}, u32[]{:S(2)}, u32[]{:S(2)}) collective-permute-start(f16[2,2,64,1536]{3,2,1,0:T(8,128)(2,1)S(1)} %pad_maximum_fusion.1), channel_id=1, source_target_pairs={{0,1},{1,0},{2,3},{3,2},{4,5},{5,4},{6,7},{7,6},{8,10},{9,11},{10,... | collective-permute-start | bytes 2359304 | tf_op jit(solution)/shard_map/ppermute | solution.py:211
  82.1 10.0 %collective-permute-done.12 = f16[2,2,64,768]{3,2,1,0:T(8,128)(2,1)S(1)} collective-permute-done((f16[2,2,64,768]{3,2,1,0:T(8,128)(2,1)S(1)}, f16[2,2,64,768]{3,2,1,0:T(8,128)(2,1)S(1)}, u32[]{:S(2)}, u32[]{:S(2)}) %collective-permute-start.12) | collective-permute-done | bytes 393248 | tf_op jit(solution)/shard_map/ppermute | solution.py:22
  93.4 2.0 %collective-permute-start.14 = (f16[2,64,768]{2,1,0:T(8,128)(2,1)S(1)}, f16[2,64,768]{2,1,0:T(8,128)(2,1)S(1)}, u32[]{:S(2)}, u32[]{:S(2)}) collective-permute-start(f16[2,64,768]{2,1,0:T(8,128)(2,1)S(1)} %fusion.25), channel_id=1, source_target_pairs={{0,1},{1,0},{2,3},{3,2},{4,5},{5,4},{6,7},{7,6},{8,9},{9,8},{10,11... | collective-permute-start | bytes 589832 | tf_op jit(solution)/shard_map/ppermute | solution.py:22
  95.4 3.9 %collective-permute-done.14 = f16[2,64,768]{2,1,0:T(8,128)(2,1)S(1)} collective-permute-done((f16[2,64,768]{2,1,0:T(8,128)(2,1)S(1)}, f16[2,64,768]{2,1,0:T(8,128)(2,1)S(1)}, u32[]{:S(2)}, u32[]{:S(2)}) %collective-permute-start.14) | collective-permute-done | bytes 196640 | tf_op jit(solution)/shard_map/ppermute | solution.py:22
  100.6 1.8 %collective-permute-start.15 = (f16[64,2304]{1,0:T(8,128)(2,1)S(1)}, f16[64,2304]{1,0:T(8,128)(2,1)S(1)}, u32[]{:S(2)}, u32[]{:S(2)}) collective-permute-start(f16[64,2304]{1,0:T(8,128)(2,1)S(1)} %pad_maximum_fusion.3), channel_id=1, source_target_pairs={{0,4},{1,5},{2,6},{3,7},{4,0},{5,1},{6,2},{7,3},{8,12},{9,13},{10,... | collective-permute-start | bytes 884744 | tf_op jit(solution)/shard_map/ppermute | solution.py:22
  102.5 12.0 %collective-permute-done.15 = f16[64,2304]{1,0:T(8,128)(2,1)S(1)} collective-permute-done((f16[64,2304]{1,0:T(8,128)(2,1)S(1)}, f16[64,2304]{1,0:T(8,128)(2,1)S(1)}, u32[]{:S(2)}, u32[]{:S(2)}) %collective-permute-start.15) | collective-permute-done | bytes 294944 | tf_op jit(solution)/shard_map/ppermute | solution.py:22
  (81 shorter events, 14.1 us)
Async XLA Ops:
  1.7 23.5 %collective-permute-start = (bf16[6,72,256]{2,1,0:T(8,128)(2,1)S(1)}, bf16[6,72,256]{2,1,0:T(8,128)(2,1)S(1)}, u32[]{:S(2)}, u32[]{:S(2)}) collective-permute-start(bf16[6,72,256]{2,1,0:T(8,128)(2,1)S(1)} %get-tuple-element.95), channel_id=1, source_target_pairs={{1,0},{2,1},{3,2},{4,3},{5,4},{6,5},{7,6},{9,8},{10,9},{11,10},{12... | collective-permute-start | bytes 663560 | tf_op jit(solution)/shard_map/ppermute | solution.py:18
  3.0 22.2 %collective-permute-start.2 = (bf16[6,72,256]{2,1,0:T(8,128)(2,1)S(1)}, bf16[6,72,256]{2,1,0:T(8,128)(2,1)S(1)}, u32[]{:S(2)}, u32[]{:S(2)}) collective-permute-start(bf16[6,72,256]{2,1,0:T(8,128)(2,1)S(1)} %get-tuple-element.95), channel_id=1, source_target_pairs={{0,2},{1,3},{2,4},{3,5},{4,6},{5,7},{8,10},{9,11},{10,12},{11,13},... | collective-permute-start | bytes 663560 | tf_op jit(solution)/shard_map/ppermute | solution.py:18
  10.0 15.2 %collective-permute-start.1 = (bf16[6,72,256]{2,1,0:T(8,128)(2,1)S(1)}, bf16[6,72,256]{2,1,0:T(8,128)(2,1)S(1)}, u32[]{:S(2)}, u32[]{:S(2)}) collective-permute-start(bf16[6,72,256]{2,1,0:T(8,128)(2,1)S(1)} %get-tuple-element.94), channel_id=1, source_target_pairs={{2,0},{3,1},{4,2},{5,3},{6,4},{7,5},{10,8},{11,9},{12,10},{13,11},... | collective-permute-start | bytes 663560 | tf_op jit(solution)/shard_map/ppermute | solution.py:18
  11.3 14.0 %collective-permute-start.3 = (bf16[6,72,256]{2,1,0:T(8,128)(2,1)S(1)}, bf16[6,72,256]{2,1,0:T(8,128)(2,1)S(1)}, u32[]{:S(2)}, u32[]{:S(2)}) collective-permute-start(bf16[6,72,256]{2,1,0:T(8,128)(2,1)S(1)} %get-tuple-element.94), channel_id=1, source_target_pairs={{0,1},{1,2},{2,3},{3,4},{4,5},{5,6},{6,7},{8,9},{9,10},{10,11},{11... | collective-permute-start | bytes 663560 | tf_op jit(solution)/shard_map/ppermute | solution.py:18
  14.5 10.1 %collective-permute-start.4 = (f32[1]{0:T(128)}, f32[1]{0:T(128)}, u32[]{:S(2)}, u32[]{:S(2)}) collective-permute-start(f32[1]{0:T(128)} %convert_element_type.114.scale_ref), channel_id=1, source_target_pairs={{0,8},{8,0},{16,24},{24,16},{1,9},{9,1},{17,25},{25,17},{2,10},{10... | collective-permute-start | bytes 20 | tf_op jit(solution)/shard_map/ppermute | solution.py:22
  25.2 4.4 %copy-start.7 = (bf16[6,72,256]{2,1,0:T(8,128)(2,1)}, bf16[6,72,256]{2,1,0:T(8,128)(2,1)S(1)}, u32[]{:S(2)}) copy-start(bf16[6,72,256]{2,1,0:T(8,128)(2,1)S(1)} %collective-permute-done.1) | copy-start | bytes 663556
  26.0 3.6 %copy-start.3 = (bf16[1,12,72,2048]{3,2,1,0:T(8,128)(2,1)S(1)}, bf16[1,12,72,2048]{3,2,1,0:T(8,128)(2,1)}, u32[]{:S(2)}) copy-start(bf16[1,12,72,2048]{3,2,1,0:T(8,128)(2,1)} %param.4) | copy-start | bytes 10616836
  26.0 10.3 %collective-permute-start.5 = (f16[2,8,64,768]{3,2,1,0:T(8,128)(2,1)S(1)}, f16[2,8,64,768]{3,2,1,0:T(8,128)(2,1)S(1)}, u32[]{:S(2)}, u32[]{:S(2)}) collective-permute-start(f16[2,8,64,768]{3,2,1,0:T(8,128)(2,1)S(1)} %convert_element_type.115), channel_id=1, source_target_pairs={{0,8},{8,0},{16,24},{24,16},{1,9},{9,1},{17,25},{25,17},{2,10},{10... | collective-permute-start | bytes 4718600 | tf_op jit(solution)/shard_map/ppermute | solution.py:22
  26.8 8.9 %collective-permute-start.6 = (f32[1]{0:T(128)}, f32[1]{0:T(128)}, u32[]{:S(2)}, u32[]{:S(2)}) collective-permute-start(f32[1]{0:T(128)} %add.57), channel_id=1, source_target_pairs={{0,16},{8,24},{16,0},{24,8},{1,17},{9,25},{17,1},{25,9},{2,18},{10... | collective-permute-start | bytes 20 | tf_op jit(solution)/shard_map/ppermute | solution.py:22
  36.6 9.6 %collective-permute-start.7 = (f16[2,8,64,768]{3,2,1,0:T(8,128)(2,1)S(1)}, f16[2,8,64,768]{3,2,1,0:T(8,128)(2,1)S(1)}, u32[]{:S(2)}, u32[]{:S(2)}) collective-permute-start(f16[2,8,64,768]{3,2,1,0:T(8,128)(2,1)S(1)} %convert_element_type.117), channel_id=1, source_target_pairs={{0,8},{8,0},{16,24},{24,16},{1,9},{9,1},{17,25},{25,17},{2,10},{10... | collective-permute-start | bytes 4718600 | tf_op jit(solution)/shard_map/ppermute | solution.py:22
  38.1 2.1 %copy-start.5 = (bf16[6,72,256]{2,1,0:T(8,128)(2,1)S(1)}, bf16[6,72,256]{2,1,0:T(8,128)(2,1)}, u32[]{:S(2)}) copy-start(bf16[6,72,256]{2,1,0:T(8,128)(2,1)} %copy-done.4) | copy-start | bytes 663556
  38.1 2.1 %copy-start.10 = (bf16[6,72,256]{2,1,0:T(8,128)(2,1)S(1)}, bf16[6,72,256]{2,1,0:T(8,128)(2,1)}, u32[]{:S(2)}) copy-start(bf16[6,72,256]{2,1,0:T(8,128)(2,1)} %copy-done.9) | copy-start | bytes 663556
  47.9 3.9 %collective-permute-start.8 = (f16[2,8,64,768]{3,2,1,0:T(8,128)(2,1)}, f16[2,8,64,768]{3,2,1,0:T(8,128)(2,1)}, u32[]{:S(2)}, u32[]{:S(2)}) collective-permute-start(f16[2,8,64,768]{3,2,1,0:T(8,128)(2,1)} %convert_element_type.122), channel_id=1, source_target_pairs={{0,8},{8,0},{16,24},{24,16},{1,9},{9,1},{17,25},{25,17},{2,10},{10... | collective-permute-start | bytes 4718600 | tf_op jit(solution)/shard_map/ppermute | solution.py:22
  54.9 22.6 %collective-permute-start.9 = (f16[2,2,2,64,1536]{4,3,2,0,1:T(8,128)(2,1)S(1)}, f16[2,2,2,64,1536]{4,3,2,0,1:T(8,128)(2,1)S(1)}, u32[]{:S(2)}, u32[]{:S(2)}) collective-permute-start(f16[2,2,2,64,1536]{4,3,2,0,1:T(8,128)(2,1)S(1)} %pad_maximum_fusion), channel_id=1, source_target_pairs={{0,16},{1,17},{2,18},{3,19},{4,20},{5,21},{6,22},{7,23},{8,9},{9,8... | collective-permute-start | bytes 4718600 | tf_op jit(solution)/shard_map/ppermute | solution.py:211
  56.7 2.9 %copy-start.1 = (bf16[1,12,72,256]{3,2,1,0:T(8,128)(2,1)S(1)}, bf16[1,12,72,256]{3,2,1,0:T(8,128)(2,1)}, u32[]{:S(2)}) copy-start(bf16[1,12,72,256]{3,2,1,0:T(8,128)(2,1)} %param.5) | copy-start | bytes 1327108
  56.7 2.9 %copy-start.6 = (bf16[6,72,256]{2,1,0:T(8,128)(2,1)S(1)}, bf16[6,72,256]{2,1,0:T(8,128)(2,1)}, u32[]{:S(2)}) copy-start(bf16[6,72,256]{2,1,0:T(8,128)(2,1)} %copy-done.4) | copy-start | bytes 663556
  56.8 2.9 %copy-start.8 = (bf16[6,72,256]{2,1,0:T(8,128)(2,1)S(1)}, bf16[6,72,256]{2,1,0:T(8,128)(2,1)}, u32[]{:S(2)}) copy-start(bf16[6,72,256]{2,1,0:T(8,128)(2,1)} %copy-done.7) | copy-start | bytes 663556
  56.8 2.9 %copy-start.11 = (bf16[6,72,256]{2,1,0:T(8,128)(2,1)S(1)}, bf16[6,72,256]{2,1,0:T(8,128)(2,1)}, u32[]{:S(2)}) copy-start(bf16[6,72,256]{2,1,0:T(8,128)(2,1)} %copy-done.9) | copy-start | bytes 663556
  56.9 20.6 %collective-permute-start.10 = (f16[2,2,2,64,768]{4,3,2,1,0:T(8,128)(2,1)S(1)}, f16[2,2,2,64,768]{4,3,2,1,0:T(8,128)(2,1)S(1)}, u32[]{:S(2)}, u32[]{:S(2)}) collective-permute-start(f16[2,2,2,64,768]{4,3,2,1,0:T(8,128)(2,1)S(1)} %fusion.9), channel_id=1, source_target_pairs={{0,2},{1,3},{2,0},{3,1},{4,6},{5,7},{6,4},{7,5},{8,10},{9,11},{10,... | collective-permute-start | bytes 2359304 | tf_op jit(solution)/shard_map/ppermute | solution.py:22
  78.4 13.7 %collective-permute-start.11 = (f16[2,2,64,1536]{3,2,1,0:T(8,128)(2,1)S(1)}, f16[2,2,64,1536]{3,2,1,0:T(8,128)(2,1)S(1)}, u32[]{:S(2)}, u32[]{:S(2)}) collective-permute-start(f16[2,2,64,1536]{3,2,1,0:T(8,128)(2,1)S(1)} %pad_maximum_fusion.1), channel_id=1, source_target_pairs={{0,1},{1,0},{2,3},{3,2},{4,5},{5,4},{6,7},{7,6},{8,10},{9,11},{10,... | collective-permute-start | bytes 2359304 | tf_op jit(solution)/shard_map/ppermute | solution.py:211
  81.5 10.6 %collective-permute-start.12 = (f16[2,2,64,768]{3,2,1,0:T(8,128)(2,1)S(1)}, f16[2,2,64,768]{3,2,1,0:T(8,128)(2,1)S(1)}, u32[]{:S(2)}, u32[]{:S(2)}) collective-permute-start(f16[2,2,64,768]{3,2,1,0:T(8,128)(2,1)S(1)} %fusion.19), channel_id=1, source_target_pairs={{0,16},{8,24},{16,0},{24,8},{1,17},{9,25},{17,1},{25,9},{2,18},{10... | collective-permute-start | bytes 1179656 | tf_op jit(solution)/shard_map/ppermute | solution.py:22
  92.4 7.8 %collective-permute-start.13 = (f16[2,64,1536]{2,1,0:T(8,128)(2,1)S(1)}, f16[2,64,1536]{2,1,0:T(8,128)(2,1)S(1)}, u32[]{:S(2)}, u32[]{:S(2)}) collective-permute-start(f16[2,64,1536]{2,1,0:T(8,128)(2,1)S(1)} %pad_maximum_fusion.2), channel_id=1, source_target_pairs={{0,2},{1,3},{2,0},{3,1},{4,6},{5,7},{6,4},{7,5},{8,24},{9,25},{10,... | collective-permute-start | bytes 1179656 | tf_op jit(solution)/shard_map/ppermute | solution.py:211
  93.4 5.8 %collective-permute-start.14 = (f16[2,64,768]{2,1,0:T(8,128)(2,1)S(1)}, f16[2,64,768]{2,1,0:T(8,128)(2,1)S(1)}, u32[]{:S(2)}, u32[]{:S(2)}) collective-permute-start(f16[2,64,768]{2,1,0:T(8,128)(2,1)S(1)} %fusion.25), channel_id=1, source_target_pairs={{0,1},{1,0},{2,3},{3,2},{4,5},{5,4},{6,7},{7,6},{8,9},{9,8},{10,11... | collective-permute-start | bytes 589832 | tf_op jit(solution)/shard_map/ppermute | solution.py:22
  100.6 13.9 %collective-permute-start.15 = (f16[64,2304]{1,0:T(8,128)(2,1)S(1)}, f16[64,2304]{1,0:T(8,128)(2,1)S(1)}, u32[]{:S(2)}, u32[]{:S(2)}) collective-permute-start(f16[64,2304]{1,0:T(8,128)(2,1)S(1)} %pad_maximum_fusion.3), channel_id=1, source_target_pairs={{0,4},{1,5},{2,6},{3,7},{4,0},{5,1},{6,2},{7,3},{8,12},{9,13},{10,... | collective-permute-start | bytes 884744 | tf_op jit(solution)/shard_map/ppermute | solution.py:22
  (6 other events, 8.1 us)

commit v3 on v2

v3 whole, which is shorter than its diff:
```python
import functools

import jax
import jax.numpy as jnp
from jax import lax
from jax.experimental import pallas as pl
from jax.experimental.pallas import tpu as pltpu
from jax.sharding import PartitionSpec as P

KERNEL_DILATION = 18
CHANNELS_PER_STEP = 256
F32, F16, BF16 = jnp.float32, jnp.float16, jnp.bfloat16


def from_behind(value, axis, steps):
    count = lax.axis_size(axis)
    leading, last = (max(0, -steps), min(count, count - steps))
    return lax.ppermute(value, axis, [(source, source + steps) for source in range(leading, last)])


def exchange(value, axis, bit):
    return lax.ppermute(value, axis, [(i, i ^ bit) for i in range(lax.axis_size(axis))])


def near_rows(tile):
    away, rest = divmod(KERNEL_DILATION, tile.shape[0])
    below = from_behind(tile[rest:], "space", -away)
    above = from_behind(tile[: tile.shape[0] - rest], "space", away)
    return below, above


def far_rows(tile):
    away, rest = divmod(KERNEL_DILATION, tile.shape[0])
    below = from_behind(tile[:rest], "space", -away - 1)
    above = from_behind(tile[tile.shape[0] - rest :], "space", away + 1)
    return below, above


def flat(piece):
    return piece.reshape(-1, piece.shape[-1])


def shift_columns(columns, pieces, out_ref, base):
    value = jnp.concatenate([ref[...].astype(F32) for ref in pieces])
    pixels, width = value.shape
    place = lax.broadcasted_iota(jnp.int32, (pixels, width), 0).astype(F32)
    column = place - jnp.floor((place + 0.5) * (1.0 / columns)) * columns
    ahead = pltpu.roll(value, pixels - KERNEL_DILATION, 0)
    behind = pltpu.roll(value, KERNEL_DILATION, 0)
    ahead = jnp.where(column < columns - KERNEL_DILATION, ahead, 0.0)
    behind = jnp.where(column >= KERNEL_DILATION, behind, 0.0)
    out_ref[:, base : base + width] = ahead.astype(BF16)
    out_ref[:, base + width : base + 2 * width] = value.astype(BF16)
    out_ref[:, base + 2 * width : base + 3 * width] = behind.astype(BF16)


def shift_rows(columns, cuts, pieces, out_ref):
    at = 0
    for row, cut in enumerate(cuts):
        width = pieces[at].shape[1]
        shift_columns(columns, pieces[at : at + cut], out_ref, 3 * row * width)
        at += cut


def place_in(order, member, block):
    spot = 0
    for axis, bit in order:
        spot = 2 * spot + ((member if axis == "dp" else block) // bit) % 2
    return spot


def kernel_term_kernel(columns, cuts, orders, parts, place_ref, scale_ref, *refs):
    images, pieces, outs, shifted_ref = refs[:parts], refs[parts:-3], refs[-3:-1], refs[-1]

    @pl.when(pl.program_id(0) == 0)
    def _():
        shift_rows(columns, cuts, pieces, shifted_ref)

    blocks = lax.axis_size("space")

    def products(side, out_ref):
        channels = out_ref.shape[1]
        for i, image_ref in enumerate(images):
            product = jnp.dot(image_ref[...].T, shifted_ref[...], preferred_element_type=F32)
            product = product * scale_ref[0]
            for j in range(blocks):
                block = jnp.bitwise_xor(j, place_ref[1])
                spots = [place_in(order, 2 * i, block) for order in orders]
                spot = jnp.where(place_ref[0] % 2 == side, spots[1], spots[0])
                out_ref[spot] = product[j * channels : (j + 1) * channels]

    for side, out_ref in enumerate(outs):

        @pl.when(pl.program_id(0) == side)
        def _():
            products(side, out_ref)


def kernel_term(columns, place, scale, image, rows_of, orders):
    pixels, channels = image.shape
    members, blocks = lax.axis_size("dp"), lax.axis_size("space")
    step, half = channels // members, members // 2
    pieces = [flat(piece) for row in rows_of for piece in row]
    cuts = tuple(len(row) for row in rows_of)
    width = 3 * len(cuts) * pieces[0].shape[1]

    def segment(i):
        return pl.BlockSpec(
            (pixels, step), lambda side, place: (0, jnp.bitwise_xor(2 * i + 1 - side, place[0]))
        )

    shape = (half * blocks, step // blocks, width)
    return pl.pallas_call(
        functools.partial(kernel_term_kernel, columns, cuts, orders, half),
        grid_spec=pltpu.PrefetchScalarGridSpec(
            num_scalar_prefetch=1,
            grid=(2,),
            in_specs=[
                pl.BlockSpec(memory_space=pltpu.SMEM),
                *[segment(i) for i in range(half)],
                *[pl.BlockSpec(piece.shape, lambda side, place: (0, 0)) for piece in pieces],
            ],
            out_specs=[pl.BlockSpec(shape, lambda side, place: (0, 0, 0))] * 2,
            scratch_shapes=[pltpu.VMEM((pixels, width), BF16)],
        ),
        out_shape=[jax.ShapeDtypeStruct(shape, F32)] * 2,
        compiler_params=pltpu.CompilerParams(vmem_limit_bytes=26 << 20),
        cost_estimate=pl.CostEstimate(
            flops=2 * pixels * channels * width,
            bytes_accessed=2 * pixels * channels + 4 * channels * width,
            transcendentals=0,
        ),
        name="kernel_term",
    )(place, scale, *[image] * half, *pieces)


def input_grad_kernel(columns, cuts, scale_ref, *refs):
    pieces = refs[: sum(cuts)]
    weight_ref = refs[len(pieces)]
    out_ref, wide_ref, taps_ref, shifted_ref = refs[-4:]
    step = out_ref.shape[1]
    width = weight_ref.shape[1]
    halves = width // 128

    @pl.when(pl.program_id(0) == 0)
    def _():
        shift_rows(columns, cuts, pieces, shifted_ref)

    for h in range(halves):
        wide_ref[h] = weight_ref[:, h * 128 : (h + 1) * 128].astype(F32)
    for t in range(9):
        for h in range(halves):
            base = t * width + h * 128
            taps_ref[:, base : base + 128] = wide_ref[h, pl.ds(t, step, stride=9), :].astype(BF16)
    total = lax.dot_general(
        shifted_ref[...], taps_ref[...], (((1,), (1,)), ((), ())), preferred_element_type=F32
    )
    out_ref[...] = (total * scale_ref[0]).astype(BF16)


def input_grad(columns, scale, rows_of, weight, first, count, before=None):
    pieces = [flat(piece) for row in rows_of for piece in row]
    cuts = tuple(len(row) for row in rows_of)
    pixels = sum(piece.shape[0] for piece in pieces) // 3
    rows, width = weight.shape
    channels = rows // 9
    step = CHANNELS_PER_STEP
    earlier = [] if before is None else [before]
    return pl.pallas_call(
        functools.partial(input_grad_kernel, columns, cuts),
        grid=(count,),
        in_specs=[
            pl.BlockSpec(memory_space=pltpu.SMEM),
            *[pl.BlockSpec(piece.shape, lambda i: (0, 0)) for piece in pieces],
            pl.BlockSpec((9 * step, width), lambda i: (i + first, 0)),
            *[pl.BlockSpec(memory_space=pl.ANY) for _ in earlier],
        ],
        out_specs=pl.BlockSpec((pixels, step), lambda i: (0, i + first)),
        out_shape=jax.ShapeDtypeStruct((pixels, channels), BF16),
        input_output_aliases={len(pieces) + 2: 0} if earlier else {},
        scratch_shapes=[
            pltpu.VMEM((width // 128, 9 * step, 128), F32),
            pltpu.VMEM((step, 9 * width), BF16),
            pltpu.VMEM((pixels, 9 * width), BF16),
        ],
        compiler_params=pltpu.CompilerParams(vmem_limit_bytes=18 << 20),
        cost_estimate=pl.CostEstimate(
            flops=2 * pixels * 9 * width * step * count,
            bytes_accessed=2 * (9 * step * width + pixels * step) * count,
            transcendentals=0,
        ),
        name="input_grad",
    )(scale, *pieces, pltpu.with_memory_space_constraint(weight, pltpu.HBM), *earlier)


def bits_of(axis):
    return [(axis, 1 << k) for k in reversed(range(lax.axis_size(axis).bit_length() - 1))]


def after(value, *others):
    return lax.optimization_barrier((value, others))[0]


def exchange_by_role(value, orders, step):
    members, blocks = lax.axis_size("dp"), lax.axis_size("space")
    pairs = []
    for member in range(members):
        for block in range(blocks):
            axis, bit = orders[member % 2][step]
            target = (member ^ bit, block) if axis == "dp" else (member, block ^ bit)
            pairs.append((member * blocks + block, target[0] * blocks + target[1]))
    return lax.ppermute(value, ("dp", "space"), pairs)


def kept(part):
    return part[: part.shape[0] // 2]


def sent(part):
    return part[part.shape[0] // 2 :].astype(F16)


def add(part, back):
    return part.astype(F32) + back.astype(F32)


def shards(features, grad_out, weight, alive):
    _, rows, columns, in_channels = features.shape
    out_channels = grad_out.shape[-1]
    pixels = rows * columns
    member_count = lax.axis_size("dp")
    core = ("dp", 1)
    across = [name for name in bits_of("dp") if name != core]
    along = bits_of("space")[::-1]
    first, inner, final_bit = along[:1], along[1:-1], along[-1:]
    orders = (across + first + inner + final_bit, first + inner + across + final_bit)
    centre_order = inner + across + first + final_bit

    own_alive = jnp.sum(alive).astype(F32)
    term_scale = (own_alive * (4.0 / member_count)).reshape(1)
    tile = grad_out.reshape(rows, columns, out_channels)
    image = features.reshape(pixels, in_channels)
    place = jnp.stack([lax.axis_index("dp"), lax.axis_index("space")]).astype(jnp.int32)

    def term(rows_of, orders, image=image):
        halves = kernel_term(columns, place, term_scale, image, rows_of, orders)
        return [value.astype(F16) for value in halves]

    def in_hbm(value):
        return pltpu.with_memory_space_constraint(value, pltpu.HBM)

    near_below, near_above = near_rows(tile)
    far_below, far_above = far_rows(tile)
    centre = term([[in_hbm(flat(tile))]], [centre_order] * 2, in_hbm(image))
    below, above, centre = lax.optimization_barrier(
        ((near_below, far_below), (far_above, near_above), centre)
    )

    back = exchange(centre[0], *core)
    lower = term([after(below, centre)], orders)
    lower, back = lax.optimization_barrier((lower, back))
    centre = add(centre[1], back)
    back = exchange(lower[0], *core)
    upper = term([after(above, lower, centre)], orders)
    upper, back = lax.optimization_barrier((upper, back))
    upper_back = exchange(upper[0], *core)
    others = [after(own_alive.reshape(1), upper[0])]
    for away in range(1, member_count):
        others.append(exchange(others[0], "dp", away))
    lower = add(lower[1], back)
    upper_back, others = lax.optimization_barrier((upper_back, others))
    upper = add(upper[1], upper_back)
    survivors = sum(others)
    scale = (own_alive / survivors).reshape(1)

    width = 3 * out_channels
    blocks = in_channels // CHANNELS_PER_STEP
    last = len(centre_order) - 1
    rows_of = [below, [in_hbm(flat(tile))], above]
    grad_features = None
    for step, name in enumerate(centre_order):
        ring_sent = [sent(lower), sent(upper)]
        centre_sent = sent(centre)
        if step < last:
            ring_sent = jnp.concatenate(ring_sent, axis=-1)
            centre_back = exchange(centre_sent, *name)
            ring_back = exchange_by_role(ring_sent, orders, step)
        else:
            ring_back = exchange(jnp.concatenate([*ring_sent, centre_sent], axis=-1), *name)
            centre_back = ring_back[..., 2 * width :]
        if step == 0:
            grad_features = input_grad(
                columns, scale, after(rows_of, ring_sent, centre_sent), weight, 0, blocks
            )
        ring_back, centre_back, grad_features = lax.optimization_barrier(
            (ring_back, centre_back, grad_features)
        )
        lower = add(kept(lower), ring_back[..., :width])
        upper = add(kept(upper), ring_back[..., width : 2 * width])
        centre = add(kept(centre), centre_back)
    final = jnp.concatenate([lower[0], centre[0], upper[0]], axis=-1)
    final = final * (member_count * 0.25 / survivors)
    return (final.reshape(-1, out_channels), grad_features.reshape(features.shape))


def solution(mesh):
    in_specs = (P("dp", "space", None, None), P("dp", "space", None, None), P(), P("dp"))
    out_specs = (P(("dp", "space"), None), P("dp", "space", None, None))
    return jax.shard_map(shards, mesh=mesh, in_specs=in_specs, out_specs=out_specs, check_vma=False)
```

time: 116 us -> 101 us (0.87)
  other arithmetic: 13.2 us -> 5.31 us
  local copies, waits for them, and re-layouts: 7.68 us -> 3.61 us
  waiting for transfers between devices: 30 us -> 26.8 us
  Pallas kernels: 33.2 us -> 30.6 us
  starting transfers between devices: 28.4 us -> 31 us
    add x12 -> x9, other arithmetic: 7.59 us -> 2.29 us  [add(): return part.astype(F32) + back.astype(F32)]
    convert_element_type x16 -> x6, other arithmetic: 4.73 us -> 1.49 us  [term(): return [value.astype(F16) for value in halves]]
    unnamed x28 -> x2, local copies, waits for them, and re-layouts: 4.5 us -> 1.62 us
    ppermute x9 -> x10, starting transfers between devices: 12.1 us -> 14.9 us  [exchange(): lax.ppermute(value, axis, [(i, i ^ bit) for i in range(lax.axis_size(axis...]
    pallas_call x3, Pallas kernels: 18 us -> 15.3 us  [kernel_term(): pl.pallas_call(functools.partial(kernel_term_kernel, columns, cuts, order...]
    ppermute x9 -> x10, waiting for transfers between devices: 29 us -> 26.8 us  [exchange(): lax.ppermute(value, axis, [(i, i ^ bit) for i in range(lax.axis_size(axis...]
    slice x4 -> x0, local copies, waits for them, and re-layouts: 1.19 us -> none  [part(): lax.index_in_dim(self.value, index, spot, keepdims=False)]
  transfers between devices with their start and end apart: 16 -> 17, of which waited for: 6 -> 4; matrix products, arithmetic and copies ran while one was open for 6% -> 3% of each run, Pallas kernels for 29% -> 30%
where the time goes in v3:
time: 101 us
  starting transfers between devices  31 us (31%)
  Pallas kernels  30.6 us (30%)
  waiting for transfers between devices  26.8 us (27%)
  other arithmetic  5.31 us (5%)
  between operations  3.74 us (4%)
  local copies, waits for them, and re-layouts  3.61 us (4%)
    ppermute x10, waiting for transfers between devices, exchange(): lax.ppermute(value, axis, [(i, i ^ bit) for i in range(lax.axis_size(axis...  26.8 us
    pallas_call x1, Pallas kernels, input_grad(): pl.pallas_call(functools.partial(input_grad_kernel, columns, cuts), grid=...  15.3 us
    pallas_call x3, Pallas kernels, kernel_term(): pl.pallas_call(functools.partial(kernel_term_kernel, columns, cuts, order...  15.3 us
    ppermute x10, starting transfers between devices, exchange(): lax.ppermute(value, axis, [(i, i ^ bit) for i in range(lax.axis_size(axis...  14.9 us
    ppermute x4, starting transfers between devices, from_behind(): lax.ppermute(value, axis, [(source, source + steps) for source in range(l...  12 us
    ppermute x3, starting transfers between devices, exchange_by_role(): return lax.ppermute(value, ('dp', 'space'), pairs)  4.1 us
    add x9, other arithmetic, add(): return part.astype(F32) + back.astype(F32)  2.29 us
  transfers between devices with their start and end apart: 17, of which 4 were waited for; matrix products, arithmetic and copies ran while one was open for 3% of the time, Pallas kernels for 30%

profile of v3, /device:TPU:0, one launch (start us, length us, event | category | flops | bytes accessed | tf_op | source)
XLA Modules:
  0.0 101.1 jit_solution(18132811740019563066)
XLA Ops:
  0.6 1.1 %slice_bitcast_fusion = (bf16[6,72,256]{2,1,0:T(8,128)(2,1)S(1)}, bf16[6,72,256]{2,1,0:T(8,128)(2,1)S(1)}) fusion(bf16[1,12,72,256]{3,2,1,0:T(8,128)(2,1)} %param.5), kind=kLoop, calls=%fused_computation.26 | loop fusion | bytes 884736 | tf_op jit(solution)/shard_map/slice | solution.py:34
  1.7 4.9 %collective-permute-start.3 = (bf16[6,72,256]{2,1,0:T(8,128)(2,1)S(1)}, bf16[6,72,256]{2,1,0:T(8,128)(2,1)S(1)}, u32[]{:S(2)}, u32[]{:S(2)}) collective-permute-start(bf16[6,72,256]{2,1,0:T(8,128)(2,1)S(1)} %get-tuple-element.96), channel_id=1, source_target_pairs={{0,1},{1,2},{2,3},{3,4},{4,5},{5,6},{6,7},{8,9},{9,10},{10,11},{11... | collective-permute-start | bytes 663560 | tf_op jit(solution)/shard_map/ppermute | solution.py:18
  6.6 1.3 %collective-permute-start.1 = (bf16[6,72,256]{2,1,0:T(8,128)(2,1)S(1)}, bf16[6,72,256]{2,1,0:T(8,128)(2,1)S(1)}, u32[]{:S(2)}, u32[]{:S(2)}) collective-permute-start(bf16[6,72,256]{2,1,0:T(8,128)(2,1)S(1)} %get-tuple-element.96), channel_id=1, source_target_pairs={{2,0},{3,1},{4,2},{5,3},{6,4},{7,5},{10,8},{11,9},{12,10},{13,11},... | collective-permute-start | bytes 663560 | tf_op jit(solution)/shard_map/ppermute | solution.py:18
  7.9 4.6 %collective-permute-start.2 = (bf16[6,72,256]{2,1,0:T(8,128)(2,1)S(1)}, bf16[6,72,256]{2,1,0:T(8,128)(2,1)S(1)}, u32[]{:S(2)}, u32[]{:S(2)}) collective-permute-start(bf16[6,72,256]{2,1,0:T(8,128)(2,1)S(1)} %get-tuple-element.97), channel_id=1, source_target_pairs={{0,2},{1,3},{2,4},{3,5},{4,6},{5,7},{8,10},{9,11},{10,12},{11,13},... | collective-permute-start | bytes 663560 | tf_op jit(solution)/shard_map/ppermute | solution.py:18
  12.5 1.3 %collective-permute-start = (bf16[6,72,256]{2,1,0:T(8,128)(2,1)S(1)}, bf16[6,72,256]{2,1,0:T(8,128)(2,1)S(1)}, u32[]{:S(2)}, u32[]{:S(2)}) collective-permute-start(bf16[6,72,256]{2,1,0:T(8,128)(2,1)S(1)} %get-tuple-element.97), channel_id=1, source_target_pairs={{1,0},{2,1},{3,2},{4,3},{5,4},{6,5},{7,6},{9,8},{10,9},{11,10},{12... | collective-permute-start | bytes 663560 | tf_op jit(solution)/shard_map/ppermute | solution.py:18
  14.5 5.9 %kernel_term.3 = (f32[16,64,768]{2,1,0:T(8,128)S(1)}, f32[16,64,768]{2,1,0:T(8,128)S(1)}) custom-call(s32[2]{0:T(128)S(1)} %pad_add_fusion.place_ref, f32[1]{0:T(128)} %convert_element_type.88.scale_ref, bf16[864,2048]{1,0:T(8,128)(2,1)} %bitcast.24, bf16[864,2048]{1,0:T(8,128)(2,1)} %bitcast.25, bf16[864,256]{1,0:T(8,128)(2,1)} %bitcast.38), custom_call_target="tpu_custom_call" | custom-call | flops 2717908992 | bytes 9830400 | tf_op jit(solution)/shard_map/kernel_term/pallas_call | solution.py:113
  21.0 1.6 %copy-done = bf16[1,12,72,2048]{3,2,1,0:T(8,128)(2,1)S(1)} copy-done((bf16[1,12,72,2048]{3,2,1,0:T(8,128)(2,1)S(1)}, bf16[1,12,72,2048]{3,2,1,0:T(8,128)(2,1)}, u32[]{:S(2)}) %copy-start) | copy-done | bytes 3538968
  22.6 4.6 %kernel_term.4 = (f32[16,64,768]{2,1,0:T(8,128)S(1)}, f32[16,64,768]{2,1,0:T(8,128)S(1)}) custom-call(s32[2]{0:T(128)S(1)} %pad_add_fusion.place_ref, f32[1]{0:T(128)} %convert_element_type.88.scale_ref, bf16[864,2048]{1,0:T(8,128)(2,1)S(1)} %bitcast.26, bf16[864,2048]{1,0:T(8,128)(2,1)S(1)} %bitcast.27, bf16[432,256]{1,0:T(8,128)(2,1)S(1)} %bitcast.36, ...), custom_call_target="tpu_custom_call" | custom-call | flops 2717908992 | bytes 9830400 | tf_op jit(solution)/shard_map/kernel_term/pallas_call | solution.py:113
  28.3 4.8 %kernel_term.5 = (f32[16,64,768]{2,1,0:T(8,128)S(1)}, f32[16,64,768]{2,1,0:T(8,128)S(1)}) custom-call(s32[2]{0:T(128)S(1)} %pad_add_fusion.place_ref, f32[1]{0:T(128)} %convert_element_type.88.scale_ref, bf16[864,2048]{1,0:T(8,128)(2,1)S(1)} %bitcast.28, bf16[864,2048]{1,0:T(8,128)(2,1)S(1)} %bitcast.29, bf16[432,256]{1,0:T(8,128)(2,1)S(1)} %bitcast.34, ...), custom_call_target="tpu_custom_call" | custom-call | flops 2717908992 | bytes 9830400 | tf_op jit(solution)/shard_map/kernel_term/pallas_call | solution.py:113
  34.2 2.5 %collective-permute-start.9 = (f32[1]{0:T(128)}, f32[1]{0:T(128)}, u32[]{:S(2)}, u32[]{:S(2)}) collective-permute-start(f32[1]{0:T(128)} %convert_element_type.88.scale_ref), channel_id=1, source_target_pairs={{0,24},{8,16},{16,8},{24,0},{1,25},{9,17},{17,9},{25,1},{2,26},{10... | collective-permute-start | bytes 20 | tf_op jit(solution)/shard_map/ppermute | solution.py:22
  36.7 1.8 %collective-permute-start.8 = (f32[1]{0:T(128)}, f32[1]{0:T(128)}, u32[]{:S(2)}, u32[]{:S(2)}) collective-permute-start(f32[1]{0:T(128)} %convert_element_type.88.scale_ref), channel_id=1, source_target_pairs={{0,16},{8,24},{16,0},{24,8},{1,17},{9,25},{17,1},{25,9},{2,18},{10... | collective-permute-start | bytes 20 | tf_op jit(solution)/shard_map/ppermute | solution.py:22
  38.5 1.0 collective-permute-start.7
  41.3 1.3 %collective-permute-start.10 = (f16[8,64,1536]{2,1,0:T(8,128)(2,1)S(1)}, f16[8,64,1536]{2,1,0:T(8,128)(2,1)S(1)}, u32[]{:S(2)}, u32[]{:S(2)}) collective-permute-start(f16[8,64,1536]{2,1,0:T(8,128)(2,1)S(1)} %pad_maximum_fusion), channel_id=1, source_target_pairs={{0,16},{1,17},{2,18},{3,19},{4,20},{5,21},{6,22},{7,23},{8,9},{9,8... | collective-permute-start | bytes 4718600 | tf_op jit(solution)/shard_map/ppermute | solution.py:212
  42.7 3.7 %collective-permute-start.11 = (f16[8,64,768]{2,1,0:T(8,128)(2,1)S(1)}, f16[8,64,768]{2,1,0:T(8,128)(2,1)S(1)}, u32[]{:S(2)}, u32[]{:S(2)}) collective-permute-start(f16[8,64,768]{2,1,0:T(8,128)(2,1)S(1)} %slice_convert_fusion), channel_id=1, source_target_pairs={{0,2},{1,3},{2,0},{3,1},{4,6},{5,7},{6,4},{7,5},{8,10},{9,11},{10,... | collective-permute-start | bytes 2359304 | tf_op jit(solution)/shard_map/ppermute | solution.py:22
  48.4 15.3 %input_grad.1 = bf16[864,2048]{1,0:T(8,128)(2,1)} custom-call(f32[1]{0:T(128)S(6)} %div.7.scale_ref, bf16[432,256]{1,0:T(8,128)(2,1)S(1)} %bitcast.37, bf16[432,256]{1,0:T(8,128)(2,1)S(1)} %bitcast.33, bf16[864,256]{1,0:T(8,128)(2,1)} %bitcast.39, bf16[432,256]{1,0:T(8,128)(2,1)S(1)} %bitcast.35, bf16[432,256]{1,0:T(8,128)(2,1)S(1)} %bitcast.31, ...), custom_call_target="tpu_custom_call" | custom-call | flops 8153726976 | bytes 12976128 | tf_op jit(solution)/shard_map/input_grad/pallas_call | solution.py:169
  64.4 1.2 %collective-permute-start.12 = (f16[4,64,1536]{2,1,0:T(8,128)(2,1)S(1)}, f16[4,64,1536]{2,1,0:T(8,128)(2,1)S(1)}, u32[]{:S(2)}, u32[]{:S(2)}) collective-permute-start(f16[4,64,1536]{2,1,0:T(8,128)(2,1)S(1)} %pad_maximum_fusion.1), channel_id=1, source_target_pairs={{0,1},{1,0},{2,3},{3,2},{4,5},{5,4},{6,7},{7,6},{8,10},{9,11},{10,... | collective-permute-start | bytes 2359304 | tf_op jit(solution)/shard_map/ppermute | solution.py:212
  65.7 1.6 %collective-permute-start.13 = (f16[4,64,768]{2,1,0:T(8,128)(2,1)S(1)}, f16[4,64,768]{2,1,0:T(8,128)(2,1)S(1)}, u32[]{:S(2)}, u32[]{:S(2)}) collective-permute-start(f16[4,64,768]{2,1,0:T(8,128)(2,1)S(1)} %slice_convert_fusion.3), channel_id=1, source_target_pairs={{0,16},{8,24},{16,0},{24,8},{1,17},{9,25},{17,1},{25,9},{2,18},{10... | collective-permute-start | bytes 1179656 | tf_op jit(solution)/shard_map/ppermute | solution.py:22
  67.3 9.2 %collective-permute-done.13 = f16[4,64,768]{2,1,0:T(8,128)(2,1)S(1)} collective-permute-done((f16[4,64,768]{2,1,0:T(8,128)(2,1)S(1)}, f16[4,64,768]{2,1,0:T(8,128)(2,1)S(1)}, u32[]{:S(2)}, u32[]{:S(2)}) %collective-permute-start.13) | collective-permute-done | bytes 393248 | tf_op jit(solution)/shard_map/ppermute | solution.py:22
  77.0 1.6 %collective-permute-start.14 = (f16[2,64,1536]{2,1,0:T(8,128)(2,1)S(1)}, f16[2,64,1536]{2,1,0:T(8,128)(2,1)S(1)}, u32[]{:S(2)}, u32[]{:S(2)}) collective-permute-start(f16[2,64,1536]{2,1,0:T(8,128)(2,1)S(1)} %pad_maximum_fusion.2), channel_id=1, source_target_pairs={{0,2},{1,3},{2,0},{3,1},{4,6},{5,7},{6,4},{7,5},{8,24},{9,25},{10,... | collective-permute-start | bytes 1179656 | tf_op jit(solution)/shard_map/ppermute | solution.py:212
  78.6 1.3 %collective-permute-start.15 = (f16[2,64,768]{2,1,0:T(8,128)(2,1)S(1)}, f16[2,64,768]{2,1,0:T(8,128)(2,1)S(1)}, u32[]{:S(2)}, u32[]{:S(2)}) collective-permute-start(f16[2,64,768]{2,1,0:T(8,128)(2,1)S(1)} %slice_convert_fusion.6), channel_id=1, source_target_pairs={{0,1},{1,0},{2,3},{3,2},{4,5},{5,4},{6,7},{7,6},{8,9},{9,8},{10,11... | collective-permute-start | bytes 589832 | tf_op jit(solution)/shard_map/ppermute | solution.py:22
  79.9 5.2 %collective-permute-done.15 = f16[2,64,768]{2,1,0:T(8,128)(2,1)S(1)} collective-permute-done((f16[2,64,768]{2,1,0:T(8,128)(2,1)S(1)}, f16[2,64,768]{2,1,0:T(8,128)(2,1)S(1)}, u32[]{:S(2)}, u32[]{:S(2)}) %collective-permute-start.15) | collective-permute-done | bytes 196640 | tf_op jit(solution)/shard_map/ppermute | solution.py:22
  85.4 2.4 %collective-permute-start.16 = (f16[1,64,2304]{2,1,0:T(8,128)(2,1)S(1)}, f16[1,64,2304]{2,1,0:T(8,128)(2,1)S(1)}, u32[]{:S(2)}, u32[]{:S(2)}) collective-permute-start(f16[1,64,2304]{2,1,0:T(8,128)(2,1)S(1)} %pad_maximum_fusion.3), channel_id=1, source_target_pairs={{0,4},{1,5},{2,6},{3,7},{4,0},{5,1},{6,2},{7,3},{8,12},{9,13},{10,... | collective-permute-start | bytes 884744 | tf_op jit(solution)/shard_map/ppermute | solution.py:22
  87.8 12.2 %collective-permute-done.16 = f16[1,64,2304]{2,1,0:T(8,128)(2,1)S(1)} collective-permute-done((f16[1,64,2304]{2,1,0:T(8,128)(2,1)S(1)}, f16[1,64,2304]{2,1,0:T(8,128)(2,1)S(1)}, u32[]{:S(2)}, u32[]{:S(2)}) %collective-permute-start.16) | collective-permute-done | bytes 294944 | tf_op jit(solution)/shard_map/ppermute | solution.py:22
  100.2 0.9 mul.17
  (53 shorter events, 6.3 us)
Async XLA Ops:
  1.7 19.2 %collective-permute-start.3 = (bf16[6,72,256]{2,1,0:T(8,128)(2,1)S(1)}, bf16[6,72,256]{2,1,0:T(8,128)(2,1)S(1)}, u32[]{:S(2)}, u32[]{:S(2)}) collective-permute-start(bf16[6,72,256]{2,1,0:T(8,128)(2,1)S(1)} %get-tuple-element.96), channel_id=1, source_target_pairs={{0,1},{1,2},{2,3},{3,4},{4,5},{5,6},{6,7},{8,9},{9,10},{10,11},{11... | collective-permute-start | bytes 663560 | tf_op jit(solution)/shard_map/ppermute | solution.py:18
  6.6 14.3 %collective-permute-start.1 = (bf16[6,72,256]{2,1,0:T(8,128)(2,1)S(1)}, bf16[6,72,256]{2,1,0:T(8,128)(2,1)S(1)}, u32[]{:S(2)}, u32[]{:S(2)}) collective-permute-start(bf16[6,72,256]{2,1,0:T(8,128)(2,1)S(1)} %get-tuple-element.96), channel_id=1, source_target_pairs={{2,0},{3,1},{4,2},{5,3},{6,4},{7,5},{10,8},{11,9},{12,10},{13,11},... | collective-permute-start | bytes 663560 | tf_op jit(solution)/shard_map/ppermute | solution.py:18
  7.9 13.0 %collective-permute-start.2 = (bf16[6,72,256]{2,1,0:T(8,128)(2,1)S(1)}, bf16[6,72,256]{2,1,0:T(8,128)(2,1)S(1)}, u32[]{:S(2)}, u32[]{:S(2)}) collective-permute-start(bf16[6,72,256]{2,1,0:T(8,128)(2,1)S(1)} %get-tuple-element.97), channel_id=1, source_target_pairs={{0,2},{1,3},{2,4},{3,5},{4,6},{5,7},{8,10},{9,11},{10,12},{11,13},... | collective-permute-start | bytes 663560 | tf_op jit(solution)/shard_map/ppermute | solution.py:18
  12.5 8.5 %collective-permute-start = (bf16[6,72,256]{2,1,0:T(8,128)(2,1)S(1)}, bf16[6,72,256]{2,1,0:T(8,128)(2,1)S(1)}, u32[]{:S(2)}, u32[]{:S(2)}) collective-permute-start(bf16[6,72,256]{2,1,0:T(8,128)(2,1)S(1)} %get-tuple-element.97), channel_id=1, source_target_pairs={{1,0},{2,1},{3,2},{4,3},{5,4},{6,5},{7,6},{9,8},{10,9},{11,10},{12... | collective-permute-start | bytes 663560 | tf_op jit(solution)/shard_map/ppermute | solution.py:18
  20.6 2.0 %copy-start = (bf16[1,12,72,2048]{3,2,1,0:T(8,128)(2,1)S(1)}, bf16[1,12,72,2048]{3,2,1,0:T(8,128)(2,1)}, u32[]{:S(2)}) copy-start(bf16[1,12,72,2048]{3,2,1,0:T(8,128)(2,1)} %param.4) | copy-start | bytes 10616836
  20.9 6.9 %collective-permute-start.4 = (f16[16,64,768]{2,1,0:T(8,128)(2,1)S(1)}, f16[16,64,768]{2,1,0:T(8,128)(2,1)S(1)}, u32[]{:S(2)}, u32[]{:S(2)}) collective-permute-start(f16[16,64,768]{2,1,0:T(8,128)(2,1)S(1)} %convert_element_type.89), channel_id=1, source_target_pairs={{0,8},{8,0},{16,24},{24,16},{1,9},{9,1},{17,25},{25,17},{2,10},{10... | collective-permute-start | bytes 4718600 | tf_op jit(solution)/shard_map/ppermute | solution.py:22
  27.8 5.8 %collective-permute-start.5 = (f16[16,64,768]{2,1,0:T(8,128)(2,1)S(1)}, f16[16,64,768]{2,1,0:T(8,128)(2,1)S(1)}, u32[]{:S(2)}, u32[]{:S(2)}) collective-permute-start(f16[16,64,768]{2,1,0:T(8,128)(2,1)S(1)} %convert_element_type.91), channel_id=1, source_target_pairs={{0,8},{8,0},{16,24},{24,16},{1,9},{9,1},{17,25},{25,17},{2,10},{10... | collective-permute-start | bytes 4718600 | tf_op jit(solution)/shard_map/ppermute | solution.py:22
  33.7 6.5 %collective-permute-start.6 = (f16[16,64,768]{2,1,0:T(8,128)(2,1)S(1)}, f16[16,64,768]{2,1,0:T(8,128)(2,1)S(1)}, u32[]{:S(2)}, u32[]{:S(2)}) collective-permute-start(f16[16,64,768]{2,1,0:T(8,128)(2,1)S(1)} %convert_element_type.96), channel_id=1, source_target_pairs={{0,8},{8,0},{16,24},{24,16},{1,9},{9,1},{17,25},{25,17},{2,10},{10... | collective-permute-start | bytes 4718600 | tf_op jit(solution)/shard_map/ppermute | solution.py:22
  34.2 5.7 %collective-permute-start.9 = (f32[1]{0:T(128)}, f32[1]{0:T(128)}, u32[]{:S(2)}, u32[]{:S(2)}) collective-permute-start(f32[1]{0:T(128)} %convert_element_type.88.scale_ref), channel_id=1, source_target_pairs={{0,24},{8,16},{16,8},{24,0},{1,25},{9,17},{17,9},{25,1},{2,26},{10... | collective-permute-start | bytes 20 | tf_op jit(solution)/shard_map/ppermute | solution.py:22
  36.7 3.5 %collective-permute-start.8 = (f32[1]{0:T(128)}, f32[1]{0:T(128)}, u32[]{:S(2)}, u32[]{:S(2)}) collective-permute-start(f32[1]{0:T(128)} %convert_element_type.88.scale_ref), channel_id=1, source_target_pairs={{0,16},{8,24},{16,0},{24,8},{1,17},{9,25},{17,1},{25,9},{2,18},{10... | collective-permute-start | bytes 20 | tf_op jit(solution)/shard_map/ppermute | solution.py:22
  38.5 1.7 %collective-permute-start.7 = (f32[1]{0:T(128)}, f32[1]{0:T(128)}, u32[]{:S(2)}, u32[]{:S(2)}) collective-permute-start(f32[1]{0:T(128)} %convert_element_type.88.scale_ref), channel_id=1, source_target_pairs={{0,8},{8,0},{16,24},{24,16},{1,9},{9,1},{17,25},{25,17},{2,10},{10... | collective-permute-start | bytes 20 | tf_op jit(solution)/shard_map/ppermute | solution.py:22
  41.3 22.4 %collective-permute-start.10 = (f16[8,64,1536]{2,1,0:T(8,128)(2,1)S(1)}, f16[8,64,1536]{2,1,0:T(8,128)(2,1)S(1)}, u32[]{:S(2)}, u32[]{:S(2)}) collective-permute-start(f16[8,64,1536]{2,1,0:T(8,128)(2,1)S(1)} %pad_maximum_fusion), channel_id=1, source_target_pairs={{0,16},{1,17},{2,18},{3,19},{4,20},{5,21},{6,22},{7,23},{8,9},{9,8... | collective-permute-start | bytes 4718600 | tf_op jit(solution)/shard_map/ppermute | solution.py:212
  42.7 21.0 %collective-permute-start.11 = (f16[8,64,768]{2,1,0:T(8,128)(2,1)S(1)}, f16[8,64,768]{2,1,0:T(8,128)(2,1)S(1)}, u32[]{:S(2)}, u32[]{:S(2)}) collective-permute-start(f16[8,64,768]{2,1,0:T(8,128)(2,1)S(1)} %slice_convert_fusion), channel_id=1, source_target_pairs={{0,2},{1,3},{2,0},{3,1},{4,6},{5,7},{6,4},{7,5},{8,10},{9,11},{10,... | collective-permute-start | bytes 2359304 | tf_op jit(solution)/shard_map/ppermute | solution.py:22
  64.4 12.1 %collective-permute-start.12 = (f16[4,64,1536]{2,1,0:T(8,128)(2,1)S(1)}, f16[4,64,1536]{2,1,0:T(8,128)(2,1)S(1)}, u32[]{:S(2)}, u32[]{:S(2)}) collective-permute-start(f16[4,64,1536]{2,1,0:T(8,128)(2,1)S(1)} %pad_maximum_fusion.1), channel_id=1, source_target_pairs={{0,1},{1,0},{2,3},{3,2},{4,5},{5,4},{6,7},{7,6},{8,10},{9,11},{10,... | collective-permute-start | bytes 2359304 | tf_op jit(solution)/shard_map/ppermute | solution.py:212
  65.7 10.7 %collective-permute-start.13 = (f16[4,64,768]{2,1,0:T(8,128)(2,1)S(1)}, f16[4,64,768]{2,1,0:T(8,128)(2,1)S(1)}, u32[]{:S(2)}, u32[]{:S(2)}) collective-permute-start(f16[4,64,768]{2,1,0:T(8,128)(2,1)S(1)} %slice_convert_fusion.3), channel_id=1, source_target_pairs={{0,16},{8,24},{16,0},{24,8},{1,17},{9,25},{17,1},{25,9},{2,18},{10... | collective-permute-start | bytes 1179656 | tf_op jit(solution)/shard_map/ppermute | solution.py:22
  77.0 8.1 %collective-permute-start.14 = (f16[2,64,1536]{2,1,0:T(8,128)(2,1)S(1)}, f16[2,64,1536]{2,1,0:T(8,128)(2,1)S(1)}, u32[]{:S(2)}, u32[]{:S(2)}) collective-permute-start(f16[2,64,1536]{2,1,0:T(8,128)(2,1)S(1)} %pad_maximum_fusion.2), channel_id=1, source_target_pairs={{0,2},{1,3},{2,0},{3,1},{4,6},{5,7},{6,4},{7,5},{8,24},{9,25},{10,... | collective-permute-start | bytes 1179656 | tf_op jit(solution)/shard_map/ppermute | solution.py:212
  78.6 6.5 %collective-permute-start.15 = (f16[2,64,768]{2,1,0:T(8,128)(2,1)S(1)}, f16[2,64,768]{2,1,0:T(8,128)(2,1)S(1)}, u32[]{:S(2)}, u32[]{:S(2)}) collective-permute-start(f16[2,64,768]{2,1,0:T(8,128)(2,1)S(1)} %slice_convert_fusion.6), channel_id=1, source_target_pairs={{0,1},{1,0},{2,3},{3,2},{4,5},{5,4},{6,7},{7,6},{8,9},{9,8},{10,11... | collective-permute-start | bytes 589832 | tf_op jit(solution)/shard_map/ppermute | solution.py:22
  85.4 14.6 %collective-permute-start.16 = (f16[1,64,2304]{2,1,0:T(8,128)(2,1)S(1)}, f16[1,64,2304]{2,1,0:T(8,128)(2,1)S(1)}, u32[]{:S(2)}, u32[]{:S(2)}) collective-permute-start(f16[1,64,2304]{2,1,0:T(8,128)(2,1)S(1)} %pad_maximum_fusion.3), channel_id=1, source_target_pairs={{0,4},{1,5},{2,6},{3,7},{4,0},{5,1},{6,2},{7,3},{8,12},{9,13},{10,... | collective-permute-start | bytes 884744 | tf_op jit(solution)/shard_map/ppermute | solution.py:22

commit v4 on v3

--- a/solution.py
+++ b/solution.py
@@ -22,18 +22,28 @@
     return lax.ppermute(value, axis, [(i, i ^ bit) for i in range(lax.axis_size(axis))])
 
 
-def near_rows(tile):
+def either(first, second):
+    return jnp.where(lax.axis_index("dp") % 2 == 0, first, second)
+
+
+def halo_rows(tile):
+    members, blocks = lax.axis_size("dp"), lax.axis_size("space")
     away, rest = divmod(KERNEL_DILATION, tile.shape[0])
-    below = from_behind(tile[rest:], "space", -away)
-    above = from_behind(tile[: tile.shape[0] - rest], "space", away)
-    return below, above
-
-
-def far_rows(tile):
-    away, rest = divmod(KERNEL_DILATION, tile.shape[0])
-    below = from_behind(tile[:rest], "space", -away - 1)
-    above = from_behind(tile[tile.shape[0] - rest :], "space", away + 1)
-    return below, above
+    assert tile.shape[0] == 2 * rest
+
+    def fetched(value, distance):
+        pairs = []
+        for member in range(members):
+            for block in range(blocks):
+                target = block + distance * (1 if member % 2 else -1)
+                if 0 <= target < blocks:
+                    pairs.append((member * blocks + block, member * blocks + target))
+        return lax.ppermute(value, ("dp", "space"), pairs)
+
+    tiles = (tile, exchange(tile, "dp", 1))
+    near = fetched(jnp.stack([either(t[rest:], t[:rest]) for t in tiles]), away)
+    far = fetched(jnp.stack([either(t[:rest], t[rest:]) for t in tiles]), away + 1)
+    return near, far
 
 
 def flat(piece):
@@ -43,8 +53,9 @@
 def shift_columns(columns, pieces, out_ref, base):
     value = jnp.concatenate([ref[...].astype(F32) for ref in pieces])
     pixels, width = value.shape
-    place = lax.broadcasted_iota(jnp.int32, (pixels, width), 0).astype(F32)
+    place = lax.broadcasted_iota(jnp.int32, (pixels, 128), 0).astype(F32)
     column = place - jnp.floor((place + 0.5) * (1.0 / columns)) * columns
+    column = jnp.concatenate([column] * (width // 128), axis=1)
     ahead = pltpu.roll(value, pixels - KERNEL_DILATION, 0)
     behind = pltpu.roll(value, KERNEL_DILATION, 0)
     ahead = jnp.where(column < columns - KERNEL_DILATION, ahead, 0.0)
@@ -69,8 +80,11 @@
     return spot
 
 
-def kernel_term_kernel(columns, cuts, orders, parts, place_ref, scale_ref, *refs):
-    images, pieces, outs, shifted_ref = refs[:parts], refs[parts:-3], refs[-3:-1], refs[-1]
+def kernel_term_kernel(columns, cuts, streams, parts, turned, place_ref, scale_ref, *refs):
+    count = 1 if turned else parts
+    images, pieces, outs, shifted_ref = refs[:count], refs[count:-3], refs[-3:-1], refs[-1]
+    if not turned:
+        pieces, turned_ref = pieces[:-1], pieces[-1]
 
     @pl.when(pl.program_id(0) == 0)
     def _():
@@ -80,14 +94,23 @@
 
     def products(side, out_ref):
         channels = out_ref.shape[1]
-        for i, image_ref in enumerate(images):
-            product = jnp.dot(image_ref[...].T, shifted_ref[...], preferred_element_type=F32)
+        for i in range(parts):
+            if turned:
+                image = images[0][0, i]
+            else:
+                image = images[i][...].T
+                turned_ref[0, i] = image
+            product = jnp.dot(image, shifted_ref[...], preferred_element_type=F32)
             product = product * scale_ref[0]
             for j in range(blocks):
                 block = jnp.bitwise_xor(j, place_ref[1])
-                spots = [place_in(order, 2 * i, block) for order in orders]
-                spot = jnp.where(place_ref[0] % 2 == side, spots[1], spots[0])
-                out_ref[spot] = product[j * channels : (j + 1) * channels]
+                rows = product[j * channels : (j + 1) * channels]
+                at = 0
+                for width, orders in streams:
+                    spots = [place_in(order, 2 * i, block) for order in orders]
+                    spot = jnp.where(place_ref[0] % 2 == side, spots[1], spots[0])
+                    out_ref[spot, :, at : at + width] = rows[:, at : at + width]
+                    at += width
 
     for side, out_ref in enumerate(outs):
 
@@ -96,8 +119,9 @@
             products(side, out_ref)
 
 
-def kernel_term(columns, place, scale, image, rows_of, orders):
-    pixels, channels = image.shape
+def kernel_term(columns, place, scale, image, rows_of, streams, turned):
+    channels = image.size // image.shape[-1] if turned else image.shape[1]
+    pixels = image.shape[-1] if turned else image.shape[0]
     members, blocks = lax.axis_size("dp"), lax.axis_size("space")
     step, half = channels // members, members // 2
     pieces = [flat(piece) for row in rows_of for piece in row]
@@ -109,21 +133,25 @@
             (pixels, step), lambda side, place: (0, jnp.bitwise_xor(2 * i + 1 - side, place[0]))
         )
 
-    shape = (half * blocks, step // blocks, width)
+    shapes = [(half * blocks, step // blocks, width)] * 2
+    turned_block = pl.BlockSpec((1, half, step, pixels), lambda side, place: (side, 0, 0, 0))
+    turned_shape = jax.ShapeDtypeStruct((2, half, step, pixels), BF16)
     return pl.pallas_call(
-        functools.partial(kernel_term_kernel, columns, cuts, orders, half),
+        functools.partial(kernel_term_kernel, columns, cuts, streams, half, turned),
         grid_spec=pltpu.PrefetchScalarGridSpec(
             num_scalar_prefetch=1,
             grid=(2,),
             in_specs=[
                 pl.BlockSpec(memory_space=pltpu.SMEM),
-                *[segment(i) for i in range(half)],
+                *([turned_block] if turned else [segment(i) for i in range(half)]),
                 *[pl.BlockSpec(piece.shape, lambda side, place: (0, 0)) for piece in pieces],
             ],
-            out_specs=[pl.BlockSpec(shape, lambda side, place: (0, 0, 0))] * 2,
+            out_specs=([] if turned else [turned_block])
+            + [pl.BlockSpec(shape, lambda side, place: (0, 0, 0)) for shape in shapes],
             scratch_shapes=[pltpu.VMEM((pixels, width), BF16)],
         ),
-        out_shape=[jax.ShapeDtypeStruct(shape, F32)] * 2,
+        out_shape=([] if turned else [turned_shape])
+        + [jax.ShapeDtypeStruct(shape, F32) for shape in shapes],
         compiler_params=pltpu.CompilerParams(vmem_limit_bytes=26 << 20),
         cost_estimate=pl.CostEstimate(
             flops=2 * pixels * channels * width,
@@ -131,7 +159,7 @@
             transcendentals=0,
         ),
         name="kernel_term",
-    )(place, scale, *[image] * half, *pieces)
+    )(place, scale, *[image] * (1 if turned else half), *pieces)
 
 
 def input_grad_kernel(columns, cuts, scale_ref, *refs):
@@ -242,63 +270,75 @@
     image = features.reshape(pixels, in_channels)
     place = jnp.stack([lax.axis_index("dp"), lax.axis_index("space")]).astype(jnp.int32)
 
-    def term(rows_of, orders, image=image):
-        halves = kernel_term(columns, place, term_scale, image, rows_of, orders)
-        return [value.astype(F16) for value in halves]
+    def term(image, rows_of, streams, turned=True):
+        *given, first, second = kernel_term(
+            columns, place, term_scale, image, rows_of, streams, turned
+        )
+        return [*given, first.astype(F16), second.astype(F16)]
 
     def in_hbm(value):
         return pltpu.with_memory_space_constraint(value, pltpu.HBM)
 
-    near_below, near_above = near_rows(tile)
-    far_below, far_above = far_rows(tile)
-    centre = term([[in_hbm(flat(tile))]], [centre_order] * 2, in_hbm(image))
-    below, above, centre = lax.optimization_barrier(
-        ((near_below, far_below), (far_above, near_above), centre)
+    near, far = halo_rows(tile)
+    width = 3 * out_channels
+    image, *centre = term(
+        in_hbm(image), [[in_hbm(flat(tile))]], [(width, [centre_order] * 2)], False
     )
-
+    alive_all = [own_alive.reshape(1)]
+    for away in range(1, member_count):
+        alive_all.append(exchange(alive_all[0], "dp", away))
+    near, far, centre, alive_all = lax.optimization_barrier((near, far, centre, alive_all))
+    survivors = sum(alive_all)
+    scale = own_alive / survivors
+
+    first_rows = either(near[0], far[0]), either(far[0], near[0])
+    other = exchange(jnp.stack([near[1], far[1]]), *core)
     back = exchange(centre[0], *core)
-    lower = term([after(below, centre)], orders)
-    lower, back = lax.optimization_barrier((lower, back))
+    first = term(image, [after(first_rows, centre)], [(width, orders)])
+    first, other, back = lax.optimization_barrier((first, other, back))
+    second_rows = either(other[1], other[0]), either(other[0], other[1])
     centre = add(centre[1], back)
-    back = exchange(lower[0], *core)
-    upper = term([after(above, lower, centre)], orders)
-    upper, back = lax.optimization_barrier((upper, back))
-    upper_back = exchange(upper[0], *core)
-    others = [after(own_alive.reshape(1), upper[0])]
-    for away in range(1, member_count):
-        others.append(exchange(others[0], "dp", away))
-    lower = add(lower[1], back)
-    upper_back, others = lax.optimization_barrier((upper_back, others))
-    upper = add(upper[1], upper_back)
-    survivors = sum(others)
-    scale = (own_alive / survivors).reshape(1)
-
-    width = 3 * out_channels
+    back = exchange(first[0], *core)
+    second = term(image, [after(second_rows, first, centre)], [(width, orders)])
+    second, back = lax.optimization_barrier((second, back))
+    ring = [None, add(second[1], back)]
+    below = [either(*rows) for rows in zip(first_rows, second_rows)]
+    above = [either(*rows) for rows in zip(second_rows, first_rows)]
+    back, scale, below, above = lax.optimization_barrier(
+        (exchange(second[0], *core), scale, below, above)
+    )
+    ring[0] = add(first[1], back)
+
     blocks = in_channels // CHANNELS_PER_STEP
+    early = blocks * 6 // 8
     last = len(centre_order) - 1
     rows_of = [below, [in_hbm(flat(tile))], above]
     grad_features = None
     for step, name in enumerate(centre_order):
-        ring_sent = [sent(lower), sent(upper)]
+        ring_sent = jnp.concatenate([sent(part) for part in ring], axis=-1)
+        ring_back = exchange_by_role(ring_sent, orders, step)
+        if step:
+            centre = add(kept(centre), after(centre_back, ring_sent))
         centre_sent = sent(centre)
-        if step < last:
-            ring_sent = jnp.concatenate(ring_sent, axis=-1)
-            centre_back = exchange(centre_sent, *name)
-            ring_back = exchange_by_role(ring_sent, orders, step)
-        else:
-            ring_back = exchange(jnp.concatenate([*ring_sent, centre_sent], axis=-1), *name)
-            centre_back = ring_back[..., 2 * width :]
-        if step == 0:
+        centre_back = exchange(centre_sent, *name)
+        if step in (0, last):
             grad_features = input_grad(
-                columns, scale, after(rows_of, ring_sent, centre_sent), weight, 0, blocks
+                columns,
+                scale,
+                after(rows_of, ring_sent, centre_sent),
+                weight,
+                early if step else 0,
+                blocks - early if step else early,
+                grad_features,
             )
-        ring_back, centre_back, grad_features = lax.optimization_barrier(
-            (ring_back, centre_back, grad_features)
-        )
-        lower = add(kept(lower), ring_back[..., :width])
-        upper = add(kept(upper), ring_back[..., width : 2 * width])
-        centre = add(kept(centre), centre_back)
-    final = jnp.concatenate([lower[0], centre[0], upper[0]], axis=-1)
+            ring_back, grad_features = lax.optimization_barrier((ring_back, grad_features))
+        ring = [
+            add(kept(part), ring_back[..., width * i : width * (i + 1)])
+            for i, part in enumerate(ring)
+        ]
+    centre = add(kept(centre), centre_back)
+    first, second = (part[0] for part in ring)
+    final = jnp.concatenate([either(first, second), centre[0], either(second, first)], axis=-1)
     final = final * (member_count * 0.25 / survivors)
     return (final.reshape(-1, out_channels), grad_features.reshape(features.shape))
 

time: 101 us -> 96.3 us (0.953)
  starting transfers between devices: 31 us -> 27.4 us
  local copies, waits for them, and re-layouts: 3.61 us -> 0.89 us
  waiting for transfers between devices: 26.8 us -> 24.4 us
  Pallas kernels: 30.6 us -> 33 us
  other arithmetic: 5.31 us -> 6.74 us
    ppermute x10 -> x12, waiting for transfers between devices: 26.8 us -> 3.2 us  [exchange(): lax.ppermute(value, axis, [(i, i ^ bit) for i in range(lax.axis_size(axis...]
    ppermute x3 -> x4, waiting for transfers between devices: 0.01 us -> 21.1 us  [exchange_by_role(): return lax.ppermute(value, ('dp', 'space'), pairs)]
    ppermute x4 -> x2, starting transfers between devices: 12 us -> 2.58 us  [fetched(): return lax.ppermute(value, ('dp', 'space'), pairs)]
    ppermute x10 -> x12, starting transfers between devices: 14.9 us -> 19.7 us  [exchange(): lax.ppermute(value, axis, [(i, i ^ bit) for i in range(lax.axis_size(axis...]
    pallas_call x1 -> x2, Pallas kernels: 15.3 us -> 18.3 us  [input_grad(): pl.pallas_call(functools.partial(input_grad_kernel, columns, cuts), grid=...]
    unnamed x2 -> x0, local copies, waits for them, and re-layouts: 1.62 us -> none
    select_n x0 -> x5, other arithmetic: none -> 1.3 us  [either(): return jnp.where(lax.axis_index('dp') % 2 == 0, first, second)]
    slice x2 -> x0, local copies, waits for them, and re-layouts: 1.09 us -> none  [the longest x1 1.07 us: far_rows(): below = from_behind(tile[:rest], 'space', -away - 1)]
  transfers between devices with their start and end apart: 17 -> 18, of which waited for: 4 -> 7; matrix products, arithmetic and copies ran while one was open for 3% -> 6% of each run, Pallas kernels for 30% -> 34%
where the time goes in v4:
time: 96.3 us; the launch traced here: 96 us
  Pallas kernels  33 us (34%)
  starting transfers between devices  27.4 us (28%)
  waiting for transfers between devices  24.4 us (25%)
  other arithmetic  6.74 us (7%)
  between operations  3.64 us (4%)
    ppermute x4, waiting for transfers between devices, exchange_by_role(): return lax.ppermute(value, ('dp', 'space'), pairs)  21.1 us
    ppermute x12, starting transfers between devices, exchange(): lax.ppermute(value, axis, [(i, i ^ bit) for i in range(lax.axis_size(axis...  19.7 us
    pallas_call x2, Pallas kernels, input_grad(): pl.pallas_call(functools.partial(input_grad_kernel, columns, cuts), grid=...  18.3 us
    pallas_call x3, Pallas kernels, kernel_term(): pl.pallas_call(functools.partial(kernel_term_kernel, columns, cuts, strea...  14.6 us
    ppermute x4, starting transfers between devices, exchange_by_role(): return lax.ppermute(value, ('dp', 'space'), pairs)  5.11 us
    ppermute x12, waiting for transfers between devices, exchange(): lax.ppermute(value, axis, [(i, i ^ bit) for i in range(lax.axis_size(axis...  3.2 us
    ppermute x2, starting transfers between devices, fetched(): return lax.ppermute(value, ('dp', 'space'), pairs)  2.58 us
    add x9, other arithmetic, add(): return part.astype(F32) + back.astype(F32)  2.41 us
  transfers between devices with their start and end apart: 18, of which 7 were waited for; matrix products, arithmetic and copies ran while one was open for 6% of the time, Pallas kernels for 34%

profile of v4, /device:TPU:0, one launch (start us, length us, event | category | flops | bytes accessed | tf_op | source)
XLA Modules:
  0.0 96.0 jit_solution(10064695410630931617)
XLA Ops:
  1.1 1.1 %broadcast_select_fusion.4 = (bf16[1,6,72,256]{3,2,1,0:T(8,128)(2,1)S(1)}, bf16[1,6,72,256]{3,2,1,0:T(8,128)(2,1)S(1)}) fusion(pred[]{:T(512)S(6)} %eq.31, bf16[1,12,72,256]{3,2,1,0:T(8,128)(2,1)} %param.5), kind=kLoop, calls=%fused_computation.38 | loop fusion | flops 221184 | bytes 884737 | tf_op jit(solution)/shard_map/jit(_where)/select_n | solution.py:26
  2.9 1.3 %collective-permute-start.1 = (bf16[2,6,72,256]{3,2,1,0:T(8,128)(2,1)S(1)}, bf16[2,6,72,256]{3,2,1,0:T(8,128)(2,1)S(1)}, u32[]{:S(2)}, u32[]{:S(2)}) collective-permute-start(bf16[2,6,72,256]{3,2,1,0:T(8,128)(2,1)S(1)} %pad_maximum_fusion.2), channel_id=1, source_target_pairs={{1,0},{2,1},{3,2},{4,3},{5,4},{6,5},{7,6},{8,9},{9,10},{10,11},{11... | collective-permute-start | bytes 1327112 | tf_op jit(solution)/shard_map/ppermute | solution.py:41
  4.2 1.3 %collective-permute-start.2 = (bf16[2,6,72,256]{3,2,1,0:T(8,128)(2,1)S(1)}, bf16[2,6,72,256]{3,2,1,0:T(8,128)(2,1)S(1)}, u32[]{:S(2)}, u32[]{:S(2)}) collective-permute-start(bf16[2,6,72,256]{3,2,1,0:T(8,128)(2,1)S(1)} %pad_maximum_fusion.3), channel_id=1, source_target_pairs={{2,0},{3,1},{4,2},{5,3},{6,4},{7,5},{8,10},{9,11},{10,12},{11,13},... | collective-permute-start | bytes 1327112 | tf_op jit(solution)/shard_map/ppermute | solution.py:41
  6.2 7.8 %collective-permute-start.5 = (f32[1]{0:T(128)}, f32[1]{0:T(128)}, u32[]{:S(2)}, u32[]{:S(2)}) collective-permute-start(f32[1]{0:T(128)} %convert_element_type.88.scale_ref), channel_id=1, source_target_pairs={{0,24},{8,16},{16,8},{24,0},{1,25},{9,17},{17,9},{25,1},{2,26},{10... | collective-permute-start | bytes 20 | tf_op jit(solution)/shard_map/ppermute | solution.py:22
  13.9 1.8 %collective-permute-start.4 = (f32[1]{0:T(128)}, f32[1]{0:T(128)}, u32[]{:S(2)}, u32[]{:S(2)}) collective-permute-start(f32[1]{0:T(128)} %convert_element_type.88.scale_ref), channel_id=1, source_target_pairs={{0,16},{8,24},{16,0},{24,8},{1,17},{9,25},{17,1},{25,9},{2,18},{10... | collective-permute-start | bytes 20 | tf_op jit(solution)/shard_map/ppermute | solution.py:22
  15.8 1.0 collective-permute-start.3
  16.8 5.9 %kernel_term.3 = (bf16[2,2,512,864]{3,2,1,0:T(8,128)(2,1)S(1)}, f32[16,64,768]{2,1,0:T(8,128)S(1)}, f32[16,64,768]{2,1,0:T(8,128)S(1)}) custom-call(s32[2]{0:T(128)S(1)} %pad_add_fusion.place_ref, f32[1]{0:T(128)} %convert_element_type.88.scale_ref, bf16[864,2048]{1,0:T(8,128)(2,1)} %bitcast.56, bf16[864,2048]{1,0:T(8,128)(2,1)} %bitcast.57, ...), custom_call_target="tpu_custom_call" | custom-call | flops 2717908992 | bytes 9830400 | tf_op jit(solution)/shard_map/kernel_term/pallas_call | solution.py:139
  24.0 4.3 %kernel_term.4 = (f32[16,64,768]{2,1,0:T(8,128)S(1)}, f32[16,64,768]{2,1,0:T(8,128)S(1)}) custom-call(s32[2]{0:T(128)S(1)} %pad_add_fusion.place_ref, f32[1]{0:T(128)} %convert_element_type.88.scale_ref, bf16[2,2,512,864]{3,2,1,0:T(8,128)(2,1)S(1)} %get-tuple-element.51.refs_0_, bf16[432,256]{1,0:T(8,128)(2,1)S(1)} %bitcast.40, bf16[432,256]{1,0:T(8,128)(2,1)S(1)} %bitcast.39), custom_call_target="tpu_custom_call" | custom-call | flops 2717908992 | bytes 9830400 | tf_op jit(solution)/shard_map/kernel_term/pallas_call | solution.py:139
  29.9 4.5 %kernel_term.5 = (f32[16,64,768]{2,1,0:T(8,128)S(1)}, f32[16,64,768]{2,1,0:T(8,128)S(1)}) custom-call(s32[2]{0:T(128)S(1)} %pad_add_fusion.place_ref, f32[1]{0:T(128)} %convert_element_type.88.scale_ref, bf16[2,2,512,864]{3,2,1,0:T(8,128)(2,1)S(1)} %get-tuple-element.51.refs_0_, bf16[432,256]{1,0:T(8,128)(2,1)S(1)} %bitcast.50, bf16[432,256]{1,0:T(8,128)(2,1)S(1)} %bitcast.49), custom_call_target="tpu_custom_call" | custom-call | flops 2717908992 | bytes 9830400 | tf_op jit(solution)/shard_map/kernel_term/pallas_call | solution.py:139
  39.4 1.5 %collective-permute-start.10 = (f16[8,64,1536]{2,1,0:T(8,128)(2,1)S(1)}, f16[8,64,1536]{2,1,0:T(8,128)(2,1)S(1)}, u32[]{:S(2)}, u32[]{:S(2)}) collective-permute-start(f16[8,64,1536]{2,1,0:T(8,128)(2,1)S(1)} %pad_maximum_fusion), channel_id=1, source_target_pairs={{0,16},{1,17},{2,18},{3,19},{4,20},{5,21},{6,22},{7,23},{8,9},{9,8... | collective-permute-start | bytes 4718600 | tf_op jit(solution)/shard_map/ppermute | solution.py:240
  41.0 1.6 %collective-permute-start.14 = (f16[8,64,768]{2,1,0:T(8,128)(2,1)S(1)}, f16[8,64,768]{2,1,0:T(8,128)(2,1)S(1)}, u32[]{:S(2)}, u32[]{:S(2)}) collective-permute-start(f16[8,64,768]{2,1,0:T(8,128)(2,1)S(1)} %slice_convert_fusion), channel_id=1, source_target_pairs={{0,2},{1,3},{2,0},{3,1},{4,6},{5,7},{6,4},{7,5},{8,10},{9,11},{10,... | collective-permute-start | bytes 2359304 | tf_op jit(solution)/shard_map/ppermute | solution.py:22
  42.6 12.2 %input_grad.2.refs_6_ = bf16[864,2048]{1,0:T(8,128)(2,1)} custom-call(f32[1]{0:T(128)S(6)} %div.7.scale_ref, bf16[432,256]{1,0:T(8,128)(2,1)S(1)} %bitcast.47, bf16[432,256]{1,0:T(8,128)(2,1)S(1)} %bitcast.45, bf16[864,256]{1,0:T(8,128)(2,1)} %bitcast.54, bf16[432,256]{1,0:T(8,128)(2,1)S(1)} %bitcast.43, bf16[432,256]{1,0:T(8,128)(2,1)S(1)} %bitcast.41, ...), custom_call_target="tpu_custom_call" | custom-call | flops 6115295232 | bytes 9732096 | tf_op jit(solution)/shard_map/input_grad/pallas_call | solution.py:197
  54.9 5.0 %collective-permute-done.10 = f16[8,64,1536]{2,1,0:T(8,128)(2,1)S(1)} collective-permute-done((f16[8,64,1536]{2,1,0:T(8,128)(2,1)S(1)}, f16[8,64,1536]{2,1,0:T(8,128)(2,1)S(1)}, u32[]{:S(2)}, u32[]{:S(2)}) %collective-permute-start.10) | collective-permute-done | bytes 1572896 | tf_op jit(solution)/shard_map/ppermute | solution.py:240
  60.5 1.6 %collective-permute-start.11 = (f16[4,64,1536]{2,1,0:T(8,128)(2,1)S(1)}, f16[4,64,1536]{2,1,0:T(8,128)(2,1)S(1)}, u32[]{:S(2)}, u32[]{:S(2)}) collective-permute-start(f16[4,64,1536]{2,1,0:T(8,128)(2,1)S(1)} %pad_maximum_fusion.1), channel_id=1, source_target_pairs={{0,1},{1,0},{2,3},{3,2},{4,5},{5,4},{6,7},{7,6},{8,10},{9,11},{10,... | collective-permute-start | bytes 2359304 | tf_op jit(solution)/shard_map/ppermute | solution.py:240
  62.4 1.5 %collective-permute-start.15 = (f16[4,64,768]{2,1,0:T(8,128)(2,1)S(1)}, f16[4,64,768]{2,1,0:T(8,128)(2,1)S(1)}, u32[]{:S(2)}, u32[]{:S(2)}) collective-permute-start(f16[4,64,768]{2,1,0:T(8,128)(2,1)S(1)} %slice_convert_fusion.3), channel_id=1, source_target_pairs={{0,16},{8,24},{16,0},{24,8},{1,17},{9,25},{17,1},{25,9},{2,18},{10... | collective-permute-start | bytes 1179656 | tf_op jit(solution)/shard_map/ppermute | solution.py:22
  64.0 8.6 %collective-permute-done.11 = f16[4,64,1536]{2,1,0:T(8,128)(2,1)S(1)} collective-permute-done((f16[4,64,1536]{2,1,0:T(8,128)(2,1)S(1)}, f16[4,64,1536]{2,1,0:T(8,128)(2,1)S(1)}, u32[]{:S(2)}, u32[]{:S(2)}) %collective-permute-start.11) | collective-permute-done | bytes 786464 | tf_op jit(solution)/shard_map/ppermute | solution.py:240
  73.0 1.6 %collective-permute-start.12 = (f16[2,64,1536]{2,1,0:T(8,128)(2,1)S(1)}, f16[2,64,1536]{2,1,0:T(8,128)(2,1)S(1)}, u32[]{:S(2)}, u32[]{:S(2)}) collective-permute-start(f16[2,64,1536]{2,1,0:T(8,128)(2,1)S(1)} %pad_maximum_fusion.5), channel_id=1, source_target_pairs={{0,2},{1,3},{2,0},{3,1},{4,6},{5,7},{6,4},{7,5},{8,24},{9,25},{10,... | collective-permute-start | bytes 1179656 | tf_op jit(solution)/shard_map/ppermute | solution.py:240
  74.8 1.6 %collective-permute-start.16 = (f16[2,64,768]{2,1,0:T(8,128)(2,1)S(1)}, f16[2,64,768]{2,1,0:T(8,128)(2,1)S(1)}, u32[]{:S(2)}, u32[]{:S(2)}) collective-permute-start(f16[2,64,768]{2,1,0:T(8,128)(2,1)S(1)} %slice_convert_fusion.6), channel_id=1, source_target_pairs={{0,1},{1,0},{2,3},{3,2},{4,5},{5,4},{6,7},{7,6},{8,9},{9,8},{10,11... | collective-permute-start | bytes 589832 | tf_op jit(solution)/shard_map/ppermute | solution.py:22
  76.3 4.5 %collective-permute-done.12 = f16[2,64,1536]{2,1,0:T(8,128)(2,1)S(1)} collective-permute-done((f16[2,64,1536]{2,1,0:T(8,128)(2,1)S(1)}, f16[2,64,1536]{2,1,0:T(8,128)(2,1)S(1)}, u32[]{:S(2)}, u32[]{:S(2)}) %collective-permute-start.12) | collective-permute-done | bytes 393248 | tf_op jit(solution)/shard_map/ppermute | solution.py:240
  81.1 2.6 %collective-permute-start.17 = (f16[1,64,768]{2,1,0:T(8,128)(2,1)S(1)}, f16[1,64,768]{2,1,0:T(8,128)(2,1)S(1)}, u32[]{:S(2)}, u32[]{:S(2)}) collective-permute-start(f16[1,64,768]{2,1,0:T(8,128)(2,1)S(1)} %slice_convert_fusion.9), channel_id=1, source_target_pairs={{0,4},{1,5},{2,6},{3,7},{4,0},{5,1},{6,2},{7,3},{8,12},{9,13},{10,... | collective-permute-start | bytes 294920 | tf_op jit(solution)/shard_map/ppermute | solution.py:22
  84.1 6.1 %input_grad.3 = bf16[864,2048]{1,0:T(8,128)(2,1)} custom-call(f32[1]{0:T(128)S(6)} %div.7.scale_ref, bf16[432,256]{1,0:T(8,128)(2,1)S(1)} %bitcast.48, bf16[432,256]{1,0:T(8,128)(2,1)S(1)} %bitcast.46, bf16[864,256]{1,0:T(8,128)(2,1)} %bitcast.55, bf16[432,256]{1,0:T(8,128)(2,1)S(1)} %bitcast.44, ...), custom_call_target="tpu_custom_call", output_to_operand_aliasing={{}: (7, {})} | custom-call | flops 2038431744 | bytes 3244032 | tf_op jit(solution)/shard_map/input_grad/pallas_call | solution.py:197
  90.2 1.8 %collective-permute-done.17 = f16[1,64,768]{2,1,0:T(8,128)(2,1)S(1)} collective-permute-done((f16[1,64,768]{2,1,0:T(8,128)(2,1)S(1)}, f16[1,64,768]{2,1,0:T(8,128)(2,1)S(1)}, u32[]{:S(2)}, u32[]{:S(2)}) %collective-permute-start.17) | collective-permute-done | bytes 98336 | tf_op jit(solution)/shard_map/ppermute | solution.py:22
  92.0 3.1 %collective-permute-done.13 = f16[1,64,1536]{2,1,0:T(8,128)(2,1)S(1)} collective-permute-done((f16[1,64,1536]{2,1,0:T(8,128)(2,1)S(1)}, f16[1,64,1536]{2,1,0:T(8,128)(2,1)S(1)}, u32[]{:S(2)}, u32[]{:S(2)}) %collective-permute-start.13) | collective-permute-done | bytes 196640 | tf_op jit(solution)/shard_map/ppermute | solution.py:240
  95.1 0.9 mul.17
  (61 shorter events, 9.3 us)
Async XLA Ops:
  0.6 2.1 %collective-permute-start = (bf16[12,72,256]{2,1,0:T(8,128)(2,1)}, bf16[12,72,256]{2,1,0:T(8,128)(2,1)S(1)}, u32[]{:S(2)}, u32[]{:S(2)}) collective-permute-start(bf16[12,72,256]{2,1,0:T(8,128)(2,1)} %bitcast.52), channel_id=1, source_target_pairs={{0,8},{8,0},{16,24},{24,16},{1,9},{9,1},{17,25},{25,17},{2,10},{10... | collective-permute-start | bytes 1327112 | tf_op jit(solution)/shard_map/ppermute | solution.py:22
  2.9 20.3 %collective-permute-start.1 = (bf16[2,6,72,256]{3,2,1,0:T(8,128)(2,1)S(1)}, bf16[2,6,72,256]{3,2,1,0:T(8,128)(2,1)S(1)}, u32[]{:S(2)}, u32[]{:S(2)}) collective-permute-start(bf16[2,6,72,256]{3,2,1,0:T(8,128)(2,1)S(1)} %pad_maximum_fusion.2), channel_id=1, source_target_pairs={{1,0},{2,1},{3,2},{4,3},{5,4},{6,5},{7,6},{8,9},{9,10},{10,11},{11... | collective-permute-start | bytes 1327112 | tf_op jit(solution)/shard_map/ppermute | solution.py:41
  4.2 19.0 %collective-permute-start.2 = (bf16[2,6,72,256]{3,2,1,0:T(8,128)(2,1)S(1)}, bf16[2,6,72,256]{3,2,1,0:T(8,128)(2,1)S(1)}, u32[]{:S(2)}, u32[]{:S(2)}) collective-permute-start(bf16[2,6,72,256]{3,2,1,0:T(8,128)(2,1)S(1)} %pad_maximum_fusion.3), channel_id=1, source_target_pairs={{2,0},{3,1},{4,2},{5,3},{6,4},{7,5},{8,10},{9,11},{10,12},{11,13},... | collective-permute-start | bytes 1327112 | tf_op jit(solution)/shard_map/ppermute | solution.py:41
  6.2 17.0 %collective-permute-start.5 = (f32[1]{0:T(128)}, f32[1]{0:T(128)}, u32[]{:S(2)}, u32[]{:S(2)}) collective-permute-start(f32[1]{0:T(128)} %convert_element_type.88.scale_ref), channel_id=1, source_target_pairs={{0,24},{8,16},{16,8},{24,0},{1,25},{9,17},{17,9},{25,1},{2,26},{10... | collective-permute-start | bytes 20 | tf_op jit(solution)/shard_map/ppermute | solution.py:22
  13.9 9.3 %collective-permute-start.4 = (f32[1]{0:T(128)}, f32[1]{0:T(128)}, u32[]{:S(2)}, u32[]{:S(2)}) collective-permute-start(f32[1]{0:T(128)} %convert_element_type.88.scale_ref), channel_id=1, source_target_pairs={{0,16},{8,24},{16,0},{24,8},{1,17},{9,25},{17,1},{25,9},{2,18},{10... | collective-permute-start | bytes 20 | tf_op jit(solution)/shard_map/ppermute | solution.py:22
  15.8 7.4 %collective-permute-start.3 = (f32[1]{0:T(128)}, f32[1]{0:T(128)}, u32[]{:S(2)}, u32[]{:S(2)}) collective-permute-start(f32[1]{0:T(128)} %convert_element_type.88.scale_ref), channel_id=1, source_target_pairs={{0,8},{8,0},{16,24},{24,16},{1,9},{9,1},{17,25},{25,17},{2,10},{10... | collective-permute-start | bytes 20 | tf_op jit(solution)/shard_map/ppermute | solution.py:22
  23.2 5.6 %collective-permute-start.7 = (f16[16,64,768]{2,1,0:T(8,128)(2,1)S(1)}, f16[16,64,768]{2,1,0:T(8,128)(2,1)S(1)}, u32[]{:S(2)}, u32[]{:S(2)}) collective-permute-start(f16[16,64,768]{2,1,0:T(8,128)(2,1)S(1)} %convert_element_type.89), channel_id=1, source_target_pairs={{0,8},{8,0},{16,24},{24,16},{1,9},{9,1},{17,25},{25,17},{2,10},{10... | collective-permute-start | bytes 4718600 | tf_op jit(solution)/shard_map/ppermute | solution.py:22
  23.9 4.9 %collective-permute-start.6 = (bf16[2,6,72,256]{3,2,1,0:T(8,128)(2,1)S(1)}, bf16[2,6,72,256]{3,2,1,0:T(8,128)(2,1)S(1)}, u32[]{:S(2)}, u32[]{:S(2)}) collective-permute-start(bf16[2,6,72,256]{3,2,1,0:T(8,128)(2,1)S(1)} %pad_maximum_fusion.4), channel_id=1, source_target_pairs={{0,8},{8,0},{16,24},{24,16},{1,9},{9,1},{17,25},{25,17},{2,10},{10... | collective-permute-start | bytes 1327112 | tf_op jit(solution)/shard_map/ppermute | solution.py:22
  28.8 6.1 %collective-permute-start.8 = (f16[16,64,768]{2,1,0:T(8,128)(2,1)S(1)}, f16[16,64,768]{2,1,0:T(8,128)(2,1)S(1)}, u32[]{:S(2)}, u32[]{:S(2)}) collective-permute-start(f16[16,64,768]{2,1,0:T(8,128)(2,1)S(1)} %convert_element_type.91), channel_id=1, source_target_pairs={{0,8},{8,0},{16,24},{24,16},{1,9},{9,1},{17,25},{25,17},{2,10},{10... | collective-permute-start | bytes 4718600 | tf_op jit(solution)/shard_map/ppermute | solution.py:22
  34.9 3.5 %collective-permute-start.9 = (f16[16,64,768]{2,1,0:T(8,128)(2,1)S(1)}, f16[16,64,768]{2,1,0:T(8,128)(2,1)S(1)}, u32[]{:S(2)}, u32[]{:S(2)}) collective-permute-start(f16[16,64,768]{2,1,0:T(8,128)(2,1)S(1)} %convert_element_type.96), channel_id=1, source_target_pairs={{0,8},{8,0},{16,24},{24,16},{1,9},{9,1},{17,25},{25,17},{2,10},{10... | collective-permute-start | bytes 4718600 | tf_op jit(solution)/shard_map/ppermute | solution.py:22
  39.4 20.5 %collective-permute-start.10 = (f16[8,64,1536]{2,1,0:T(8,128)(2,1)S(1)}, f16[8,64,1536]{2,1,0:T(8,128)(2,1)S(1)}, u32[]{:S(2)}, u32[]{:S(2)}) collective-permute-start(f16[8,64,1536]{2,1,0:T(8,128)(2,1)S(1)} %pad_maximum_fusion), channel_id=1, source_target_pairs={{0,16},{1,17},{2,18},{3,19},{4,20},{5,21},{6,22},{7,23},{8,9},{9,8... | collective-permute-start | bytes 4718600 | tf_op jit(solution)/shard_map/ppermute | solution.py:240
  41.0 21.2 %collective-permute-start.14 = (f16[8,64,768]{2,1,0:T(8,128)(2,1)S(1)}, f16[8,64,768]{2,1,0:T(8,128)(2,1)S(1)}, u32[]{:S(2)}, u32[]{:S(2)}) collective-permute-start(f16[8,64,768]{2,1,0:T(8,128)(2,1)S(1)} %slice_convert_fusion), channel_id=1, source_target_pairs={{0,2},{1,3},{2,0},{3,1},{4,6},{5,7},{6,4},{7,5},{8,10},{9,11},{10,... | collective-permute-start | bytes 2359304 | tf_op jit(solution)/shard_map/ppermute | solution.py:22
  60.5 12.1 %collective-permute-start.11 = (f16[4,64,1536]{2,1,0:T(8,128)(2,1)S(1)}, f16[4,64,1536]{2,1,0:T(8,128)(2,1)S(1)}, u32[]{:S(2)}, u32[]{:S(2)}) collective-permute-start(f16[4,64,1536]{2,1,0:T(8,128)(2,1)S(1)} %pad_maximum_fusion.1), channel_id=1, source_target_pairs={{0,1},{1,0},{2,3},{3,2},{4,5},{5,4},{6,7},{7,6},{8,10},{9,11},{10,... | collective-permute-start | bytes 2359304 | tf_op jit(solution)/shard_map/ppermute | solution.py:240
  62.4 12.2 %collective-permute-start.15 = (f16[4,64,768]{2,1,0:T(8,128)(2,1)S(1)}, f16[4,64,768]{2,1,0:T(8,128)(2,1)S(1)}, u32[]{:S(2)}, u32[]{:S(2)}) collective-permute-start(f16[4,64,768]{2,1,0:T(8,128)(2,1)S(1)} %slice_convert_fusion.3), channel_id=1, source_target_pairs={{0,16},{8,24},{16,0},{24,8},{1,17},{9,25},{17,1},{25,9},{2,18},{10... | collective-permute-start | bytes 1179656 | tf_op jit(solution)/shard_map/ppermute | solution.py:22
  73.0 7.8 %collective-permute-start.12 = (f16[2,64,1536]{2,1,0:T(8,128)(2,1)S(1)}, f16[2,64,1536]{2,1,0:T(8,128)(2,1)S(1)}, u32[]{:S(2)}, u32[]{:S(2)}) collective-permute-start(f16[2,64,1536]{2,1,0:T(8,128)(2,1)S(1)} %pad_maximum_fusion.5), channel_id=1, source_target_pairs={{0,2},{1,3},{2,0},{3,1},{4,6},{5,7},{6,4},{7,5},{8,24},{9,25},{10,... | collective-permute-start | bytes 1179656 | tf_op jit(solution)/shard_map/ppermute | solution.py:240
  74.8 6.3 %collective-permute-start.16 = (f16[2,64,768]{2,1,0:T(8,128)(2,1)S(1)}, f16[2,64,768]{2,1,0:T(8,128)(2,1)S(1)}, u32[]{:S(2)}, u32[]{:S(2)}) collective-permute-start(f16[2,64,768]{2,1,0:T(8,128)(2,1)S(1)} %slice_convert_fusion.6), channel_id=1, source_target_pairs={{0,1},{1,0},{2,3},{3,2},{4,5},{5,4},{6,7},{7,6},{8,9},{9,8},{10,11... | collective-permute-start | bytes 589832 | tf_op jit(solution)/shard_map/ppermute | solution.py:22
  81.1 10.9 %collective-permute-start.17 = (f16[1,64,768]{2,1,0:T(8,128)(2,1)S(1)}, f16[1,64,768]{2,1,0:T(8,128)(2,1)S(1)}, u32[]{:S(2)}, u32[]{:S(2)}) collective-permute-start(f16[1,64,768]{2,1,0:T(8,128)(2,1)S(1)} %slice_convert_fusion.9), channel_id=1, source_target_pairs={{0,4},{1,5},{2,6},{3,7},{4,0},{5,1},{6,2},{7,3},{8,12},{9,13},{10,... | collective-permute-start | bytes 294920 | tf_op jit(solution)/shard_map/ppermute | solution.py:22
  83.7 11.3 %collective-permute-start.13 = (f16[1,64,1536]{2,1,0:T(8,128)(2,1)S(1)}, f16[1,64,1536]{2,1,0:T(8,128)(2,1)S(1)}, u32[]{:S(2)}, u32[]{:S(2)}) collective-permute-start(f16[1,64,1536]{2,1,0:T(8,128)(2,1)S(1)} %pad_maximum_fusion.6), channel_id=1, source_target_pairs={{0,4},{1,5},{2,6},{3,7},{4,0},{5,1},{6,2},{7,3},{8,12},{9,13},{10,... | collective-permute-start | bytes 589832 | tf_op jit(solution)/shard_map/ppermute | solution.py:240

commit v5 on v4

--- a/solution.py
+++ b/solution.py
@@ -288,8 +288,6 @@
     for away in range(1, member_count):
         alive_all.append(exchange(alive_all[0], "dp", away))
     near, far, centre, alive_all = lax.optimization_barrier((near, far, centre, alive_all))
-    survivors = sum(alive_all)
-    scale = own_alive / survivors
 
     first_rows = either(near[0], far[0]), either(far[0], near[0])
     other = exchange(jnp.stack([near[1], far[1]]), *core)
@@ -304,41 +302,44 @@
     ring = [None, add(second[1], back)]
     below = [either(*rows) for rows in zip(first_rows, second_rows)]
     above = [either(*rows) for rows in zip(second_rows, first_rows)]
-    back, scale, below, above = lax.optimization_barrier(
-        (exchange(second[0], *core), scale, below, above)
-    )
+    back, below, above = lax.optimization_barrier((exchange(second[0], *core), below, above))
     ring[0] = add(first[1], back)
 
     blocks = in_channels // CHANNELS_PER_STEP
-    early = blocks * 6 // 8
+    early = blocks * 4 // 8
     last = len(centre_order) - 1
     rows_of = [below, [in_hbm(flat(tile))], above]
-    grad_features = None
-    for step, name in enumerate(centre_order):
-        ring_sent = jnp.concatenate([sent(part) for part in ring], axis=-1)
-        ring_back = exchange_by_role(ring_sent, orders, step)
-        if step:
-            centre = add(kept(centre), after(centre_back, ring_sent))
-        centre_sent = sent(centre)
-        centre_back = exchange(centre_sent, *name)
-        if step in (0, last):
+    chains = [[ring[1], orders, None], [centre, (centre_order, centre_order), None], [ring[0], orders, None]]
+    grad_features = token = None
+    for step in range(last):
+        operands = []
+        for chain in chains if step == 0 else [chains[i] for i in (0,1,2)]:
+            part, order, back = chain
+            if step:
+                part = add(kept(part), after(back, token))
+            token = sent(part)
+            operands.append(token)
+            chain[0], chain[2] = part, exchange_by_role(token, order, step)
+        if step == 0:
+            survivors = sum(after(alive_all, *operands))
+            scale = own_alive / survivors
             grad_features = input_grad(
-                columns,
-                scale,
-                after(rows_of, ring_sent, centre_sent),
-                weight,
-                early if step else 0,
-                blocks - early if step else early,
-                grad_features,
+                columns, scale, after(rows_of, *operands), weight, 0, early, grad_features
             )
-            ring_back, grad_features = lax.optimization_barrier((ring_back, grad_features))
-        ring = [
-            add(kept(part), ring_back[..., width * i : width * (i + 1)])
-            for i, part in enumerate(ring)
-        ]
-    centre = add(kept(centre), centre_back)
-    first, second = (part[0] for part in ring)
-    final = jnp.concatenate([either(first, second), centre[0], either(second, first)], axis=-1)
+            token = grad_features
+    parts = []
+    for part, order, back in chains:
+        parts.append(add(kept(part), after(back, token)))
+        token = sent(parts[-1])
+    operands = jnp.concatenate([sent(part) for part in parts], axis=-1)
+    back = exchange(operands, *centre_order[last])
+    grad_features = input_grad(
+        columns, scale, after(rows_of, operands), weight, early, blocks - early, grad_features
+    )
+    back, grad_features = lax.optimization_barrier((back, grad_features))
+    parts = [add(kept(part), back[..., width * i : width * (i + 1)]) for i, part in enumerate(parts)]
+    second, centre, first = (part[0] for part in parts)
+    final = jnp.concatenate([either(first, second), centre, either(second, first)], axis=-1)
     final = final * (member_count * 0.25 / survivors)
     return (final.reshape(-1, out_channels), grad_features.reshape(features.shape))
 

time: 96.3 us -> 90.8 us (0.943)
  waiting for transfers between devices: 24.4 us -> 16.7 us
  starting transfers between devices: 27.4 us -> 30.2 us
    ppermute x4 -> x9, starting transfers between devices: 5.11 us -> 11.2 us  [exchange_by_role(): return lax.ppermute(value, ('dp', 'space'), pairs)]
    ppermute x4 -> x9, waiting for transfers between devices: 21.1 us -> 16.1 us  [exchange_by_role(): return lax.ppermute(value, ('dp', 'space'), pairs)]
    ppermute x12 -> x9, starting transfers between devices: 19.7 us -> 16.4 us  [exchange(): lax.ppermute(value, axis, [(i, i ^ bit) for i in range(lax.axis_size(axis...]
    ppermute x12 -> x9, waiting for transfers between devices: 3.2 us -> 0.57 us  [exchange(): lax.ppermute(value, axis, [(i, i ^ bit) for i in range(lax.axis_size(axis...]
    add x9 -> x12, other arithmetic: 2.41 us -> 2.33 us  [add(): return part.astype(F32) + back.astype(F32)]
  transfers between devices with their start and end apart: 18 -> 20, of which waited for: 7 -> 5; matrix products, arithmetic and copies ran while one was open for 6% -> 6% of each run, Pallas kernels for 34% -> 36%
where the time goes in v5:
time: 90.8 us; the launch traced here: 90.5 us
  Pallas kernels  33 us (36%)
  starting transfers between devices  30.2 us (33%)
  waiting for transfers between devices  16.7 us (18%)
  other arithmetic  6.1 us (7%)
  between operations  3.61 us (4%)
    pallas_call x2, Pallas kernels, input_grad(): pl.pallas_call(functools.partial(input_grad_kernel, columns, cuts), grid=...  18.4 us
    ppermute x9, starting transfers between devices, exchange(): lax.ppermute(value, axis, [(i, i ^ bit) for i in range(lax.axis_size(axis...  16.4 us
    ppermute x9, waiting for transfers between devices, exchange_by_role(): return lax.ppermute(value, ('dp', 'space'), pairs)  16.1 us
    pallas_call x3, Pallas kernels, kernel_term(): pl.pallas_call(functools.partial(kernel_term_kernel, columns, cuts, strea...  14.6 us
    ppermute x9, starting transfers between devices, exchange_by_role(): return lax.ppermute(value, ('dp', 'space'), pairs)  11.2 us
    ppermute x2, starting transfers between devices, fetched(): return lax.ppermute(value, ('dp', 'space'), pairs)  2.58 us
    add x12, other arithmetic, add(): return part.astype(F32) + back.astype(F32)  2.33 us
  transfers between devices with their start and end apart: 20, of which 5 were waited for; matrix products, arithmetic and copies ran while one was open for 6% of the time, Pallas kernels for 36%

profile of v5, /device:TPU:0, one launch (start us, length us, event | category | flops | bytes accessed | tf_op | source)
XLA Modules:
  0.0 90.5 jit_solution(12927157914341738861)
XLA Ops:
  1.1 1.1 %broadcast_select_fusion.4 = (bf16[1,6,72,256]{3,2,1,0:T(8,128)(2,1)S(1)}, bf16[1,6,72,256]{3,2,1,0:T(8,128)(2,1)S(1)}) fusion(pred[]{:T(512)S(6)} %eq.31, bf16[1,12,72,256]{3,2,1,0:T(8,128)(2,1)} %param.5), kind=kLoop, calls=%fused_computation.36 | loop fusion | flops 221184 | bytes 884737 | tf_op jit(solution)/shard_map/jit(_where)/select_n | solution.py:26
  2.9 1.3 %collective-permute-start.1 = (bf16[2,6,72,256]{3,2,1,0:T(8,128)(2,1)S(1)}, bf16[2,6,72,256]{3,2,1,0:T(8,128)(2,1)S(1)}, u32[]{:S(2)}, u32[]{:S(2)}) collective-permute-start(bf16[2,6,72,256]{3,2,1,0:T(8,128)(2,1)S(1)} %pad_maximum_fusion), channel_id=1, source_target_pairs={{1,0},{2,1},{3,2},{4,3},{5,4},{6,5},{7,6},{8,9},{9,10},{10,11},{11... | collective-permute-start | bytes 1327112 | tf_op jit(solution)/shard_map/ppermute | solution.py:41
  4.2 1.3 %collective-permute-start.2 = (bf16[2,6,72,256]{3,2,1,0:T(8,128)(2,1)S(1)}, bf16[2,6,72,256]{3,2,1,0:T(8,128)(2,1)S(1)}, u32[]{:S(2)}, u32[]{:S(2)}) collective-permute-start(bf16[2,6,72,256]{3,2,1,0:T(8,128)(2,1)S(1)} %pad_maximum_fusion.1), channel_id=1, source_target_pairs={{2,0},{3,1},{4,2},{5,3},{6,4},{7,5},{8,10},{9,11},{10,12},{11,13},... | collective-permute-start | bytes 1327112 | tf_op jit(solution)/shard_map/ppermute | solution.py:41
  6.2 7.8 %collective-permute-start.5 = (f32[1]{0:T(128)}, f32[1]{0:T(128)}, u32[]{:S(2)}, u32[]{:S(2)}) collective-permute-start(f32[1]{0:T(128)} %convert_element_type.90.scale_ref), channel_id=1, source_target_pairs={{0,24},{8,16},{16,8},{24,0},{1,25},{9,17},{17,9},{25,1},{2,26},{10... | collective-permute-start | bytes 20 | tf_op jit(solution)/shard_map/ppermute | solution.py:22
  13.9 1.8 %collective-permute-start.4 = (f32[1]{0:T(128)}, f32[1]{0:T(128)}, u32[]{:S(2)}, u32[]{:S(2)}) collective-permute-start(f32[1]{0:T(128)} %convert_element_type.90.scale_ref), channel_id=1, source_target_pairs={{0,16},{8,24},{16,0},{24,8},{1,17},{9,25},{17,1},{25,9},{2,18},{10... | collective-permute-start | bytes 20 | tf_op jit(solution)/shard_map/ppermute | solution.py:22
  15.8 1.0 %collective-permute-start.3 = (f32[1]{0:T(128)}, f32[1]{0:T(128)}, u32[]{:S(2)}, u32[]{:S(2)}) collective-permute-start(f32[1]{0:T(128)} %convert_element_type.90.scale_ref), channel_id=1, source_target_pairs={{0,8},{8,0},{16,24},{24,16},{1,9},{9,1},{17,25},{25,17},{2,10},{10... | collective-permute-start | bytes 20 | tf_op jit(solution)/shard_map/ppermute | solution.py:22
  16.8 5.9 %kernel_term.3 = (bf16[2,2,512,864]{3,2,1,0:T(8,128)(2,1)S(1)}, f32[16,64,768]{2,1,0:T(8,128)S(1)}, f32[16,64,768]{2,1,0:T(8,128)S(1)}) custom-call(s32[2]{0:T(128)S(1)} %pad_add_fusion.place_ref, f32[1]{0:T(128)} %convert_element_type.90.scale_ref, bf16[864,2048]{1,0:T(8,128)(2,1)} %bitcast.56, bf16[864,2048]{1,0:T(8,128)(2,1)} %bitcast.57, ...), custom_call_target="tpu_custom_call" | custom-call | flops 2717908992 | bytes 9830400 | tf_op jit(solution)/shard_map/kernel_term/pallas_call | solution.py:139
  23.2 0.6 collective-permute-start.7
  24.0 4.3 %kernel_term.4 = (f32[16,64,768]{2,1,0:T(8,128)S(1)}, f32[16,64,768]{2,1,0:T(8,128)S(1)}) custom-call(s32[2]{0:T(128)S(1)} %pad_add_fusion.place_ref, f32[1]{0:T(128)} %convert_element_type.90.scale_ref, bf16[2,2,512,864]{3,2,1,0:T(8,128)(2,1)S(1)} %get-tuple-element.58.refs_0_, bf16[432,256]{1,0:T(8,128)(2,1)S(1)} %bitcast.40, bf16[432,256]{1,0:T(8,128)(2,1)S(1)} %bitcast.39), custom_call_target="tpu_custom_call" | custom-call | flops 2717908992 | bytes 9830400 | tf_op jit(solution)/shard_map/kernel_term/pallas_call | solution.py:139
  29.9 4.5 %kernel_term.5 = (f32[16,64,768]{2,1,0:T(8,128)S(1)}, f32[16,64,768]{2,1,0:T(8,128)S(1)}) custom-call(s32[2]{0:T(128)S(1)} %pad_add_fusion.place_ref, f32[1]{0:T(128)} %convert_element_type.90.scale_ref, bf16[2,2,512,864]{3,2,1,0:T(8,128)(2,1)S(1)} %get-tuple-element.58.refs_0_, bf16[432,256]{1,0:T(8,128)(2,1)S(1)} %bitcast.50, bf16[432,256]{1,0:T(8,128)(2,1)S(1)} %bitcast.49), custom_call_target="tpu_custom_call" | custom-call | flops 2717908992 | bytes 9830400 | tf_op jit(solution)/shard_map/kernel_term/pallas_call | solution.py:139
  35.8 1.6 %collective-permute-start.12 = (f16[8,64,768]{2,1,0:T(8,128)(2,1)S(1)}, f16[8,64,768]{2,1,0:T(8,128)(2,1)S(1)}, u32[]{:S(2)}, u32[]{:S(2)}) collective-permute-start(f16[8,64,768]{2,1,0:T(8,128)(2,1)S(1)} %get-tuple-element.133), channel_id=1, source_target_pairs={{0,16},{1,17},{2,18},{3,19},{4,20},{5,21},{6,22},{7,23},{8,9},{9,8... | collective-permute-start | bytes 2359304 | tf_op jit(solution)/shard_map/ppermute | solution.py:240
  37.3 1.6 %collective-permute-start.11 = (f16[8,64,768]{2,1,0:T(8,128)(2,1)S(1)}, f16[8,64,768]{2,1,0:T(8,128)(2,1)S(1)}, u32[]{:S(2)}, u32[]{:S(2)}) collective-permute-start(f16[8,64,768]{2,1,0:T(8,128)(2,1)S(1)} %get-tuple-element.134), channel_id=1, source_target_pairs={{0,2},{1,3},{2,0},{3,1},{4,6},{5,7},{6,4},{7,5},{8,10},{9,11},{10,... | collective-permute-start | bytes 2359304 | tf_op jit(solution)/shard_map/ppermute | solution.py:240
  39.5 1.0 %collective-permute-start.10 = (f16[8,64,768]{2,1,0:T(8,128)(2,1)S(1)}, f16[8,64,768]{2,1,0:T(8,128)(2,1)S(1)}, u32[]{:S(2)}, u32[]{:S(2)}) collective-permute-start(f16[8,64,768]{2,1,0:T(8,128)(2,1)S(1)} %slice_convert_fusion.2), channel_id=1, source_target_pairs={{0,16},{1,17},{2,18},{3,19},{4,20},{5,21},{6,22},{7,23},{8,9},{9,8... | collective-permute-start | bytes 2359304 | tf_op jit(solution)/shard_map/ppermute | solution.py:240
  42.5 9.2 %input_grad.2.refs_6_ = bf16[864,2048]{1,0:T(8,128)(2,1)} custom-call(f32[1]{0:T(128)S(6)} %div.7.scale_ref, bf16[432,256]{1,0:T(8,128)(2,1)S(1)} %bitcast.47, bf16[432,256]{1,0:T(8,128)(2,1)S(1)} %bitcast.45, bf16[864,256]{1,0:T(8,128)(2,1)} %bitcast.54, bf16[432,256]{1,0:T(8,128)(2,1)S(1)} %bitcast.43, bf16[432,256]{1,0:T(8,128)(2,1)S(1)} %bitcast.41, ...), custom_call_target="tpu_custom_call" | custom-call | flops 4076863488 | bytes 6488064 | tf_op jit(solution)/shard_map/input_grad/pallas_call | solution.py:197
  51.9 1.6 %collective-permute-start.15 = (f16[4,64,768]{2,1,0:T(8,128)(2,1)S(1)}, f16[4,64,768]{2,1,0:T(8,128)(2,1)S(1)}, u32[]{:S(2)}, u32[]{:S(2)}) collective-permute-start(f16[4,64,768]{2,1,0:T(8,128)(2,1)S(1)} %slice_convert_fusion.5), channel_id=1, source_target_pairs={{0,1},{1,0},{2,3},{3,2},{4,5},{5,4},{6,7},{7,6},{8,10},{9,11},{10,... | collective-permute-start | bytes 1179656 | tf_op jit(solution)/shard_map/ppermute | solution.py:240
  53.5 4.2 %collective-permute-done.11 = f16[8,64,768]{2,1,0:T(8,128)(2,1)S(1)} collective-permute-done((f16[8,64,768]{2,1,0:T(8,128)(2,1)S(1)}, f16[8,64,768]{2,1,0:T(8,128)(2,1)S(1)}, u32[]{:S(2)}, u32[]{:S(2)}) %collective-permute-start.11) | collective-permute-done | bytes 786464 | tf_op jit(solution)/shard_map/ppermute | solution.py:240
  58.6 1.8 %collective-permute-start.13 = (f16[4,64,768]{2,1,0:T(8,128)(2,1)S(1)}, f16[4,64,768]{2,1,0:T(8,128)(2,1)S(1)}, u32[]{:S(2)}, u32[]{:S(2)}) collective-permute-start(f16[4,64,768]{2,1,0:T(8,128)(2,1)S(1)} %slice_convert_fusion.3), channel_id=1, source_target_pairs={{0,1},{1,0},{2,3},{3,2},{4,5},{5,4},{6,7},{7,6},{8,10},{9,11},{10,... | collective-permute-start | bytes 1179656 | tf_op jit(solution)/shard_map/ppermute | solution.py:240
  60.5 1.6 %collective-permute-start.18 = (f16[2,64,768]{2,1,0:T(8,128)(2,1)S(1)}, f16[2,64,768]{2,1,0:T(8,128)(2,1)S(1)}, u32[]{:S(2)}, u32[]{:S(2)}) collective-permute-start(f16[2,64,768]{2,1,0:T(8,128)(2,1)S(1)} %slice_convert_fusion.8), channel_id=1, source_target_pairs={{0,2},{1,3},{2,0},{3,1},{4,6},{5,7},{6,4},{7,5},{8,24},{9,25},{10,... | collective-permute-start | bytes 589832 | tf_op jit(solution)/shard_map/ppermute | solution.py:240
  62.1 7.9 %collective-permute-done.14 = f16[4,64,768]{2,1,0:T(8,128)(2,1)S(1)} collective-permute-done((f16[4,64,768]{2,1,0:T(8,128)(2,1)S(1)}, f16[4,64,768]{2,1,0:T(8,128)(2,1)S(1)}, u32[]{:S(2)}, u32[]{:S(2)}) %collective-permute-start.14) | collective-permute-done | bytes 393248 | tf_op jit(solution)/shard_map/ppermute | solution.py:240
  70.4 1.6 %collective-permute-start.16 = (f16[2,64,768]{2,1,0:T(8,128)(2,1)S(1)}, f16[2,64,768]{2,1,0:T(8,128)(2,1)S(1)}, u32[]{:S(2)}, u32[]{:S(2)}) collective-permute-start(f16[2,64,768]{2,1,0:T(8,128)(2,1)S(1)} %slice_convert_fusion.6), channel_id=1, source_target_pairs={{0,2},{1,3},{2,0},{3,1},{4,6},{5,7},{6,4},{7,5},{8,24},{9,25},{10,... | collective-permute-start | bytes 589832 | tf_op jit(solution)/shard_map/ppermute | solution.py:240
  72.1 3.8 %collective-permute-done.17 = f16[2,64,768]{2,1,0:T(8,128)(2,1)S(1)} collective-permute-done((f16[2,64,768]{2,1,0:T(8,128)(2,1)S(1)}, f16[2,64,768]{2,1,0:T(8,128)(2,1)S(1)}, u32[]{:S(2)}, u32[]{:S(2)}) %collective-permute-start.17) | collective-permute-done | bytes 196640 | tf_op jit(solution)/shard_map/ppermute | solution.py:240
  76.3 4.0 %collective-permute-start.19 = (f16[1,64,2304]{2,1,0:T(8,128)(2,1)S(1)}, f16[1,64,2304]{2,1,0:T(8,128)(2,1)S(1)}, u32[]{:S(2)}, u32[]{:S(2)}) collective-permute-start(f16[1,64,2304]{2,1,0:T(8,128)(2,1)S(1)} %pad_maximum_fusion.3), channel_id=1, source_target_pairs={{0,4},{1,5},{2,6},{3,7},{4,0},{5,1},{6,2},{7,3},{8,12},{9,13},{10,... | collective-permute-start | bytes 884744 | tf_op jit(solution)/shard_map/ppermute | solution.py:22
  80.3 9.2 %input_grad.3 = bf16[864,2048]{1,0:T(8,128)(2,1)} custom-call(f32[1]{0:T(128)S(6)} %div.7.scale_ref, bf16[432,256]{1,0:T(8,128)(2,1)S(1)} %bitcast.48, bf16[432,256]{1,0:T(8,128)(2,1)S(1)} %bitcast.46, bf16[864,256]{1,0:T(8,128)(2,1)} %bitcast.55, bf16[432,256]{1,0:T(8,128)(2,1)S(1)} %bitcast.44, ...), custom_call_target="tpu_custom_call", output_to_operand_aliasing={{}: (7, {})} | custom-call | flops 4076863488 | bytes 6488064 | tf_op jit(solution)/shard_map/input_grad/pallas_call | solution.py:197
  89.6 0.9 mul.17
  (63 shorter events, 7.5 us)
Async XLA Ops:
  0.6 2.1 %collective-permute-start = (bf16[12,72,256]{2,1,0:T(8,128)(2,1)}, bf16[12,72,256]{2,1,0:T(8,128)(2,1)S(1)}, u32[]{:S(2)}, u32[]{:S(2)}) collective-permute-start(bf16[12,72,256]{2,1,0:T(8,128)(2,1)} %bitcast.52), channel_id=1, source_target_pairs={{0,8},{8,0},{16,24},{24,16},{1,9},{9,1},{17,25},{25,17},{2,10},{10... | collective-permute-start | bytes 1327112 | tf_op jit(solution)/shard_map/ppermute | solution.py:22
  2.9 20.3 %collective-permute-start.1 = (bf16[2,6,72,256]{3,2,1,0:T(8,128)(2,1)S(1)}, bf16[2,6,72,256]{3,2,1,0:T(8,128)(2,1)S(1)}, u32[]{:S(2)}, u32[]{:S(2)}) collective-permute-start(bf16[2,6,72,256]{3,2,1,0:T(8,128)(2,1)S(1)} %pad_maximum_fusion), channel_id=1, source_target_pairs={{1,0},{2,1},{3,2},{4,3},{5,4},{6,5},{7,6},{8,9},{9,10},{10,11},{11... | collective-permute-start | bytes 1327112 | tf_op jit(solution)/shard_map/ppermute | solution.py:41
  4.2 19.0 %collective-permute-start.2 = (bf16[2,6,72,256]{3,2,1,0:T(8,128)(2,1)S(1)}, bf16[2,6,72,256]{3,2,1,0:T(8,128)(2,1)S(1)}, u32[]{:S(2)}, u32[]{:S(2)}) collective-permute-start(bf16[2,6,72,256]{3,2,1,0:T(8,128)(2,1)S(1)} %pad_maximum_fusion.1), channel_id=1, source_target_pairs={{2,0},{3,1},{4,2},{5,3},{6,4},{7,5},{8,10},{9,11},{10,12},{11,13},... | collective-permute-start | bytes 1327112 | tf_op jit(solution)/shard_map/ppermute | solution.py:41
  6.2 17.0 %collective-permute-start.5 = (f32[1]{0:T(128)}, f32[1]{0:T(128)}, u32[]{:S(2)}, u32[]{:S(2)}) collective-permute-start(f32[1]{0:T(128)} %convert_element_type.90.scale_ref), channel_id=1, source_target_pairs={{0,24},{8,16},{16,8},{24,0},{1,25},{9,17},{17,9},{25,1},{2,26},{10... | collective-permute-start | bytes 20 | tf_op jit(solution)/shard_map/ppermute | solution.py:22
  13.9 9.3 %collective-permute-start.4 = (f32[1]{0:T(128)}, f32[1]{0:T(128)}, u32[]{:S(2)}, u32[]{:S(2)}) collective-permute-start(f32[1]{0:T(128)} %convert_element_type.90.scale_ref), channel_id=1, source_target_pairs={{0,16},{8,24},{16,0},{24,8},{1,17},{9,25},{17,1},{25,9},{2,18},{10... | collective-permute-start | bytes 20 | tf_op jit(solution)/shard_map/ppermute | solution.py:22
  15.8 7.4 %collective-permute-start.3 = (f32[1]{0:T(128)}, f32[1]{0:T(128)}, u32[]{:S(2)}, u32[]{:S(2)}) collective-permute-start(f32[1]{0:T(128)} %convert_element_type.90.scale_ref), channel_id=1, source_target_pairs={{0,8},{8,0},{16,24},{24,16},{1,9},{9,1},{17,25},{25,17},{2,10},{10... | collective-permute-start | bytes 20 | tf_op jit(solution)/shard_map/ppermute | solution.py:22
  23.2 5.6 %collective-permute-start.7 = (f16[16,64,768]{2,1,0:T(8,128)(2,1)S(1)}, f16[16,64,768]{2,1,0:T(8,128)(2,1)S(1)}, u32[]{:S(2)}, u32[]{:S(2)}) collective-permute-start(f16[16,64,768]{2,1,0:T(8,128)(2,1)S(1)} %convert_element_type.91), channel_id=1, source_target_pairs={{0,8},{8,0},{16,24},{24,16},{1,9},{9,1},{17,25},{25,17},{2,10},{10... | collective-permute-start | bytes 4718600 | tf_op jit(solution)/shard_map/ppermute | solution.py:22
  23.9 4.9 %collective-permute-start.6 = (bf16[2,6,72,256]{3,2,1,0:T(8,128)(2,1)S(1)}, bf16[2,6,72,256]{3,2,1,0:T(8,128)(2,1)S(1)}, u32[]{:S(2)}, u32[]{:S(2)}) collective-permute-start(bf16[2,6,72,256]{3,2,1,0:T(8,128)(2,1)S(1)} %pad_maximum_fusion.2), channel_id=1, source_target_pairs={{0,8},{8,0},{16,24},{24,16},{1,9},{9,1},{17,25},{25,17},{2,10},{10... | collective-permute-start | bytes 1327112 | tf_op jit(solution)/shard_map/ppermute | solution.py:22
  28.8 6.1 %collective-permute-start.8 = (f16[16,64,768]{2,1,0:T(8,128)(2,1)S(1)}, f16[16,64,768]{2,1,0:T(8,128)(2,1)S(1)}, u32[]{:S(2)}, u32[]{:S(2)}) collective-permute-start(f16[16,64,768]{2,1,0:T(8,128)(2,1)S(1)} %convert_element_type.93), channel_id=1, source_target_pairs={{0,8},{8,0},{16,24},{24,16},{1,9},{9,1},{17,25},{25,17},{2,10},{10... | collective-permute-start | bytes 4718600 | tf_op jit(solution)/shard_map/ppermute | solution.py:22
  34.9 4.0 %collective-permute-start.9 = (f16[16,64,768]{2,1,0:T(8,128)(2,1)S(1)}, f16[16,64,768]{2,1,0:T(8,128)(2,1)S(1)}, u32[]{:S(2)}, u32[]{:S(2)}) collective-permute-start(f16[16,64,768]{2,1,0:T(8,128)(2,1)S(1)} %convert_element_type.98), channel_id=1, source_target_pairs={{0,8},{8,0},{16,24},{24,16},{1,9},{9,1},{17,25},{25,17},{2,10},{10... | collective-permute-start | bytes 4718600 | tf_op jit(solution)/shard_map/ppermute | solution.py:22
  35.8 15.9 %collective-permute-start.12 = (f16[8,64,768]{2,1,0:T(8,128)(2,1)S(1)}, f16[8,64,768]{2,1,0:T(8,128)(2,1)S(1)}, u32[]{:S(2)}, u32[]{:S(2)}) collective-permute-start(f16[8,64,768]{2,1,0:T(8,128)(2,1)S(1)} %get-tuple-element.133), channel_id=1, source_target_pairs={{0,16},{1,17},{2,18},{3,19},{4,20},{5,21},{6,22},{7,23},{8,9},{9,8... | collective-permute-start | bytes 2359304 | tf_op jit(solution)/shard_map/ppermute | solution.py:240
  37.3 20.4 %collective-permute-start.11 = (f16[8,64,768]{2,1,0:T(8,128)(2,1)S(1)}, f16[8,64,768]{2,1,0:T(8,128)(2,1)S(1)}, u32[]{:S(2)}, u32[]{:S(2)}) collective-permute-start(f16[8,64,768]{2,1,0:T(8,128)(2,1)S(1)} %get-tuple-element.134), channel_id=1, source_target_pairs={{0,2},{1,3},{2,0},{3,1},{4,6},{5,7},{6,4},{7,5},{8,10},{9,11},{10,... | collective-permute-start | bytes 2359304 | tf_op jit(solution)/shard_map/ppermute | solution.py:240
  39.5 18.9 %collective-permute-start.10 = (f16[8,64,768]{2,1,0:T(8,128)(2,1)S(1)}, f16[8,64,768]{2,1,0:T(8,128)(2,1)S(1)}, u32[]{:S(2)}, u32[]{:S(2)}) collective-permute-start(f16[8,64,768]{2,1,0:T(8,128)(2,1)S(1)} %slice_convert_fusion.2), channel_id=1, source_target_pairs={{0,16},{1,17},{2,18},{3,19},{4,20},{5,21},{6,22},{7,23},{8,9},{9,8... | collective-permute-start | bytes 2359304 | tf_op jit(solution)/shard_map/ppermute | solution.py:240
  51.9 8.5 %collective-permute-start.15 = (f16[4,64,768]{2,1,0:T(8,128)(2,1)S(1)}, f16[4,64,768]{2,1,0:T(8,128)(2,1)S(1)}, u32[]{:S(2)}, u32[]{:S(2)}) collective-permute-start(f16[4,64,768]{2,1,0:T(8,128)(2,1)S(1)} %slice_convert_fusion.5), channel_id=1, source_target_pairs={{0,1},{1,0},{2,3},{3,2},{4,5},{5,4},{6,7},{7,6},{8,10},{9,11},{10,... | collective-permute-start | bytes 1179656 | tf_op jit(solution)/shard_map/ppermute | solution.py:240
  57.9 12.1 %collective-permute-start.14 = (f16[4,64,768]{2,1,0:T(8,128)(2,1)S(1)}, f16[4,64,768]{2,1,0:T(8,128)(2,1)S(1)}, u32[]{:S(2)}, u32[]{:S(2)}) collective-permute-start(f16[4,64,768]{2,1,0:T(8,128)(2,1)S(1)} %slice_convert_fusion.4), channel_id=1, source_target_pairs={{0,16},{1,17},{2,18},{3,19},{4,20},{5,21},{6,22},{7,23},{8,24},{9,... | collective-permute-start | bytes 1179656 | tf_op jit(solution)/shard_map/ppermute | solution.py:240
  58.6 11.6 %collective-permute-start.13 = (f16[4,64,768]{2,1,0:T(8,128)(2,1)S(1)}, f16[4,64,768]{2,1,0:T(8,128)(2,1)S(1)}, u32[]{:S(2)}, u32[]{:S(2)}) collective-permute-start(f16[4,64,768]{2,1,0:T(8,128)(2,1)S(1)} %slice_convert_fusion.3), channel_id=1, source_target_pairs={{0,1},{1,0},{2,3},{3,2},{4,5},{5,4},{6,7},{7,6},{8,10},{9,11},{10,... | collective-permute-start | bytes 1179656 | tf_op jit(solution)/shard_map/ppermute | solution.py:240
  60.5 11.5 %collective-permute-start.18 = (f16[2,64,768]{2,1,0:T(8,128)(2,1)S(1)}, f16[2,64,768]{2,1,0:T(8,128)(2,1)S(1)}, u32[]{:S(2)}, u32[]{:S(2)}) collective-permute-start(f16[2,64,768]{2,1,0:T(8,128)(2,1)S(1)} %slice_convert_fusion.8), channel_id=1, source_target_pairs={{0,2},{1,3},{2,0},{3,1},{4,6},{5,7},{6,4},{7,5},{8,24},{9,25},{10,... | collective-permute-start | bytes 589832 | tf_op jit(solution)/shard_map/ppermute | solution.py:240
  70.2 5.7 %collective-permute-start.17 = (f16[2,64,768]{2,1,0:T(8,128)(2,1)S(1)}, f16[2,64,768]{2,1,0:T(8,128)(2,1)S(1)}, u32[]{:S(2)}, u32[]{:S(2)}) collective-permute-start(f16[2,64,768]{2,1,0:T(8,128)(2,1)S(1)} %slice_convert_fusion.7), channel_id=1, source_target_pairs={{0,1},{1,0},{2,3},{3,2},{4,5},{5,4},{6,7},{7,6},{8,9},{9,8},{10,11... | collective-permute-start | bytes 589832 | tf_op jit(solution)/shard_map/ppermute | solution.py:240
  70.4 5.7 %collective-permute-start.16 = (f16[2,64,768]{2,1,0:T(8,128)(2,1)S(1)}, f16[2,64,768]{2,1,0:T(8,128)(2,1)S(1)}, u32[]{:S(2)}, u32[]{:S(2)}) collective-permute-start(f16[2,64,768]{2,1,0:T(8,128)(2,1)S(1)} %slice_convert_fusion.6), channel_id=1, source_target_pairs={{0,2},{1,3},{2,0},{3,1},{4,6},{5,7},{6,4},{7,5},{8,24},{9,25},{10,... | collective-permute-start | bytes 589832 | tf_op jit(solution)/shard_map/ppermute | solution.py:240
  76.3 13.2 %collective-permute-start.19 = (f16[1,64,2304]{2,1,0:T(8,128)(2,1)S(1)}, f16[1,64,2304]{2,1,0:T(8,128)(2,1)S(1)}, u32[]{:S(2)}, u32[]{:S(2)}) collective-permute-start(f16[1,64,2304]{2,1,0:T(8,128)(2,1)S(1)} %pad_maximum_fusion.3), channel_id=1, source_target_pairs={{0,4},{1,5},{2,6},{3,7},{4,0},{5,1},{6,2},{7,3},{8,12},{9,13},{10,... | collective-permute-start | bytes 884744 | tf_op jit(solution)/shard_map/ppermute | solution.py:22

commit v6 on v5

--- a/solution.py
+++ b/solution.py
@@ -306,39 +306,52 @@
     ring[0] = add(first[1], back)
 
     blocks = in_channels // CHANNELS_PER_STEP
-    early = blocks * 4 // 8
+    cuts = [0, blocks * 3 // 8, blocks * 5 // 8, blocks]
     last = len(centre_order) - 1
     rows_of = [below, [in_hbm(flat(tile))], above]
     chains = [[ring[1], orders, None], [centre, (centre_order, centre_order), None], [ring[0], orders, None]]
     grad_features = token = None
+
+    def next_columns(turn, *operands):
+        return input_grad(
+            columns,
+            scale,
+            after(rows_of, *operands),
+            weight,
+            cuts[turn],
+            cuts[turn + 1] - cuts[turn],
+            grad_features,
+        )
+
     for step in range(last):
         operands = []
-        for chain in chains if step == 0 else [chains[i] for i in (0,1,2)]:
+        for chain in chains:
             part, order, back = chain
             if step:
                 part = add(kept(part), after(back, token))
             token = sent(part)
             operands.append(token)
             chain[0], chain[2] = part, exchange_by_role(token, order, step)
+            if step == last - 1 and chain is chains[0]:
+                token = grad_features = next_columns(1, token)
         if step == 0:
             survivors = sum(after(alive_all, *operands))
             scale = own_alive / survivors
-            grad_features = input_grad(
-                columns, scale, after(rows_of, *operands), weight, 0, early, grad_features
-            )
-            token = grad_features
+            token = grad_features = next_columns(0, *operands)
     parts = []
     for part, order, back in chains:
         parts.append(add(kept(part), after(back, token)))
         token = sent(parts[-1])
-    operands = jnp.concatenate([sent(part) for part in parts], axis=-1)
+        if len(parts) == 1:
+            ahead = exchange(token, *centre_order[last])
+    operands = jnp.concatenate([sent(part) for part in parts[1:]], axis=-1)
     back = exchange(operands, *centre_order[last])
-    grad_features = input_grad(
-        columns, scale, after(rows_of, operands), weight, early, blocks - early, grad_features
+    grad_features = next_columns(2, operands)
+    back, ahead, grad_features = lax.optimization_barrier((back, ahead, grad_features))
+    second, centre, first = (
+        add(kept(part), value)[0]
+        for part, value in zip(parts, (ahead, back[..., :width], back[..., width:]))
     )
-    back, grad_features = lax.optimization_barrier((back, grad_features))
-    parts = [add(kept(part), back[..., width * i : width * (i + 1)]) for i, part in enumerate(parts)]
-    second, centre, first = (part[0] for part in parts)
     final = jnp.concatenate([either(first, second), centre, either(second, first)], axis=-1)
     final = final * (member_count * 0.25 / survivors)
     return (final.reshape(-1, out_channels), grad_features.reshape(features.shape))

time: 90.8 us -> 88.4 us (0.974)
  Pallas kernels: 33 us -> 36.1 us
  waiting for transfers between devices: 16.7 us -> 13.7 us
  starting transfers between devices: 30.2 us -> 27.8 us
    ppermute x9, waiting for transfers between devices: 16.1 us -> 12.6 us  [exchange_by_role(): return lax.ppermute(value, ('dp', 'space'), pairs)]
    pallas_call x2 -> x3, Pallas kernels: 18.4 us -> 21.4 us  [input_grad(): pl.pallas_call(functools.partial(input_grad_kernel, columns, cuts), grid=...]
    ppermute x9 -> x10, starting transfers between devices: 16.4 us -> 14 us  [exchange(): lax.ppermute(value, axis, [(i, i ^ bit) for i in range(lax.axis_size(axis...]
  transfers between devices with their start and end apart: 20 -> 21, of which waited for: 5 -> 6; matrix products, arithmetic and copies ran while one was open for 6% -> 7% of each run, Pallas kernels for 36% -> 41%
where the time goes in v6:
time: 88.4 us; the launch traced here: 88.1 us
  Pallas kernels  36.1 us (41%)
  starting transfers between devices  27.8 us (31%)
  waiting for transfers between devices  13.7 us (15%)
  other arithmetic  6.04 us (7%)
  between operations  3.63 us (4%)
  local copies, waits for them, and re-layouts  0.89 us (1%)
    pallas_call x3, Pallas kernels, input_grad(): pl.pallas_call(functools.partial(input_grad_kernel, columns, cuts), grid=...  21.4 us
    pallas_call x3, Pallas kernels, kernel_term(): pl.pallas_call(functools.partial(kernel_term_kernel, columns, cuts, strea...  14.6 us
    ppermute x10, starting transfers between devices, exchange(): lax.ppermute(value, axis, [(i, i ^ bit) for i in range(lax.axis_size(axis...  14 us
    ppermute x9, waiting for transfers between devices, exchange_by_role(): return lax.ppermute(value, ('dp', 'space'), pairs)  12.6 us
    ppermute x9, starting transfers between devices, exchange_by_role(): return lax.ppermute(value, ('dp', 'space'), pairs)  11.2 us
    ppermute x2, starting transfers between devices, fetched(): return lax.ppermute(value, ('dp', 'space'), pairs)  2.58 us
    add x12, other arithmetic, add(): return part.astype(F32) + back.astype(F32)  2.33 us
  transfers between devices with their start and end apart: 21, of which 6 were waited for; matrix products, arithmetic and copies ran while one was open for 7% of the time, Pallas kernels for 41%

profile of v6, /device:TPU:0, one launch (start us, length us, event | category | flops | bytes accessed | tf_op | source)
XLA Modules:
  0.0 88.1 jit_solution(14316601167294499435)
XLA Ops:
  1.1 1.1 %broadcast_select_fusion.4 = (bf16[1,6,72,256]{3,2,1,0:T(8,128)(2,1)S(1)}, bf16[1,6,72,256]{3,2,1,0:T(8,128)(2,1)S(1)}) fusion(pred[]{:T(512)S(6)} %eq.31, bf16[1,12,72,256]{3,2,1,0:T(8,128)(2,1)} %param.5), kind=kLoop, calls=%fused_computation.35 | loop fusion | flops 221184 | bytes 884737 | tf_op jit(solution)/shard_map/jit(_where)/select_n | solution.py:26
  2.9 1.3 %collective-permute-start.1 = (bf16[2,6,72,256]{3,2,1,0:T(8,128)(2,1)S(1)}, bf16[2,6,72,256]{3,2,1,0:T(8,128)(2,1)S(1)}, u32[]{:S(2)}, u32[]{:S(2)}) collective-permute-start(bf16[2,6,72,256]{3,2,1,0:T(8,128)(2,1)S(1)} %pad_maximum_fusion), channel_id=1, source_target_pairs={{1,0},{2,1},{3,2},{4,3},{5,4},{6,5},{7,6},{8,9},{9,10},{10,11},{11... | collective-permute-start | bytes 1327112 | tf_op jit(solution)/shard_map/ppermute | solution.py:41
  4.2 1.3 %collective-permute-start.2 = (bf16[2,6,72,256]{3,2,1,0:T(8,128)(2,1)S(1)}, bf16[2,6,72,256]{3,2,1,0:T(8,128)(2,1)S(1)}, u32[]{:S(2)}, u32[]{:S(2)}) collective-permute-start(bf16[2,6,72,256]{3,2,1,0:T(8,128)(2,1)S(1)} %pad_maximum_fusion.1), channel_id=1, source_target_pairs={{2,0},{3,1},{4,2},{5,3},{6,4},{7,5},{8,10},{9,11},{10,12},{11,13},... | collective-permute-start | bytes 1327112 | tf_op jit(solution)/shard_map/ppermute | solution.py:41
  6.2 7.8 %collective-permute-start.5 = (f32[1]{0:T(128)}, f32[1]{0:T(128)}, u32[]{:S(2)}, u32[]{:S(2)}) collective-permute-start(f32[1]{0:T(128)} %convert_element_type.89.scale_ref), channel_id=1, source_target_pairs={{0,24},{8,16},{16,8},{24,0},{1,25},{9,17},{17,9},{25,1},{2,26},{10... | collective-permute-start | bytes 20 | tf_op jit(solution)/shard_map/ppermute | solution.py:22
  13.9 1.8 %collective-permute-start.4 = (f32[1]{0:T(128)}, f32[1]{0:T(128)}, u32[]{:S(2)}, u32[]{:S(2)}) collective-permute-start(f32[1]{0:T(128)} %convert_element_type.89.scale_ref), channel_id=1, source_target_pairs={{0,16},{8,24},{16,0},{24,8},{1,17},{9,25},{17,1},{25,9},{2,18},{10... | collective-permute-start | bytes 20 | tf_op jit(solution)/shard_map/ppermute | solution.py:22
  16.7 5.9 %kernel_term.3 = (bf16[2,2,512,864]{3,2,1,0:T(8,128)(2,1)S(1)}, f32[16,64,768]{2,1,0:T(8,128)S(1)}, f32[16,64,768]{2,1,0:T(8,128)S(1)}) custom-call(s32[2]{0:T(128)S(1)} %pad_add_fusion.place_ref, f32[1]{0:T(128)} %convert_element_type.89.scale_ref, bf16[864,2048]{1,0:T(8,128)(2,1)} %bitcast.65, bf16[864,2048]{1,0:T(8,128)(2,1)} %bitcast.66, ...), custom_call_target="tpu_custom_call" | custom-call | flops 2717908992 | bytes 9830400 | tf_op jit(solution)/shard_map/kernel_term/pallas_call | solution.py:139
  23.9 4.3 %kernel_term.4 = (f32[16,64,768]{2,1,0:T(8,128)S(1)}, f32[16,64,768]{2,1,0:T(8,128)S(1)}) custom-call(s32[2]{0:T(128)S(1)} %pad_add_fusion.place_ref, f32[1]{0:T(128)} %convert_element_type.89.scale_ref, bf16[2,2,512,864]{3,2,1,0:T(8,128)(2,1)S(1)} %get-tuple-element.64.refs_0_, bf16[432,256]{1,0:T(8,128)(2,1)S(1)} %bitcast.56, bf16[432,256]{1,0:T(8,128)(2,1)S(1)} %bitcast.55), custom_call_target="tpu_custom_call" | custom-call | flops 2717908992 | bytes 9830400 | tf_op jit(solution)/shard_map/kernel_term/pallas_call | solution.py:139
  29.8 4.5 %kernel_term.5 = (f32[16,64,768]{2,1,0:T(8,128)S(1)}, f32[16,64,768]{2,1,0:T(8,128)S(1)}) custom-call(s32[2]{0:T(128)S(1)} %pad_add_fusion.place_ref, f32[1]{0:T(128)} %convert_element_type.89.scale_ref, bf16[2,2,512,864]{3,2,1,0:T(8,128)(2,1)S(1)} %get-tuple-element.64.refs_0_, bf16[432,256]{1,0:T(8,128)(2,1)S(1)} %bitcast.58, bf16[432,256]{1,0:T(8,128)(2,1)S(1)} %bitcast.57), custom_call_target="tpu_custom_call" | custom-call | flops 2717908992 | bytes 9830400 | tf_op jit(solution)/shard_map/kernel_term/pallas_call | solution.py:139
  35.6 1.6 %collective-permute-start.12 = (f16[8,64,768]{2,1,0:T(8,128)(2,1)S(1)}, f16[8,64,768]{2,1,0:T(8,128)(2,1)S(1)}, u32[]{:S(2)}, u32[]{:S(2)}) collective-permute-start(f16[8,64,768]{2,1,0:T(8,128)(2,1)S(1)} %get-tuple-element.145), channel_id=1, source_target_pairs={{0,16},{1,17},{2,18},{3,19},{4,20},{5,21},{6,22},{7,23},{8,9},{9,8... | collective-permute-start | bytes 2359304 | tf_op jit(solution)/shard_map/ppermute | solution.py:240
  37.2 1.6 %collective-permute-start.11 = (f16[8,64,768]{2,1,0:T(8,128)(2,1)S(1)}, f16[8,64,768]{2,1,0:T(8,128)(2,1)S(1)}, u32[]{:S(2)}, u32[]{:S(2)}) collective-permute-start(f16[8,64,768]{2,1,0:T(8,128)(2,1)S(1)} %get-tuple-element.146), channel_id=1, source_target_pairs={{0,2},{1,3},{2,0},{3,1},{4,6},{5,7},{6,4},{7,5},{8,10},{9,11},{10,... | collective-permute-start | bytes 2359304 | tf_op jit(solution)/shard_map/ppermute | solution.py:240
  39.3 1.1 %collective-permute-start.10 = (f16[8,64,768]{2,1,0:T(8,128)(2,1)S(1)}, f16[8,64,768]{2,1,0:T(8,128)(2,1)S(1)}, u32[]{:S(2)}, u32[]{:S(2)}) collective-permute-start(f16[8,64,768]{2,1,0:T(8,128)(2,1)S(1)} %slice_convert_fusion.2), channel_id=1, source_target_pairs={{0,16},{1,17},{2,18},{3,19},{4,20},{5,21},{6,22},{7,23},{8,9},{9,8... | collective-permute-start | bytes 2359304 | tf_op jit(solution)/shard_map/ppermute | solution.py:240
  42.4 7.7 %input_grad.3.refs_6_ = bf16[864,2048]{1,0:T(8,128)(2,1)} custom-call(f32[1]{0:T(128)S(6)} %div.7.scale_ref, bf16[432,256]{1,0:T(8,128)(2,1)S(1)} %bitcast.52, bf16[432,256]{1,0:T(8,128)(2,1)S(1)} %bitcast.49, bf16[864,256]{1,0:T(8,128)(2,1)} %bitcast.62, bf16[432,256]{1,0:T(8,128)(2,1)S(1)} %bitcast.46, bf16[432,256]{1,0:T(8,128)(2,1)S(1)} %bitcast.43, ...), custom_call_target="tpu_custom_call" | custom-call | flops 3057647616 | bytes 4866048 | tf_op jit(solution)/shard_map/input_grad/pallas_call | solution.py:197
  50.3 1.6 %collective-permute-start.15 = (f16[4,64,768]{2,1,0:T(8,128)(2,1)S(1)}, f16[4,64,768]{2,1,0:T(8,128)(2,1)S(1)}, u32[]{:S(2)}, u32[]{:S(2)}) collective-permute-start(f16[4,64,768]{2,1,0:T(8,128)(2,1)S(1)} %slice_convert_fusion.5), channel_id=1, source_target_pairs={{0,1},{1,0},{2,3},{3,2},{4,5},{5,4},{6,7},{7,6},{8,10},{9,11},{10,... | collective-permute-start | bytes 1179656 | tf_op jit(solution)/shard_map/ppermute | solution.py:240
  51.9 5.7 %collective-permute-done.11 = f16[8,64,768]{2,1,0:T(8,128)(2,1)S(1)} collective-permute-done((f16[8,64,768]{2,1,0:T(8,128)(2,1)S(1)}, f16[8,64,768]{2,1,0:T(8,128)(2,1)S(1)}, u32[]{:S(2)}, u32[]{:S(2)}) %collective-permute-start.11) | collective-permute-done | bytes 786464 | tf_op jit(solution)/shard_map/ppermute | solution.py:240
  58.4 1.8 %collective-permute-start.13 = (f16[4,64,768]{2,1,0:T(8,128)(2,1)S(1)}, f16[4,64,768]{2,1,0:T(8,128)(2,1)S(1)}, u32[]{:S(2)}, u32[]{:S(2)}) collective-permute-start(f16[4,64,768]{2,1,0:T(8,128)(2,1)S(1)} %slice_convert_fusion.3), channel_id=1, source_target_pairs={{0,1},{1,0},{2,3},{3,2},{4,5},{5,4},{6,7},{7,6},{8,10},{9,11},{10,... | collective-permute-start | bytes 1179656 | tf_op jit(solution)/shard_map/ppermute | solution.py:240
  60.3 1.6 %collective-permute-start.18 = (f16[2,64,768]{2,1,0:T(8,128)(2,1)S(1)}, f16[2,64,768]{2,1,0:T(8,128)(2,1)S(1)}, u32[]{:S(2)}, u32[]{:S(2)}) collective-permute-start(f16[2,64,768]{2,1,0:T(8,128)(2,1)S(1)} %slice_convert_fusion.8), channel_id=1, source_target_pairs={{0,2},{1,3},{2,0},{3,1},{4,6},{5,7},{6,4},{7,5},{8,24},{9,25},{10,... | collective-permute-start | bytes 589832 | tf_op jit(solution)/shard_map/ppermute | solution.py:240
  61.9 6.1 %input_grad.4.refs_6_ = bf16[864,2048]{1,0:T(8,128)(2,1)} custom-call(f32[1]{0:T(128)S(6)} %div.7.scale_ref, bf16[432,256]{1,0:T(8,128)(2,1)S(1)} %bitcast.53, bf16[432,256]{1,0:T(8,128)(2,1)S(1)} %bitcast.50, bf16[864,256]{1,0:T(8,128)(2,1)} %bitcast.63, bf16[432,256]{1,0:T(8,128)(2,1)S(1)} %bitcast.47, ...), custom_call_target="tpu_custom_call", output_to_operand_aliasing={{}: (7, {})} | custom-call | flops 2038431744 | bytes 3244032 | tf_op jit(solution)/shard_map/input_grad/pallas_call | solution.py:197
  68.1 1.8 %collective-permute-done.14 = f16[4,64,768]{2,1,0:T(8,128)(2,1)S(1)} collective-permute-done((f16[4,64,768]{2,1,0:T(8,128)(2,1)S(1)}, f16[4,64,768]{2,1,0:T(8,128)(2,1)S(1)}, u32[]{:S(2)}, u32[]{:S(2)}) %collective-permute-start.14) | collective-permute-done | bytes 393248 | tf_op jit(solution)/shard_map/ppermute | solution.py:240
  70.3 1.6 %collective-permute-start.16 = (f16[2,64,768]{2,1,0:T(8,128)(2,1)S(1)}, f16[2,64,768]{2,1,0:T(8,128)(2,1)S(1)}, u32[]{:S(2)}, u32[]{:S(2)}) collective-permute-start(f16[2,64,768]{2,1,0:T(8,128)(2,1)S(1)} %slice_convert_fusion.6), channel_id=1, source_target_pairs={{0,2},{1,3},{2,0},{3,1},{4,6},{5,7},{6,4},{7,5},{8,24},{9,25},{10,... | collective-permute-start | bytes 589832 | tf_op jit(solution)/shard_map/ppermute | solution.py:240
  72.0 1.5 %collective-permute-start.20 = (f16[1,64,768]{2,1,0:T(8,128)(2,1)S(1)}, f16[1,64,768]{2,1,0:T(8,128)(2,1)S(1)}, u32[]{:S(2)}, u32[]{:S(2)}) collective-permute-start(f16[1,64,768]{2,1,0:T(8,128)(2,1)S(1)} %slice_convert_fusion.11), channel_id=1, source_target_pairs={{0,4},{1,5},{2,6},{3,7},{4,0},{5,1},{6,2},{7,3},{8,12},{9,13},{10,... | collective-permute-start | bytes 294920 | tf_op jit(solution)/shard_map/ppermute | solution.py:22
  73.4 2.3 %collective-permute-done.17 = f16[2,64,768]{2,1,0:T(8,128)(2,1)S(1)} collective-permute-done((f16[2,64,768]{2,1,0:T(8,128)(2,1)S(1)}, f16[2,64,768]{2,1,0:T(8,128)(2,1)S(1)}, u32[]{:S(2)}, u32[]{:S(2)}) %collective-permute-start.17) | collective-permute-done | bytes 196640 | tf_op jit(solution)/shard_map/ppermute | solution.py:240
  75.9 2.7 %collective-permute-done.16 = f16[2,64,768]{2,1,0:T(8,128)(2,1)S(1)} collective-permute-done((f16[2,64,768]{2,1,0:T(8,128)(2,1)S(1)}, f16[2,64,768]{2,1,0:T(8,128)(2,1)S(1)}, u32[]{:S(2)}, u32[]{:S(2)}) %collective-permute-start.16) | collective-permute-done | bytes 196640 | tf_op jit(solution)/shard_map/ppermute | solution.py:240
  79.0 7.6 %input_grad.5 = bf16[864,2048]{1,0:T(8,128)(2,1)} custom-call(f32[1]{0:T(128)S(6)} %div.7.scale_ref, bf16[432,256]{1,0:T(8,128)(2,1)S(1)} %bitcast.54, bf16[432,256]{1,0:T(8,128)(2,1)S(1)} %bitcast.51, bf16[864,256]{1,0:T(8,128)(2,1)} %bitcast.64, bf16[432,256]{1,0:T(8,128)(2,1)S(1)} %bitcast.48, ...), custom_call_target="tpu_custom_call", output_to_operand_aliasing={{}: (7, {})} | custom-call | flops 3057647616 | bytes 4866048 | tf_op jit(solution)/shard_map/input_grad/pallas_call | solution.py:197
  87.2 0.9 %mul.17 = f32[576,256]{1,0:T(8,128)} reshape(f32[64,2304]{1,0:T(8,128)S(1)} %maximum_multiply_fusion) | data formatting | bytes 1179648 | tf_op jit(solution)/shard_map/mul | solution.py:356
  (66 shorter events, 9.5 us)
Async XLA Ops:
  0.6 2.1 %collective-permute-start = (bf16[12,72,256]{2,1,0:T(8,128)(2,1)}, bf16[12,72,256]{2,1,0:T(8,128)(2,1)S(1)}, u32[]{:S(2)}, u32[]{:S(2)}) collective-permute-start(bf16[12,72,256]{2,1,0:T(8,128)(2,1)} %bitcast.60), channel_id=1, source_target_pairs={{0,8},{8,0},{16,24},{24,16},{1,9},{9,1},{17,25},{25,17},{2,10},{10... | collective-permute-start | bytes 1327112 | tf_op jit(solution)/shard_map/ppermute | solution.py:22
  2.9 20.2 %collective-permute-start.1 = (bf16[2,6,72,256]{3,2,1,0:T(8,128)(2,1)S(1)}, bf16[2,6,72,256]{3,2,1,0:T(8,128)(2,1)S(1)}, u32[]{:S(2)}, u32[]{:S(2)}) collective-permute-start(bf16[2,6,72,256]{3,2,1,0:T(8,128)(2,1)S(1)} %pad_maximum_fusion), channel_id=1, source_target_pairs={{1,0},{2,1},{3,2},{4,3},{5,4},{6,5},{7,6},{8,9},{9,10},{10,11},{11... | collective-permute-start | bytes 1327112 | tf_op jit(solution)/shard_map/ppermute | solution.py:41
  4.2 18.9 %collective-permute-start.2 = (bf16[2,6,72,256]{3,2,1,0:T(8,128)(2,1)S(1)}, bf16[2,6,72,256]{3,2,1,0:T(8,128)(2,1)S(1)}, u32[]{:S(2)}, u32[]{:S(2)}) collective-permute-start(bf16[2,6,72,256]{3,2,1,0:T(8,128)(2,1)S(1)} %pad_maximum_fusion.1), channel_id=1, source_target_pairs={{2,0},{3,1},{4,2},{5,3},{6,4},{7,5},{8,10},{9,11},{10,12},{11,13},... | collective-permute-start | bytes 1327112 | tf_op jit(solution)/shard_map/ppermute | solution.py:41
  6.2 16.9 %collective-permute-start.5 = (f32[1]{0:T(128)}, f32[1]{0:T(128)}, u32[]{:S(2)}, u32[]{:S(2)}) collective-permute-start(f32[1]{0:T(128)} %convert_element_type.89.scale_ref), channel_id=1, source_target_pairs={{0,24},{8,16},{16,8},{24,0},{1,25},{9,17},{17,9},{25,1},{2,26},{10... | collective-permute-start | bytes 20 | tf_op jit(solution)/shard_map/ppermute | solution.py:22
  13.9 9.1 %collective-permute-start.4 = (f32[1]{0:T(128)}, f32[1]{0:T(128)}, u32[]{:S(2)}, u32[]{:S(2)}) collective-permute-start(f32[1]{0:T(128)} %convert_element_type.89.scale_ref), channel_id=1, source_target_pairs={{0,16},{8,24},{16,0},{24,8},{1,17},{9,25},{17,1},{25,9},{2,18},{10... | collective-permute-start | bytes 20 | tf_op jit(solution)/shard_map/ppermute | solution.py:22
  15.8 7.3 %collective-permute-start.3 = (f32[1]{0:T(128)}, f32[1]{0:T(128)}, u32[]{:S(2)}, u32[]{:S(2)}) collective-permute-start(f32[1]{0:T(128)} %convert_element_type.89.scale_ref), channel_id=1, source_target_pairs={{0,8},{8,0},{16,24},{24,16},{1,9},{9,1},{17,25},{25,17},{2,10},{10... | collective-permute-start | bytes 20 | tf_op jit(solution)/shard_map/ppermute | solution.py:22
  23.1 5.6 %collective-permute-start.7 = (f16[16,64,768]{2,1,0:T(8,128)(2,1)S(1)}, f16[16,64,768]{2,1,0:T(8,128)(2,1)S(1)}, u32[]{:S(2)}, u32[]{:S(2)}) collective-permute-start(f16[16,64,768]{2,1,0:T(8,128)(2,1)S(1)} %convert_element_type.90), channel_id=1, source_target_pairs={{0,8},{8,0},{16,24},{24,16},{1,9},{9,1},{17,25},{25,17},{2,10},{10... | collective-permute-start | bytes 4718600 | tf_op jit(solution)/shard_map/ppermute | solution.py:22
  23.8 4.9 %collective-permute-start.6 = (bf16[2,6,72,256]{3,2,1,0:T(8,128)(2,1)S(1)}, bf16[2,6,72,256]{3,2,1,0:T(8,128)(2,1)S(1)}, u32[]{:S(2)}, u32[]{:S(2)}) collective-permute-start(bf16[2,6,72,256]{3,2,1,0:T(8,128)(2,1)S(1)} %pad_maximum_fusion.2), channel_id=1, source_target_pairs={{0,8},{8,0},{16,24},{24,16},{1,9},{9,1},{17,25},{25,17},{2,10},{10... | collective-permute-start | bytes 1327112 | tf_op jit(solution)/shard_map/ppermute | solution.py:22
  28.7 6.0 %collective-permute-start.8 = (f16[16,64,768]{2,1,0:T(8,128)(2,1)S(1)}, f16[16,64,768]{2,1,0:T(8,128)(2,1)S(1)}, u32[]{:S(2)}, u32[]{:S(2)}) collective-permute-start(f16[16,64,768]{2,1,0:T(8,128)(2,1)S(1)} %convert_element_type.92), channel_id=1, source_target_pairs={{0,8},{8,0},{16,24},{24,16},{1,9},{9,1},{17,25},{25,17},{2,10},{10... | collective-permute-start | bytes 4718600 | tf_op jit(solution)/shard_map/ppermute | solution.py:22
  34.8 4.0 %collective-permute-start.9 = (f16[16,64,768]{2,1,0:T(8,128)(2,1)S(1)}, f16[16,64,768]{2,1,0:T(8,128)(2,1)S(1)}, u32[]{:S(2)}, u32[]{:S(2)}) collective-permute-start(f16[16,64,768]{2,1,0:T(8,128)(2,1)S(1)} %convert_element_type.97), channel_id=1, source_target_pairs={{0,8},{8,0},{16,24},{24,16},{1,9},{9,1},{17,25},{25,17},{2,10},{10... | collective-permute-start | bytes 4718600 | tf_op jit(solution)/shard_map/ppermute | solution.py:22
  35.6 14.4 %collective-permute-start.12 = (f16[8,64,768]{2,1,0:T(8,128)(2,1)S(1)}, f16[8,64,768]{2,1,0:T(8,128)(2,1)S(1)}, u32[]{:S(2)}, u32[]{:S(2)}) collective-permute-start(f16[8,64,768]{2,1,0:T(8,128)(2,1)S(1)} %get-tuple-element.145), channel_id=1, source_target_pairs={{0,16},{1,17},{2,18},{3,19},{4,20},{5,21},{6,22},{7,23},{8,9},{9,8... | collective-permute-start | bytes 2359304 | tf_op jit(solution)/shard_map/ppermute | solution.py:240
  37.2 20.4 %collective-permute-start.11 = (f16[8,64,768]{2,1,0:T(8,128)(2,1)S(1)}, f16[8,64,768]{2,1,0:T(8,128)(2,1)S(1)}, u32[]{:S(2)}, u32[]{:S(2)}) collective-permute-start(f16[8,64,768]{2,1,0:T(8,128)(2,1)S(1)} %get-tuple-element.146), channel_id=1, source_target_pairs={{0,2},{1,3},{2,0},{3,1},{4,6},{5,7},{6,4},{7,5},{8,10},{9,11},{10,... | collective-permute-start | bytes 2359304 | tf_op jit(solution)/shard_map/ppermute | solution.py:240
  39.3 18.9 %collective-permute-start.10 = (f16[8,64,768]{2,1,0:T(8,128)(2,1)S(1)}, f16[8,64,768]{2,1,0:T(8,128)(2,1)S(1)}, u32[]{:S(2)}, u32[]{:S(2)}) collective-permute-start(f16[8,64,768]{2,1,0:T(8,128)(2,1)S(1)} %slice_convert_fusion.2), channel_id=1, source_target_pairs={{0,16},{1,17},{2,18},{3,19},{4,20},{5,21},{6,22},{7,23},{8,9},{9,8... | collective-permute-start | bytes 2359304 | tf_op jit(solution)/shard_map/ppermute | solution.py:240
  50.3 9.9 %collective-permute-start.15 = (f16[4,64,768]{2,1,0:T(8,128)(2,1)S(1)}, f16[4,64,768]{2,1,0:T(8,128)(2,1)S(1)}, u32[]{:S(2)}, u32[]{:S(2)}) collective-permute-start(f16[4,64,768]{2,1,0:T(8,128)(2,1)S(1)} %slice_convert_fusion.5), channel_id=1, source_target_pairs={{0,1},{1,0},{2,3},{3,2},{4,5},{5,4},{6,7},{7,6},{8,10},{9,11},{10,... | collective-permute-start | bytes 1179656 | tf_op jit(solution)/shard_map/ppermute | solution.py:240
  57.8 12.1 %collective-permute-start.14 = (f16[4,64,768]{2,1,0:T(8,128)(2,1)S(1)}, f16[4,64,768]{2,1,0:T(8,128)(2,1)S(1)}, u32[]{:S(2)}, u32[]{:S(2)}) collective-permute-start(f16[4,64,768]{2,1,0:T(8,128)(2,1)S(1)} %slice_convert_fusion.4), channel_id=1, source_target_pairs={{0,16},{1,17},{2,18},{3,19},{4,20},{5,21},{6,22},{7,23},{8,24},{9,... | collective-permute-start | bytes 1179656 | tf_op jit(solution)/shard_map/ppermute | solution.py:240
  58.4 11.7 %collective-permute-start.13 = (f16[4,64,768]{2,1,0:T(8,128)(2,1)S(1)}, f16[4,64,768]{2,1,0:T(8,128)(2,1)S(1)}, u32[]{:S(2)}, u32[]{:S(2)}) collective-permute-start(f16[4,64,768]{2,1,0:T(8,128)(2,1)S(1)} %slice_convert_fusion.3), channel_id=1, source_target_pairs={{0,1},{1,0},{2,3},{3,2},{4,5},{5,4},{6,7},{7,6},{8,10},{9,11},{10,... | collective-permute-start | bytes 1179656 | tf_op jit(solution)/shard_map/ppermute | solution.py:240
  60.3 11.6 %collective-permute-start.18 = (f16[2,64,768]{2,1,0:T(8,128)(2,1)S(1)}, f16[2,64,768]{2,1,0:T(8,128)(2,1)S(1)}, u32[]{:S(2)}, u32[]{:S(2)}) collective-permute-start(f16[2,64,768]{2,1,0:T(8,128)(2,1)S(1)} %slice_convert_fusion.8), channel_id=1, source_target_pairs={{0,2},{1,3},{2,0},{3,1},{4,6},{5,7},{6,4},{7,5},{8,24},{9,25},{10,... | collective-permute-start | bytes 589832 | tf_op jit(solution)/shard_map/ppermute | solution.py:240
  70.1 5.7 %collective-permute-start.17 = (f16[2,64,768]{2,1,0:T(8,128)(2,1)S(1)}, f16[2,64,768]{2,1,0:T(8,128)(2,1)S(1)}, u32[]{:S(2)}, u32[]{:S(2)}) collective-permute-start(f16[2,64,768]{2,1,0:T(8,128)(2,1)S(1)} %slice_convert_fusion.7), channel_id=1, source_target_pairs={{0,1},{1,0},{2,3},{3,2},{4,5},{5,4},{6,7},{7,6},{8,9},{9,8},{10,11... | collective-permute-start | bytes 589832 | tf_op jit(solution)/shard_map/ppermute | solution.py:240
  70.3 8.2 %collective-permute-start.16 = (f16[2,64,768]{2,1,0:T(8,128)(2,1)S(1)}, f16[2,64,768]{2,1,0:T(8,128)(2,1)S(1)}, u32[]{:S(2)}, u32[]{:S(2)}) collective-permute-start(f16[2,64,768]{2,1,0:T(8,128)(2,1)S(1)} %slice_convert_fusion.6), channel_id=1, source_target_pairs={{0,2},{1,3},{2,0},{3,1},{4,6},{5,7},{6,4},{7,5},{8,24},{9,25},{10,... | collective-permute-start | bytes 589832 | tf_op jit(solution)/shard_map/ppermute | solution.py:240
  72.0 14.6 %collective-permute-start.20 = (f16[1,64,768]{2,1,0:T(8,128)(2,1)S(1)}, f16[1,64,768]{2,1,0:T(8,128)(2,1)S(1)}, u32[]{:S(2)}, u32[]{:S(2)}) collective-permute-start(f16[1,64,768]{2,1,0:T(8,128)(2,1)S(1)} %slice_convert_fusion.11), channel_id=1, source_target_pairs={{0,4},{1,5},{2,6},{3,7},{4,0},{5,1},{6,2},{7,3},{8,12},{9,13},{10,... | collective-permute-start | bytes 294920 | tf_op jit(solution)/shard_map/ppermute | solution.py:22
  78.7 8.5 %collective-permute-start.19 = (f16[1,64,1536]{2,1,0:T(8,128)(2,1)S(1)}, f16[1,64,1536]{2,1,0:T(8,128)(2,1)S(1)}, u32[]{:S(2)}, u32[]{:S(2)}) collective-permute-start(f16[1,64,1536]{2,1,0:T(8,128)(2,1)S(1)} %pad_maximum_fusion.3), channel_id=1, source_target_pairs={{0,4},{1,5},{2,6},{3,7},{4,0},{5,1},{6,2},{7,3},{8,12},{9,13},{10,... | collective-permute-start | bytes 589832 | tf_op jit(solution)/shard_map/ppermute | solution.py:22

commit v7 on v6

--- a/solution.py
+++ b/solution.py
@@ -163,16 +163,19 @@
 
 
 def input_grad_kernel(columns, cuts, scale_ref, *refs):
-    pieces = refs[: sum(cuts)]
+    pieces = refs[: sum(cuts) or 1]
     weight_ref = refs[len(pieces)]
-    out_ref, wide_ref, taps_ref, shifted_ref = refs[-4:]
+    wide_ref, taps_ref = refs[-2:]
+    out_ref, shifted_ref = refs[-4:-2] if cuts else (refs[-3], pieces[0])
     step = out_ref.shape[1]
     width = weight_ref.shape[1]
     halves = width // 128
 
-    @pl.when(pl.program_id(0) == 0)
-    def _():
-        shift_rows(columns, cuts, pieces, shifted_ref)
+    if cuts:
+
+        @pl.when(pl.program_id(0) == 0)
+        def _():
+            shift_rows(columns, cuts, pieces, shifted_ref)
 
     for h in range(halves):
         wide_ref[h] = weight_ref[:, h * 128 : (h + 1) * 128].astype(F32)
@@ -187,38 +190,52 @@
 
 
 def input_grad(columns, scale, rows_of, weight, first, count, before=None):
-    pieces = [flat(piece) for row in rows_of for piece in row]
-    cuts = tuple(len(row) for row in rows_of)
-    pixels = sum(piece.shape[0] for piece in pieces) // 3
+    reuse = before is not None
+    pieces = [rows_of] if reuse else [flat(piece) for row in rows_of for piece in row]
+    cuts = () if reuse else tuple(len(row) for row in rows_of)
+    pixels = pieces[0].shape[0] if reuse else sum(piece.shape[0] for piece in pieces) // 3
     rows, width = weight.shape
     channels = rows // 9
     step = CHANNELS_PER_STEP
-    earlier = [] if before is None else [before]
-    return pl.pallas_call(
+    results = [
+        (
+            pl.BlockSpec((pixels, step), lambda i: (0, i + first)),
+            jax.ShapeDtypeStruct((pixels, channels), BF16),
+        )
+    ]
+    if not reuse:
+        shape = (pixels, 9 * width)
+        results.append((pl.BlockSpec(shape, lambda i: (0, 0)), jax.ShapeDtypeStruct(shape, BF16)))
+    parts = pl.pallas_call(
         functools.partial(input_grad_kernel, columns, cuts),
         grid=(count,),
         in_specs=[
             pl.BlockSpec(memory_space=pltpu.SMEM),
             *[pl.BlockSpec(piece.shape, lambda i: (0, 0)) for piece in pieces],
             pl.BlockSpec((9 * step, width), lambda i: (i + first, 0)),
-            *[pl.BlockSpec(memory_space=pl.ANY) for _ in earlier],
+            *[pl.BlockSpec(memory_space=pl.ANY) for _ in range(reuse)],
         ],
-        out_specs=pl.BlockSpec((pixels, step), lambda i: (0, i + first)),
-        out_shape=jax.ShapeDtypeStruct((pixels, channels), BF16),
-        input_output_aliases={len(pieces) + 2: 0} if earlier else {},
+        out_specs=[spec for spec, _ in results],
+        out_shape=[kind for _, kind in results],
+        input_output_aliases={len(pieces) + 2: 0} if reuse else {},
         scratch_shapes=[
             pltpu.VMEM((width // 128, 9 * step, 128), F32),
             pltpu.VMEM((step, 9 * width), BF16),
-            pltpu.VMEM((pixels, 9 * width), BF16),
         ],
-        compiler_params=pltpu.CompilerParams(vmem_limit_bytes=18 << 20),
+        compiler_params=pltpu.CompilerParams(vmem_limit_bytes=26 << 20),
         cost_estimate=pl.CostEstimate(
             flops=2 * pixels * 9 * width * step * count,
             bytes_accessed=2 * (9 * step * width + pixels * step) * count,
             transcendentals=0,
         ),
         name="input_grad",
-    )(scale, *pieces, pltpu.with_memory_space_constraint(weight, pltpu.HBM), *earlier)
+    )(
+        scale,
+        *pieces,
+        pltpu.with_memory_space_constraint(weight, pltpu.HBM),
+        *([before] if reuse else []),
+    )
+    return (parts[0], rows_of) if reuse else tuple(parts)
 
 
 def bits_of(axis):
@@ -284,16 +301,18 @@
     image, *centre = term(
         in_hbm(image), [[in_hbm(flat(tile))]], [(width, [centre_order] * 2)], False
     )
-    alive_all = [own_alive.reshape(1)]
-    for away in range(1, member_count):
-        alive_all.append(exchange(alive_all[0], "dp", away))
-    near, far, centre, alive_all = lax.optimization_barrier((near, far, centre, alive_all))
+    pair = own_alive.reshape(1)
+    pair = pair + exchange(pair, *core)
+    near, far, centre, pair = lax.optimization_barrier((near, far, centre, pair))
+    alive_all = [pair]
+    for away in range(2, member_count, 2):
+        alive_all.append(exchange(pair, "dp", away))
 
     first_rows = either(near[0], far[0]), either(far[0], near[0])
     other = exchange(jnp.stack([near[1], far[1]]), *core)
     back = exchange(centre[0], *core)
     first = term(image, [after(first_rows, centre)], [(width, orders)])
-    first, other, back = lax.optimization_barrier((first, other, back))
+    first, other, back, alive_all = lax.optimization_barrier((first, other, back, alive_all))
     second_rows = either(other[1], other[0]), either(other[0], other[1])
     centre = add(centre[1], back)
     back = exchange(first[0], *core)
@@ -306,13 +325,13 @@
     ring[0] = add(first[1], back)
 
     blocks = in_channels // CHANNELS_PER_STEP
-    cuts = [0, blocks * 3 // 8, blocks * 5 // 8, blocks]
+    cuts = [0, blocks * 2 // 8, blocks * 5 // 8, blocks]
     last = len(centre_order) - 1
     rows_of = [below, [in_hbm(flat(tile))], above]
     chains = [[ring[1], orders, None], [centre, (centre_order, centre_order), None], [ring[0], orders, None]]
     grad_features = token = None
 
-    def next_columns(turn, *operands):
+    def next_columns(turn, rows_of, *operands):
         return input_grad(
             columns,
             scale,
@@ -333,11 +352,13 @@
             operands.append(token)
             chain[0], chain[2] = part, exchange_by_role(token, order, step)
             if step == last - 1 and chain is chains[0]:
-                token = grad_features = next_columns(1, token)
+                grad_features, rows_of = next_columns(1, rows_of, token)
+                token = grad_features
         if step == 0:
             survivors = sum(after(alive_all, *operands))
             scale = own_alive / survivors
-            token = grad_features = next_columns(0, *operands)
+            grad_features, rows_of = next_columns(0, rows_of, *operands)
+            token = grad_features
     parts = []
     for part, order, back in chains:
         parts.append(add(kept(part), after(back, token)))
@@ -346,7 +367,7 @@
             ahead = exchange(token, *centre_order[last])
     operands = jnp.concatenate([sent(part) for part in parts[1:]], axis=-1)
     back = exchange(operands, *centre_order[last])
-    grad_features = next_columns(2, operands)
+    grad_features, _ = next_columns(2, rows_of, operands)
     back, ahead, grad_features = lax.optimization_barrier((back, ahead, grad_features))
     second, centre, first = (
         add(kept(part), value)[0]

time: 88.4 us -> 88.1 us (level)
  waiting for transfers between devices: 13.7 us -> 15.8 us
  Pallas kernels: 36.1 us -> 34.1 us
    pallas_call x3, Pallas kernels: 21.4 us -> 19.4 us  [input_grad(): pl.pallas_call(functools.partial(input_grad_kernel, columns, cuts), grid=...]
    ppermute x10 -> x9, waiting for transfers between devices: 1.09 us -> 2.72 us  [exchange(): lax.ppermute(value, axis, [(i, i ^ bit) for i in range(lax.axis_size(axis...]
    ppermute x10 -> x9, starting transfers between devices: 14 us -> 13.4 us  [exchange(): lax.ppermute(value, axis, [(i, i ^ bit) for i in range(lax.axis_size(axis...]
  transfers between devices with their start and end apart: 21 -> 20, of which waited for: 6 -> 9; matrix products, arithmetic and copies ran while one was open for 7% -> 7% of each run, Pallas kernels for 41% -> 39%
where the time goes in v7:
time: 88.1 us; the launch traced here: 87.8 us
  Pallas kernels  34.1 us (39%)
  starting transfers between devices  27.8 us (32%)
  waiting for transfers between devices  15.8 us (18%)
  other arithmetic  6.05 us (7%)
  between operations  3.11 us (4%)
  local copies, waits for them, and re-layouts  0.89 us (1%)
    pallas_call x3, Pallas kernels, input_grad(): pl.pallas_call(functools.partial(input_grad_kernel, columns, cuts), grid=...  19.4 us
    pallas_call x3, Pallas kernels, kernel_term(): pl.pallas_call(functools.partial(kernel_term_kernel, columns, cuts, strea...  14.6 us
    ppermute x9, starting transfers between devices, exchange(): lax.ppermute(value, axis, [(i, i ^ bit) for i in range(lax.axis_size(axis...  13.4 us
    ppermute x9, waiting for transfers between devices, exchange_by_role(): return lax.ppermute(value, ('dp', 'space'), pairs)  12.4 us
    ppermute x9, starting transfers between devices, exchange_by_role(): return lax.ppermute(value, ('dp', 'space'), pairs)  11.9 us
    ppermute x9, waiting for transfers between devices, exchange(): lax.ppermute(value, axis, [(i, i ^ bit) for i in range(lax.axis_size(axis...  2.72 us
    ppermute x2, starting transfers between devices, fetched(): return lax.ppermute(value, ('dp', 'space'), pairs)  2.58 us
    add x12, other arithmetic, add(): return part.astype(F32) + back.astype(F32)  2.29 us
  transfers between devices with their start and end apart: 20, of which 9 were waited for; matrix products, arithmetic and copies ran while one was open for 7% of the time, Pallas kernels for 39%

profile of v7, /device:TPU:0, one launch (start us, length us, event | category | flops | bytes accessed | tf_op | source)
XLA Modules:
  0.0 87.8 jit_solution(16631425884408455258)
XLA Ops:
  1.1 1.1 %broadcast_select_fusion.4 = (bf16[1,6,72,256]{3,2,1,0:T(8,128)(2,1)S(1)}, bf16[1,6,72,256]{3,2,1,0:T(8,128)(2,1)S(1)}) fusion(pred[]{:T(512)S(6)} %eq.31, bf16[1,12,72,256]{3,2,1,0:T(8,128)(2,1)} %param.5), kind=kLoop, calls=%fused_computation.35 | loop fusion | flops 221184 | bytes 884737 | tf_op jit(solution)/shard_map/jit(_where)/select_n | solution.py:26
  2.9 1.3 %collective-permute-start.1 = (bf16[2,6,72,256]{3,2,1,0:T(8,128)(2,1)S(1)}, bf16[2,6,72,256]{3,2,1,0:T(8,128)(2,1)S(1)}, u32[]{:S(2)}, u32[]{:S(2)}) collective-permute-start(bf16[2,6,72,256]{3,2,1,0:T(8,128)(2,1)S(1)} %pad_maximum_fusion), channel_id=1, source_target_pairs={{1,0},{2,1},{3,2},{4,3},{5,4},{6,5},{7,6},{8,9},{9,10},{10,11},{11... | collective-permute-start | bytes 1327112 | tf_op jit(solution)/shard_map/ppermute | solution.py:41
  4.2 1.3 %collective-permute-start.2 = (bf16[2,6,72,256]{3,2,1,0:T(8,128)(2,1)S(1)}, bf16[2,6,72,256]{3,2,1,0:T(8,128)(2,1)S(1)}, u32[]{:S(2)}, u32[]{:S(2)}) collective-permute-start(bf16[2,6,72,256]{3,2,1,0:T(8,128)(2,1)S(1)} %pad_maximum_fusion.1), channel_id=1, source_target_pairs={{2,0},{3,1},{4,2},{5,3},{6,4},{7,5},{8,10},{9,11},{10,12},{11,13},... | collective-permute-start | bytes 1327112 | tf_op jit(solution)/shard_map/ppermute | solution.py:41
  6.2 6.2 %collective-permute-start.3 = (f32[1]{0:T(128)}, f32[1]{0:T(128)}, u32[]{:S(2)}, u32[]{:S(2)}) collective-permute-start(f32[1]{0:T(128)} %convert_element_type.89.scale_ref), channel_id=1, source_target_pairs={{0,8},{8,0},{16,24},{24,16},{1,9},{9,1},{17,25},{25,17},{2,10},{10... | collective-permute-start | bytes 20 | tf_op jit(solution)/shard_map/ppermute | solution.py:22
  12.4 5.9 %kernel_term.3 = (bf16[2,2,512,864]{3,2,1,0:T(8,128)(2,1)S(1)}, f32[16,64,768]{2,1,0:T(8,128)S(1)}, f32[16,64,768]{2,1,0:T(8,128)S(1)}) custom-call(s32[2]{0:T(128)S(1)} %pad_add_fusion.place_ref, f32[1]{0:T(128)} %convert_element_type.89.scale_ref, bf16[864,2048]{1,0:T(8,128)(2,1)} %bitcast.47, bf16[864,2048]{1,0:T(8,128)(2,1)} %bitcast.48, ...), custom_call_target="tpu_custom_call" | custom-call | flops 2717908992 | bytes 9830400 | tf_op jit(solution)/shard_map/kernel_term/pallas_call | solution.py:139
  20.9 2.8 %collective-permute-start.6 = (f32[1]{0:T(128)}, f32[1]{0:T(128)}, u32[]{:S(2)}, u32[]{:S(2)}) collective-permute-start(f32[1]{0:T(128)} %add.69), channel_id=1, source_target_pairs={{0,16},{8,24},{16,0},{24,8},{1,17},{9,25},{17,1},{25,9},{2,18},{10... | collective-permute-start | bytes 20 | tf_op jit(solution)/shard_map/ppermute | solution.py:22
  23.7 4.3 %kernel_term.4 = (f32[16,64,768]{2,1,0:T(8,128)S(1)}, f32[16,64,768]{2,1,0:T(8,128)S(1)}) custom-call(s32[2]{0:T(128)S(1)} %pad_add_fusion.place_ref, f32[1]{0:T(128)} %convert_element_type.89.scale_ref, bf16[2,2,512,864]{3,2,1,0:T(8,128)(2,1)S(1)} %get-tuple-element.55.refs_0_, bf16[432,256]{1,0:T(8,128)(2,1)S(1)} %bitcast.36, bf16[432,256]{1,0:T(8,128)(2,1)S(1)} %bitcast.35), custom_call_target="tpu_custom_call" | custom-call | flops 2717908992 | bytes 9830400 | tf_op jit(solution)/shard_map/kernel_term/pallas_call | solution.py:139
  29.1 4.5 %kernel_term.5 = (f32[16,64,768]{2,1,0:T(8,128)S(1)}, f32[16,64,768]{2,1,0:T(8,128)S(1)}) custom-call(s32[2]{0:T(128)S(1)} %pad_add_fusion.place_ref, f32[1]{0:T(128)} %convert_element_type.89.scale_ref, bf16[2,2,512,864]{3,2,1,0:T(8,128)(2,1)S(1)} %get-tuple-element.55.refs_0_, bf16[432,256]{1,0:T(8,128)(2,1)S(1)} %bitcast.38, bf16[432,256]{1,0:T(8,128)(2,1)S(1)} %bitcast.37), custom_call_target="tpu_custom_call" | custom-call | flops 2717908992 | bytes 9830400 | tf_op jit(solution)/shard_map/kernel_term/pallas_call | solution.py:139
  36.0 1.6 %collective-permute-start.10 = (f16[8,64,768]{2,1,0:T(8,128)(2,1)S(1)}, f16[8,64,768]{2,1,0:T(8,128)(2,1)S(1)}, u32[]{:S(2)}, u32[]{:S(2)}) collective-permute-start(f16[8,64,768]{2,1,0:T(8,128)(2,1)S(1)} %get-tuple-element.128), channel_id=1, source_target_pairs={{0,2},{1,3},{2,0},{3,1},{4,6},{5,7},{6,4},{7,5},{8,10},{9,11},{10,... | collective-permute-start | bytes 2359304 | tf_op jit(solution)/shard_map/ppermute | solution.py:257
  38.3 1.4 %collective-permute-start.9 = (f16[8,64,768]{2,1,0:T(8,128)(2,1)S(1)}, f16[8,64,768]{2,1,0:T(8,128)(2,1)S(1)}, u32[]{:S(2)}, u32[]{:S(2)}) collective-permute-start(f16[8,64,768]{2,1,0:T(8,128)(2,1)S(1)} %slice_convert_fusion.2), channel_id=1, source_target_pairs={{0,16},{1,17},{2,18},{3,19},{4,20},{5,21},{6,22},{7,23},{8,9},{9,8... | collective-permute-start | bytes 2359304 | tf_op jit(solution)/shard_map/ppermute | solution.py:257
  40.5 6.2 %input_grad.3 = (bf16[864,2048]{1,0:T(8,128)(2,1)}, bf16[864,2304]{1,0:T(8,128)(2,1)S(1)}) custom-call(f32[1]{0:T(128)S(6)} %div.7.scale_ref, bf16[432,256]{1,0:T(8,128)(2,1)S(1)} %bitcast.42, bf16[432,256]{1,0:T(8,128)(2,1)S(1)} %bitcast.41, bf16[864,256]{1,0:T(8,128)(2,1)} %bitcast.46, bf16[432,256]{1,0:T(8,128)(2,1)S(1)} %bitcast.40, ...), custom_call_target="tpu_custom_call" | custom-call | flops 2038431744 | bytes 3244032 | tf_op jit(solution)/shard_map/input_grad/pallas_call | solution.py:209
  48.8 7.6 %collective-permute-done.10 = f16[8,64,768]{2,1,0:T(8,128)(2,1)S(1)} collective-permute-done((f16[8,64,768]{2,1,0:T(8,128)(2,1)S(1)}, f16[8,64,768]{2,1,0:T(8,128)(2,1)S(1)}, u32[]{:S(2)}, u32[]{:S(2)}) %collective-permute-start.10) | collective-permute-done | bytes 786464 | tf_op jit(solution)/shard_map/ppermute | solution.py:257
  56.7 1.7 %collective-permute-start.13 = (f16[4,64,768]{2,1,0:T(8,128)(2,1)S(1)}, f16[4,64,768]{2,1,0:T(8,128)(2,1)S(1)}, u32[]{:S(2)}, u32[]{:S(2)}) collective-permute-start(f16[4,64,768]{2,1,0:T(8,128)(2,1)S(1)} %slice_convert_fusion.4), channel_id=1, source_target_pairs={{0,16},{1,17},{2,18},{3,19},{4,20},{5,21},{6,22},{7,23},{8,24},{9,... | collective-permute-start | bytes 1179656 | tf_op jit(solution)/shard_map/ppermute | solution.py:257
  58.6 1.0 %collective-permute-start.12 = (f16[4,64,768]{2,1,0:T(8,128)(2,1)S(1)}, f16[4,64,768]{2,1,0:T(8,128)(2,1)S(1)}, u32[]{:S(2)}, u32[]{:S(2)}) collective-permute-start(f16[4,64,768]{2,1,0:T(8,128)(2,1)S(1)} %slice_convert_fusion.3), channel_id=1, source_target_pairs={{0,1},{1,0},{2,3},{3,2},{4,5},{5,4},{6,7},{7,6},{8,10},{9,11},{10,... | collective-permute-start | bytes 1179656 | tf_op jit(solution)/shard_map/ppermute | solution.py:257
  59.7 1.6 %collective-permute-start.17 = (f16[2,64,768]{2,1,0:T(8,128)(2,1)S(1)}, f16[2,64,768]{2,1,0:T(8,128)(2,1)S(1)}, u32[]{:S(2)}, u32[]{:S(2)}) collective-permute-start(f16[2,64,768]{2,1,0:T(8,128)(2,1)S(1)} %slice_convert_fusion.8), channel_id=1, source_target_pairs={{0,2},{1,3},{2,0},{3,1},{4,6},{5,7},{6,4},{7,5},{8,24},{9,25},{10,... | collective-permute-start | bytes 589832 | tf_op jit(solution)/shard_map/ppermute | solution.py:257
  61.4 6.6 %input_grad.4.refs_2_ = bf16[864,2048]{1,0:T(8,128)(2,1)} custom-call(f32[1]{0:T(128)S(6)} %div.7.scale_ref, bf16[864,2304]{1,0:T(8,128)(2,1)S(1)} %get-tuple-element.104.refs_0_, bf16[18432,256]{1,0:T(8,128)(2,1)} %refs_1_.3, bf16[864,2048]{1,0:T(8,128)(2,1)} %get-tuple-element.92.refs_2_), custom_call_target="tpu_custom_call", output_to_operand_aliasing={{}: (3, {})} | custom-call | flops 3057647616 | bytes 4866048 | tf_op jit(solution)/shard_map/input_grad/pallas_call | solution.py:209
  68.5 1.3 %collective-permute-start.16 = (f16[2,64,768]{2,1,0:T(8,128)(2,1)S(1)}, f16[2,64,768]{2,1,0:T(8,128)(2,1)S(1)}, u32[]{:S(2)}, u32[]{:S(2)}) collective-permute-start(f16[2,64,768]{2,1,0:T(8,128)(2,1)S(1)} %slice_convert_fusion.7), channel_id=1, source_target_pairs={{0,1},{1,0},{2,3},{3,2},{4,5},{5,4},{6,7},{7,6},{8,9},{9,8},{10,11... | collective-permute-start | bytes 589832 | tf_op jit(solution)/shard_map/ppermute | solution.py:257
  69.9 1.7 %collective-permute-start.15 = (f16[2,64,768]{2,1,0:T(8,128)(2,1)S(1)}, f16[2,64,768]{2,1,0:T(8,128)(2,1)S(1)}, u32[]{:S(2)}, u32[]{:S(2)}) collective-permute-start(f16[2,64,768]{2,1,0:T(8,128)(2,1)S(1)} %slice_convert_fusion.6), channel_id=1, source_target_pairs={{0,2},{1,3},{2,0},{3,1},{4,6},{5,7},{6,4},{7,5},{8,24},{9,25},{10,... | collective-permute-start | bytes 589832 | tf_op jit(solution)/shard_map/ppermute | solution.py:257
  71.7 1.0 %collective-permute-start.19 = (f16[1,64,768]{2,1,0:T(8,128)(2,1)S(1)}, f16[1,64,768]{2,1,0:T(8,128)(2,1)S(1)}, u32[]{:S(2)}, u32[]{:S(2)}) collective-permute-start(f16[1,64,768]{2,1,0:T(8,128)(2,1)S(1)} %slice_convert_fusion.11), channel_id=1, source_target_pairs={{0,4},{1,5},{2,6},{3,7},{4,0},{5,1},{6,2},{7,3},{8,12},{9,13},{10,... | collective-permute-start | bytes 294920 | tf_op jit(solution)/shard_map/ppermute | solution.py:22
  72.7 1.6 %collective-permute-done.16 = f16[2,64,768]{2,1,0:T(8,128)(2,1)S(1)} collective-permute-done((f16[2,64,768]{2,1,0:T(8,128)(2,1)S(1)}, f16[2,64,768]{2,1,0:T(8,128)(2,1)S(1)}, u32[]{:S(2)}, u32[]{:S(2)}) %collective-permute-start.16) | collective-permute-done | bytes 196640 | tf_op jit(solution)/shard_map/ppermute | solution.py:257
  74.4 1.9 %collective-permute-done.15 = f16[2,64,768]{2,1,0:T(8,128)(2,1)S(1)} collective-permute-done((f16[2,64,768]{2,1,0:T(8,128)(2,1)S(1)}, f16[2,64,768]{2,1,0:T(8,128)(2,1)S(1)}, u32[]{:S(2)}, u32[]{:S(2)}) %collective-permute-start.15) | collective-permute-done | bytes 196640 | tf_op jit(solution)/shard_map/ppermute | solution.py:257
  76.4 1.7 %collective-permute-start.18 = (f16[1,64,1536]{2,1,0:T(8,128)(2,1)S(1)}, f16[1,64,1536]{2,1,0:T(8,128)(2,1)S(1)}, u32[]{:S(2)}, u32[]{:S(2)}) collective-permute-start(f16[1,64,1536]{2,1,0:T(8,128)(2,1)S(1)} %pad_maximum_fusion.3), channel_id=1, source_target_pairs={{0,4},{1,5},{2,6},{3,7},{4,0},{5,1},{6,2},{7,3},{8,12},{9,13},{10,... | collective-permute-start | bytes 589832 | tf_op jit(solution)/shard_map/ppermute | solution.py:22
  78.1 6.6 %input_grad.5 = bf16[864,2048]{1,0:T(8,128)(2,1)} custom-call(f32[1]{0:T(128)S(6)} %div.7.scale_ref, bf16[864,2304]{1,0:T(8,128)(2,1)S(1)} %get-tuple-element.104.refs_0_, bf16[18432,256]{1,0:T(8,128)(2,1)} %refs_1_.3, bf16[864,2048]{1,0:T(8,128)(2,1)} %input_grad.4.refs_2_), custom_call_target="tpu_custom_call", output_to_operand_aliasing={{}: (3, {})} | custom-call | flops 3057647616 | bytes 4866048 | tf_op jit(solution)/shard_map/input_grad/pallas_call | solution.py:209
  84.7 2.0 %collective-permute-done.18 = f16[1,64,1536]{2,1,0:T(8,128)(2,1)S(1)} collective-permute-done((f16[1,64,1536]{2,1,0:T(8,128)(2,1)S(1)}, f16[1,64,1536]{2,1,0:T(8,128)(2,1)S(1)}, u32[]{:S(2)}, u32[]{:S(2)}) %collective-permute-start.18) | collective-permute-done | bytes 196640 | tf_op jit(solution)/shard_map/ppermute | solution.py:22
  (64 shorter events, 11.8 us)
Async XLA Ops:
  0.6 2.1 %collective-permute-start = (bf16[12,72,256]{2,1,0:T(8,128)(2,1)}, bf16[12,72,256]{2,1,0:T(8,128)(2,1)S(1)}, u32[]{:S(2)}, u32[]{:S(2)}) collective-permute-start(bf16[12,72,256]{2,1,0:T(8,128)(2,1)} %bitcast.44), channel_id=1, source_target_pairs={{0,8},{8,0},{16,24},{24,16},{1,9},{9,1},{17,25},{25,17},{2,10},{10... | collective-permute-start | bytes 1327112 | tf_op jit(solution)/shard_map/ppermute | solution.py:22
  2.9 16.6 %collective-permute-start.1 = (bf16[2,6,72,256]{3,2,1,0:T(8,128)(2,1)S(1)}, bf16[2,6,72,256]{3,2,1,0:T(8,128)(2,1)S(1)}, u32[]{:S(2)}, u32[]{:S(2)}) collective-permute-start(bf16[2,6,72,256]{3,2,1,0:T(8,128)(2,1)S(1)} %pad_maximum_fusion), channel_id=1, source_target_pairs={{1,0},{2,1},{3,2},{4,3},{5,4},{6,5},{7,6},{8,9},{9,10},{10,11},{11... | collective-permute-start | bytes 1327112 | tf_op jit(solution)/shard_map/ppermute | solution.py:41
  4.2 16.0 %collective-permute-start.2 = (bf16[2,6,72,256]{3,2,1,0:T(8,128)(2,1)S(1)}, bf16[2,6,72,256]{3,2,1,0:T(8,128)(2,1)S(1)}, u32[]{:S(2)}, u32[]{:S(2)}) collective-permute-start(bf16[2,6,72,256]{3,2,1,0:T(8,128)(2,1)S(1)} %pad_maximum_fusion.1), channel_id=1, source_target_pairs={{2,0},{3,1},{4,2},{5,3},{6,4},{7,5},{8,10},{9,11},{10,12},{11,13},... | collective-permute-start | bytes 1327112 | tf_op jit(solution)/shard_map/ppermute | solution.py:41
  6.2 12.6 %collective-permute-start.3 = (f32[1]{0:T(128)}, f32[1]{0:T(128)}, u32[]{:S(2)}, u32[]{:S(2)}) collective-permute-start(f32[1]{0:T(128)} %convert_element_type.89.scale_ref), channel_id=1, source_target_pairs={{0,8},{8,0},{16,24},{24,16},{1,9},{9,1},{17,25},{25,17},{2,10},{10... | collective-permute-start | bytes 20 | tf_op jit(solution)/shard_map/ppermute | solution.py:22
  20.2 8.3 %collective-permute-start.5 = (f16[16,64,768]{2,1,0:T(8,128)(2,1)S(1)}, f16[16,64,768]{2,1,0:T(8,128)(2,1)S(1)}, u32[]{:S(2)}, u32[]{:S(2)}) collective-permute-start(f16[16,64,768]{2,1,0:T(8,128)(2,1)S(1)} %convert_element_type.90), channel_id=1, source_target_pairs={{0,8},{8,0},{16,24},{24,16},{1,9},{9,1},{17,25},{25,17},{2,10},{10... | collective-permute-start | bytes 4718600 | tf_op jit(solution)/shard_map/ppermute | solution.py:22
  20.3 8.2 %collective-permute-start.4 = (bf16[2,6,72,256]{3,2,1,0:T(8,128)(2,1)S(1)}, bf16[2,6,72,256]{3,2,1,0:T(8,128)(2,1)S(1)}, u32[]{:S(2)}, u32[]{:S(2)}) collective-permute-start(bf16[2,6,72,256]{3,2,1,0:T(8,128)(2,1)S(1)} %pad_maximum_fusion.2), channel_id=1, source_target_pairs={{0,8},{8,0},{16,24},{24,16},{1,9},{9,1},{17,25},{25,17},{2,10},{10... | collective-permute-start | bytes 1327112 | tf_op jit(solution)/shard_map/ppermute | solution.py:22
  20.9 7.6 %collective-permute-start.6 = (f32[1]{0:T(128)}, f32[1]{0:T(128)}, u32[]{:S(2)}, u32[]{:S(2)}) collective-permute-start(f32[1]{0:T(128)} %add.69), channel_id=1, source_target_pairs={{0,16},{8,24},{16,0},{24,8},{1,17},{9,25},{17,1},{25,9},{2,18},{10... | collective-permute-start | bytes 20 | tf_op jit(solution)/shard_map/ppermute | solution.py:22
  28.5 5.6 %collective-permute-start.7 = (f16[16,64,768]{2,1,0:T(8,128)(2,1)S(1)}, f16[16,64,768]{2,1,0:T(8,128)(2,1)S(1)}, u32[]{:S(2)}, u32[]{:S(2)}) collective-permute-start(f16[16,64,768]{2,1,0:T(8,128)(2,1)S(1)} %convert_element_type.92), channel_id=1, source_target_pairs={{0,8},{8,0},{16,24},{24,16},{1,9},{9,1},{17,25},{25,17},{2,10},{10... | collective-permute-start | bytes 4718600 | tf_op jit(solution)/shard_map/ppermute | solution.py:22
  34.1 3.6 %collective-permute-start.8 = (f16[16,64,768]{2,1,0:T(8,128)(2,1)S(1)}, f16[16,64,768]{2,1,0:T(8,128)(2,1)S(1)}, u32[]{:S(2)}, u32[]{:S(2)}) collective-permute-start(f16[16,64,768]{2,1,0:T(8,128)(2,1)S(1)} %convert_element_type.97), channel_id=1, source_target_pairs={{0,8},{8,0},{16,24},{24,16},{1,9},{9,1},{17,25},{25,17},{2,10},{10... | collective-permute-start | bytes 4718600 | tf_op jit(solution)/shard_map/ppermute | solution.py:22
  35.4 12.1 %collective-permute-start.11 = (f16[8,64,768]{2,1,0:T(8,128)(2,1)S(1)}, f16[8,64,768]{2,1,0:T(8,128)(2,1)S(1)}, u32[]{:S(2)}, u32[]{:S(2)}) collective-permute-start(f16[8,64,768]{2,1,0:T(8,128)(2,1)S(1)} %get-tuple-element.127), channel_id=1, source_target_pairs={{0,16},{1,17},{2,18},{3,19},{4,20},{5,21},{6,22},{7,23},{8,9},{9,8... | collective-permute-start | bytes 2359304 | tf_op jit(solution)/shard_map/ppermute | solution.py:257
  36.0 20.4 %collective-permute-start.10 = (f16[8,64,768]{2,1,0:T(8,128)(2,1)S(1)}, f16[8,64,768]{2,1,0:T(8,128)(2,1)S(1)}, u32[]{:S(2)}, u32[]{:S(2)}) collective-permute-start(f16[8,64,768]{2,1,0:T(8,128)(2,1)S(1)} %get-tuple-element.128), channel_id=1, source_target_pairs={{0,2},{1,3},{2,0},{3,1},{4,6},{5,7},{6,4},{7,5},{8,10},{9,11},{10,... | collective-permute-start | bytes 2359304 | tf_op jit(solution)/shard_map/ppermute | solution.py:257
  38.3 20.1 %collective-permute-start.9 = (f16[8,64,768]{2,1,0:T(8,128)(2,1)S(1)}, f16[8,64,768]{2,1,0:T(8,128)(2,1)S(1)}, u32[]{:S(2)}, u32[]{:S(2)}) collective-permute-start(f16[8,64,768]{2,1,0:T(8,128)(2,1)S(1)} %slice_convert_fusion.2), channel_id=1, source_target_pairs={{0,16},{1,17},{2,18},{3,19},{4,20},{5,21},{6,22},{7,23},{8,9},{9,8... | collective-permute-start | bytes 2359304 | tf_op jit(solution)/shard_map/ppermute | solution.py:257
  47.8 11.8 %collective-permute-start.14 = (f16[4,64,768]{2,1,0:T(8,128)(2,1)S(1)}, f16[4,64,768]{2,1,0:T(8,128)(2,1)S(1)}, u32[]{:S(2)}, u32[]{:S(2)}) collective-permute-start(f16[4,64,768]{2,1,0:T(8,128)(2,1)S(1)} %slice_convert_fusion.5), channel_id=1, source_target_pairs={{0,1},{1,0},{2,3},{3,2},{4,5},{5,4},{6,7},{7,6},{8,10},{9,11},{10,... | collective-permute-start | bytes 1179656 | tf_op jit(solution)/shard_map/ppermute | solution.py:257
  56.7 11.7 %collective-permute-start.13 = (f16[4,64,768]{2,1,0:T(8,128)(2,1)S(1)}, f16[4,64,768]{2,1,0:T(8,128)(2,1)S(1)}, u32[]{:S(2)}, u32[]{:S(2)}) collective-permute-start(f16[4,64,768]{2,1,0:T(8,128)(2,1)S(1)} %slice_convert_fusion.4), channel_id=1, source_target_pairs={{0,16},{1,17},{2,18},{3,19},{4,20},{5,21},{6,22},{7,23},{8,24},{9,... | collective-permute-start | bytes 1179656 | tf_op jit(solution)/shard_map/ppermute | solution.py:257
  58.6 11.2 %collective-permute-start.12 = (f16[4,64,768]{2,1,0:T(8,128)(2,1)S(1)}, f16[4,64,768]{2,1,0:T(8,128)(2,1)S(1)}, u32[]{:S(2)}, u32[]{:S(2)}) collective-permute-start(f16[4,64,768]{2,1,0:T(8,128)(2,1)S(1)} %slice_convert_fusion.3), channel_id=1, source_target_pairs={{0,1},{1,0},{2,3},{3,2},{4,5},{5,4},{6,7},{7,6},{8,10},{9,11},{10,... | collective-permute-start | bytes 1179656 | tf_op jit(solution)/shard_map/ppermute | solution.py:257
  59.7 11.9 %collective-permute-start.17 = (f16[2,64,768]{2,1,0:T(8,128)(2,1)S(1)}, f16[2,64,768]{2,1,0:T(8,128)(2,1)S(1)}, u32[]{:S(2)}, u32[]{:S(2)}) collective-permute-start(f16[2,64,768]{2,1,0:T(8,128)(2,1)S(1)} %slice_convert_fusion.8), channel_id=1, source_target_pairs={{0,2},{1,3},{2,0},{3,1},{4,6},{5,7},{6,4},{7,5},{8,24},{9,25},{10,... | collective-permute-start | bytes 589832 | tf_op jit(solution)/shard_map/ppermute | solution.py:257
  68.5 5.8 %collective-permute-start.16 = (f16[2,64,768]{2,1,0:T(8,128)(2,1)S(1)}, f16[2,64,768]{2,1,0:T(8,128)(2,1)S(1)}, u32[]{:S(2)}, u32[]{:S(2)}) collective-permute-start(f16[2,64,768]{2,1,0:T(8,128)(2,1)S(1)} %slice_convert_fusion.7), channel_id=1, source_target_pairs={{0,1},{1,0},{2,3},{3,2},{4,5},{5,4},{6,7},{7,6},{8,9},{9,8},{10,11... | collective-permute-start | bytes 589832 | tf_op jit(solution)/shard_map/ppermute | solution.py:257
  69.9 6.4 %collective-permute-start.15 = (f16[2,64,768]{2,1,0:T(8,128)(2,1)S(1)}, f16[2,64,768]{2,1,0:T(8,128)(2,1)S(1)}, u32[]{:S(2)}, u32[]{:S(2)}) collective-permute-start(f16[2,64,768]{2,1,0:T(8,128)(2,1)S(1)} %slice_convert_fusion.6), channel_id=1, source_target_pairs={{0,2},{1,3},{2,0},{3,1},{4,6},{5,7},{6,4},{7,5},{8,24},{9,25},{10,... | collective-permute-start | bytes 589832 | tf_op jit(solution)/shard_map/ppermute | solution.py:257
  71.7 13.0 %collective-permute-start.19 = (f16[1,64,768]{2,1,0:T(8,128)(2,1)S(1)}, f16[1,64,768]{2,1,0:T(8,128)(2,1)S(1)}, u32[]{:S(2)}, u32[]{:S(2)}) collective-permute-start(f16[1,64,768]{2,1,0:T(8,128)(2,1)S(1)} %slice_convert_fusion.11), channel_id=1, source_target_pairs={{0,4},{1,5},{2,6},{3,7},{4,0},{5,1},{6,2},{7,3},{8,12},{9,13},{10,... | collective-permute-start | bytes 294920 | tf_op jit(solution)/shard_map/ppermute | solution.py:22
  76.4 10.3 %collective-permute-start.18 = (f16[1,64,1536]{2,1,0:T(8,128)(2,1)S(1)}, f16[1,64,1536]{2,1,0:T(8,128)(2,1)S(1)}, u32[]{:S(2)}, u32[]{:S(2)}) collective-permute-start(f16[1,64,1536]{2,1,0:T(8,128)(2,1)S(1)} %pad_maximum_fusion.3), channel_id=1, source_target_pairs={{0,4},{1,5},{2,6},{3,7},{4,0},{5,1},{6,2},{7,3},{8,12},{9,13},{10,... | collective-permute-start | bytes 589832 | tf_op jit(solution)/shard_map/ppermute | solution.py:22

commit v8 on v7

--- a/solution.py
+++ b/solution.py
@@ -8,7 +8,7 @@
 from jax.sharding import PartitionSpec as P
 
 KERNEL_DILATION = 18
-CHANNELS_PER_STEP = 256
+CHANNELS_PER_STEP = 512
 F32, F16, BF16 = jnp.float32, jnp.float16, jnp.bfloat16
 
 
@@ -152,7 +152,7 @@
         ),
         out_shape=([] if turned else [turned_shape])
         + [jax.ShapeDtypeStruct(shape, F32) for shape in shapes],
-        compiler_params=pltpu.CompilerParams(vmem_limit_bytes=26 << 20),
+        compiler_params=pltpu.CompilerParams(vmem_limit_bytes=32 << 20),
         cost_estimate=pl.CostEstimate(
             flops=2 * pixels * channels * width,
             bytes_accessed=2 * pixels * channels + 4 * channels * width,
@@ -222,7 +222,7 @@
             pltpu.VMEM((width // 128, 9 * step, 128), F32),
             pltpu.VMEM((step, 9 * width), BF16),
         ],
-        compiler_params=pltpu.CompilerParams(vmem_limit_bytes=26 << 20),
+        compiler_params=pltpu.CompilerParams(vmem_limit_bytes=32 << 20),
         cost_estimate=pl.CostEstimate(
             flops=2 * pixels * 9 * width * step * count,
             bytes_accessed=2 * (9 * step * width + pixels * step) * count,

time: 88.1 us -> 88 us (level)
    ppermute x9, waiting for transfers between devices: 12.4 us -> 13.4 us  [exchange_by_role(): return lax.ppermute(value, ('dp', 'space'), pairs)]
where the time goes in v8:
time: 88 us; the launch traced here: 87.8 us
  Pallas kernels  34.1 us (39%)
  starting transfers between devices  27.4 us (31%)
  waiting for transfers between devices  16.2 us (18%)
  other arithmetic  6.05 us (7%)
  between operations  3.11 us (4%)
  local copies, waits for them, and re-layouts  0.89 us (1%)
    pallas_call x3, Pallas kernels, input_grad(): pl.pallas_call(functools.partial(input_grad_kernel, columns, cuts), grid=...  19.4 us
    pallas_call x3, Pallas kernels, kernel_term(): pl.pallas_call(functools.partial(kernel_term_kernel, columns, cuts, strea...  14.6 us
    ppermute x9, waiting for transfers between devices, exchange_by_role(): return lax.ppermute(value, ('dp', 'space'), pairs)  13.4 us
    ppermute x9, starting transfers between devices, exchange(): lax.ppermute(value, axis, [(i, i ^ bit) for i in range(lax.axis_size(axis...  13 us
    ppermute x9, starting transfers between devices, exchange_by_role(): return lax.ppermute(value, ('dp', 'space'), pairs)  11.9 us
    ppermute x2, starting transfers between devices, fetched(): return lax.ppermute(value, ('dp', 'space'), pairs)  2.58 us
    add x12, other arithmetic, add(): return part.astype(F32) + back.astype(F32)  2.29 us
    ppermute x9, waiting for transfers between devices, exchange(): lax.ppermute(value, axis, [(i, i ^ bit) for i in range(lax.axis_size(axis...  2.11 us
  transfers between devices with their start and end apart: 20, of which 9 were waited for; matrix products, arithmetic and copies ran while one was open for 7% of the time, Pallas kernels for 39%

profile of v8, /device:TPU:0, one launch (start us, length us, event | category | flops | bytes accessed | tf_op | source)
XLA Modules:
  0.0 87.8 jit_solution(15715248895114205793)
XLA Ops:
  1.1 1.1 %broadcast_select_fusion.4 = (bf16[1,6,72,256]{3,2,1,0:T(8,128)(2,1)S(1)}, bf16[1,6,72,256]{3,2,1,0:T(8,128)(2,1)S(1)}) fusion(pred[]{:T(512)S(6)} %eq.31, bf16[1,12,72,256]{3,2,1,0:T(8,128)(2,1)} %param.5), kind=kLoop, calls=%fused_computation.35 | loop fusion | flops 221184 | bytes 884737 | tf_op jit(solution)/shard_map/jit(_where)/select_n | solution.py:26
  2.9 1.3 %collective-permute-start.1 = (bf16[2,6,72,256]{3,2,1,0:T(8,128)(2,1)S(1)}, bf16[2,6,72,256]{3,2,1,0:T(8,128)(2,1)S(1)}, u32[]{:S(2)}, u32[]{:S(2)}) collective-permute-start(bf16[2,6,72,256]{3,2,1,0:T(8,128)(2,1)S(1)} %pad_maximum_fusion), channel_id=1, source_target_pairs={{1,0},{2,1},{3,2},{4,3},{5,4},{6,5},{7,6},{8,9},{9,10},{10,11},{11... | collective-permute-start | bytes 1327112 | tf_op jit(solution)/shard_map/ppermute | solution.py:41
  4.2 1.3 %collective-permute-start.2 = (bf16[2,6,72,256]{3,2,1,0:T(8,128)(2,1)S(1)}, bf16[2,6,72,256]{3,2,1,0:T(8,128)(2,1)S(1)}, u32[]{:S(2)}, u32[]{:S(2)}) collective-permute-start(bf16[2,6,72,256]{3,2,1,0:T(8,128)(2,1)S(1)} %pad_maximum_fusion.1), channel_id=1, source_target_pairs={{2,0},{3,1},{4,2},{5,3},{6,4},{7,5},{8,10},{9,11},{10,12},{11,13},... | collective-permute-start | bytes 1327112 | tf_op jit(solution)/shard_map/ppermute | solution.py:41
  6.2 6.2 %collective-permute-start.3 = (f32[1]{0:T(128)}, f32[1]{0:T(128)}, u32[]{:S(2)}, u32[]{:S(2)}) collective-permute-start(f32[1]{0:T(128)} %convert_element_type.89.scale_ref), channel_id=1, source_target_pairs={{0,8},{8,0},{16,24},{24,16},{1,9},{9,1},{17,25},{25,17},{2,10},{10... | collective-permute-start | bytes 20 | tf_op jit(solution)/shard_map/ppermute | solution.py:22
  12.4 5.9 %kernel_term.3 = (bf16[2,2,512,864]{3,2,1,0:T(8,128)(2,1)S(1)}, f32[16,64,768]{2,1,0:T(8,128)S(1)}, f32[16,64,768]{2,1,0:T(8,128)S(1)}) custom-call(s32[2]{0:T(128)S(1)} %pad_add_fusion.place_ref, f32[1]{0:T(128)} %convert_element_type.89.scale_ref, bf16[864,2048]{1,0:T(8,128)(2,1)} %bitcast.47, bf16[864,2048]{1,0:T(8,128)(2,1)} %bitcast.48, ...), custom_call_target="tpu_custom_call" | custom-call | flops 2717908992 | bytes 9830400 | tf_op jit(solution)/shard_map/kernel_term/pallas_call | solution.py:139
  20.9 2.8 %collective-permute-start.6 = (f32[1]{0:T(128)}, f32[1]{0:T(128)}, u32[]{:S(2)}, u32[]{:S(2)}) collective-permute-start(f32[1]{0:T(128)} %add.69), channel_id=1, source_target_pairs={{0,16},{8,24},{16,0},{24,8},{1,17},{9,25},{17,1},{25,9},{2,18},{10... | collective-permute-start | bytes 20 | tf_op jit(solution)/shard_map/ppermute | solution.py:22
  23.7 4.3 %kernel_term.4 = (f32[16,64,768]{2,1,0:T(8,128)S(1)}, f32[16,64,768]{2,1,0:T(8,128)S(1)}) custom-call(s32[2]{0:T(128)S(1)} %pad_add_fusion.place_ref, f32[1]{0:T(128)} %convert_element_type.89.scale_ref, bf16[2,2,512,864]{3,2,1,0:T(8,128)(2,1)S(1)} %get-tuple-element.55.refs_0_, bf16[432,256]{1,0:T(8,128)(2,1)S(1)} %bitcast.36, bf16[432,256]{1,0:T(8,128)(2,1)S(1)} %bitcast.35), custom_call_target="tpu_custom_call" | custom-call | flops 2717908992 | bytes 9830400 | tf_op jit(solution)/shard_map/kernel_term/pallas_call | solution.py:139
  29.1 4.5 %kernel_term.5 = (f32[16,64,768]{2,1,0:T(8,128)S(1)}, f32[16,64,768]{2,1,0:T(8,128)S(1)}) custom-call(s32[2]{0:T(128)S(1)} %pad_add_fusion.place_ref, f32[1]{0:T(128)} %convert_element_type.89.scale_ref, bf16[2,2,512,864]{3,2,1,0:T(8,128)(2,1)S(1)} %get-tuple-element.55.refs_0_, bf16[432,256]{1,0:T(8,128)(2,1)S(1)} %bitcast.38, bf16[432,256]{1,0:T(8,128)(2,1)S(1)} %bitcast.37), custom_call_target="tpu_custom_call" | custom-call | flops 2717908992 | bytes 9830400 | tf_op jit(solution)/shard_map/kernel_term/pallas_call | solution.py:139
  36.0 1.6 %collective-permute-start.10 = (f16[8,64,768]{2,1,0:T(8,128)(2,1)S(1)}, f16[8,64,768]{2,1,0:T(8,128)(2,1)S(1)}, u32[]{:S(2)}, u32[]{:S(2)}) collective-permute-start(f16[8,64,768]{2,1,0:T(8,128)(2,1)S(1)} %get-tuple-element.128), channel_id=1, source_target_pairs={{0,2},{1,3},{2,0},{3,1},{4,6},{5,7},{6,4},{7,5},{8,10},{9,11},{10,... | collective-permute-start | bytes 2359304 | tf_op jit(solution)/shard_map/ppermute | solution.py:257
  38.3 1.4 %collective-permute-start.9 = (f16[8,64,768]{2,1,0:T(8,128)(2,1)S(1)}, f16[8,64,768]{2,1,0:T(8,128)(2,1)S(1)}, u32[]{:S(2)}, u32[]{:S(2)}) collective-permute-start(f16[8,64,768]{2,1,0:T(8,128)(2,1)S(1)} %slice_convert_fusion.2), channel_id=1, source_target_pairs={{0,16},{1,17},{2,18},{3,19},{4,20},{5,21},{6,22},{7,23},{8,9},{9,8... | collective-permute-start | bytes 2359304 | tf_op jit(solution)/shard_map/ppermute | solution.py:257
  40.5 5.8 %input_grad.3 = (bf16[864,2048]{1,0:T(8,128)(2,1)}, bf16[864,2304]{1,0:T(8,128)(2,1)S(1)}) custom-call(f32[1]{0:T(128)S(6)} %div.7.scale_ref, bf16[432,256]{1,0:T(8,128)(2,1)S(1)} %bitcast.42, bf16[432,256]{1,0:T(8,128)(2,1)S(1)} %bitcast.41, bf16[864,256]{1,0:T(8,128)(2,1)} %bitcast.46, bf16[432,256]{1,0:T(8,128)(2,1)S(1)} %bitcast.40, ...), custom_call_target="tpu_custom_call" | custom-call | flops 2038431744 | bytes 3244032 | tf_op jit(solution)/shard_map/input_grad/pallas_call | solution.py:209
  46.3 1.2 %collective-permute-done.11 = f16[8,64,768]{2,1,0:T(8,128)(2,1)S(1)} collective-permute-done((f16[8,64,768]{2,1,0:T(8,128)(2,1)S(1)}, f16[8,64,768]{2,1,0:T(8,128)(2,1)S(1)}, u32[]{:S(2)}, u32[]{:S(2)}) %collective-permute-start.11) | collective-permute-done | bytes 786464 | tf_op jit(solution)/shard_map/ppermute | solution.py:257
  48.8 7.6 %collective-permute-done.10 = f16[8,64,768]{2,1,0:T(8,128)(2,1)S(1)} collective-permute-done((f16[8,64,768]{2,1,0:T(8,128)(2,1)S(1)}, f16[8,64,768]{2,1,0:T(8,128)(2,1)S(1)}, u32[]{:S(2)}, u32[]{:S(2)}) %collective-permute-start.10) | collective-permute-done | bytes 786464 | tf_op jit(solution)/shard_map/ppermute | solution.py:257
  56.7 1.7 %collective-permute-start.13 = (f16[4,64,768]{2,1,0:T(8,128)(2,1)S(1)}, f16[4,64,768]{2,1,0:T(8,128)(2,1)S(1)}, u32[]{:S(2)}, u32[]{:S(2)}) collective-permute-start(f16[4,64,768]{2,1,0:T(8,128)(2,1)S(1)} %slice_convert_fusion.4), channel_id=1, source_target_pairs={{0,16},{1,17},{2,18},{3,19},{4,20},{5,21},{6,22},{7,23},{8,24},{9,... | collective-permute-start | bytes 1179656 | tf_op jit(solution)/shard_map/ppermute | solution.py:257
  59.7 1.6 %collective-permute-start.17 = (f16[2,64,768]{2,1,0:T(8,128)(2,1)S(1)}, f16[2,64,768]{2,1,0:T(8,128)(2,1)S(1)}, u32[]{:S(2)}, u32[]{:S(2)}) collective-permute-start(f16[2,64,768]{2,1,0:T(8,128)(2,1)S(1)} %slice_convert_fusion.8), channel_id=1, source_target_pairs={{0,2},{1,3},{2,0},{3,1},{4,6},{5,7},{6,4},{7,5},{8,24},{9,25},{10,... | collective-permute-start | bytes 589832 | tf_op jit(solution)/shard_map/ppermute | solution.py:257
  61.4 5.4 %input_grad.4.refs_2_ = bf16[864,2048]{1,0:T(8,128)(2,1)} custom-call(f32[1]{0:T(128)S(6)} %div.7.scale_ref, bf16[864,2304]{1,0:T(8,128)(2,1)S(1)} %get-tuple-element.104.refs_0_, bf16[18432,256]{1,0:T(8,128)(2,1)} %refs_1_.3, bf16[864,2048]{1,0:T(8,128)(2,1)} %get-tuple-element.92.refs_2_), custom_call_target="tpu_custom_call", output_to_operand_aliasing={{}: (3, {})} | custom-call | flops 2038431744 | bytes 3244032 | tf_op jit(solution)/shard_map/input_grad/pallas_call | solution.py:209
  66.8 1.6 %collective-permute-done.13 = f16[4,64,768]{2,1,0:T(8,128)(2,1)S(1)} collective-permute-done((f16[4,64,768]{2,1,0:T(8,128)(2,1)S(1)}, f16[4,64,768]{2,1,0:T(8,128)(2,1)S(1)}, u32[]{:S(2)}, u32[]{:S(2)}) %collective-permute-start.13) | collective-permute-done | bytes 393248 | tf_op jit(solution)/shard_map/ppermute | solution.py:257
  68.5 1.3 %collective-permute-start.16 = (f16[2,64,768]{2,1,0:T(8,128)(2,1)S(1)}, f16[2,64,768]{2,1,0:T(8,128)(2,1)S(1)}, u32[]{:S(2)}, u32[]{:S(2)}) collective-permute-start(f16[2,64,768]{2,1,0:T(8,128)(2,1)S(1)} %slice_convert_fusion.7), channel_id=1, source_target_pairs={{0,1},{1,0},{2,3},{3,2},{4,5},{5,4},{6,7},{7,6},{8,9},{9,8},{10,11... | collective-permute-start | bytes 589832 | tf_op jit(solution)/shard_map/ppermute | solution.py:257
  69.9 1.7 %collective-permute-start.15 = (f16[2,64,768]{2,1,0:T(8,128)(2,1)S(1)}, f16[2,64,768]{2,1,0:T(8,128)(2,1)S(1)}, u32[]{:S(2)}, u32[]{:S(2)}) collective-permute-start(f16[2,64,768]{2,1,0:T(8,128)(2,1)S(1)} %slice_convert_fusion.6), channel_id=1, source_target_pairs={{0,2},{1,3},{2,0},{3,1},{4,6},{5,7},{6,4},{7,5},{8,24},{9,25},{10,... | collective-permute-start | bytes 589832 | tf_op jit(solution)/shard_map/ppermute | solution.py:257
  72.7 1.5 %collective-permute-done.16 = f16[2,64,768]{2,1,0:T(8,128)(2,1)S(1)} collective-permute-done((f16[2,64,768]{2,1,0:T(8,128)(2,1)S(1)}, f16[2,64,768]{2,1,0:T(8,128)(2,1)S(1)}, u32[]{:S(2)}, u32[]{:S(2)}) %collective-permute-start.16) | collective-permute-done | bytes 196640 | tf_op jit(solution)/shard_map/ppermute | solution.py:257
  74.3 1.4 %collective-permute-done.15 = f16[2,64,768]{2,1,0:T(8,128)(2,1)S(1)} collective-permute-done((f16[2,64,768]{2,1,0:T(8,128)(2,1)S(1)}, f16[2,64,768]{2,1,0:T(8,128)(2,1)S(1)}, u32[]{:S(2)}, u32[]{:S(2)}) %collective-permute-start.15) | collective-permute-done | bytes 196640 | tf_op jit(solution)/shard_map/ppermute | solution.py:257
  75.8 1.3 %collective-permute-start.18 = (f16[1,64,1536]{2,1,0:T(8,128)(2,1)S(1)}, f16[1,64,1536]{2,1,0:T(8,128)(2,1)S(1)}, u32[]{:S(2)}, u32[]{:S(2)}) collective-permute-start(f16[1,64,1536]{2,1,0:T(8,128)(2,1)S(1)} %pad_maximum_fusion.3), channel_id=1, source_target_pairs={{0,4},{1,5},{2,6},{3,7},{4,0},{5,1},{6,2},{7,3},{8,12},{9,13},{10,... | collective-permute-start | bytes 589832 | tf_op jit(solution)/shard_map/ppermute | solution.py:22
  77.1 8.3 %input_grad.5 = bf16[864,2048]{1,0:T(8,128)(2,1)} custom-call(f32[1]{0:T(128)S(6)} %div.7.scale_ref, bf16[864,2304]{1,0:T(8,128)(2,1)S(1)} %get-tuple-element.104.refs_0_, bf16[18432,256]{1,0:T(8,128)(2,1)} %refs_1_.3, bf16[864,2048]{1,0:T(8,128)(2,1)} %input_grad.4.refs_2_), custom_call_target="tpu_custom_call", output_to_operand_aliasing={{}: (3, {})} | custom-call | flops 4076863488 | bytes 6488064 | tf_op jit(solution)/shard_map/input_grad/pallas_call | solution.py:209
  85.3 1.4 %collective-permute-done.18 = f16[1,64,1536]{2,1,0:T(8,128)(2,1)S(1)} collective-permute-done((f16[1,64,1536]{2,1,0:T(8,128)(2,1)S(1)}, f16[1,64,1536]{2,1,0:T(8,128)(2,1)S(1)}, u32[]{:S(2)}, u32[]{:S(2)}) %collective-permute-start.18) | collective-permute-done | bytes 196640 | tf_op jit(solution)/shard_map/ppermute | solution.py:22
  (64 shorter events, 12.6 us)
Async XLA Ops:
  0.6 2.1 %collective-permute-start = (bf16[12,72,256]{2,1,0:T(8,128)(2,1)}, bf16[12,72,256]{2,1,0:T(8,128)(2,1)S(1)}, u32[]{:S(2)}, u32[]{:S(2)}) collective-permute-start(bf16[12,72,256]{2,1,0:T(8,128)(2,1)} %bitcast.44), channel_id=1, source_target_pairs={{0,8},{8,0},{16,24},{24,16},{1,9},{9,1},{17,25},{25,17},{2,10},{10... | collective-permute-start | bytes 1327112 | tf_op jit(solution)/shard_map/ppermute | solution.py:22
  2.9 16.6 %collective-permute-start.1 = (bf16[2,6,72,256]{3,2,1,0:T(8,128)(2,1)S(1)}, bf16[2,6,72,256]{3,2,1,0:T(8,128)(2,1)S(1)}, u32[]{:S(2)}, u32[]{:S(2)}) collective-permute-start(bf16[2,6,72,256]{3,2,1,0:T(8,128)(2,1)S(1)} %pad_maximum_fusion), channel_id=1, source_target_pairs={{1,0},{2,1},{3,2},{4,3},{5,4},{6,5},{7,6},{8,9},{9,10},{10,11},{11... | collective-permute-start | bytes 1327112 | tf_op jit(solution)/shard_map/ppermute | solution.py:41
  4.2 16.0 %collective-permute-start.2 = (bf16[2,6,72,256]{3,2,1,0:T(8,128)(2,1)S(1)}, bf16[2,6,72,256]{3,2,1,0:T(8,128)(2,1)S(1)}, u32[]{:S(2)}, u32[]{:S(2)}) collective-permute-start(bf16[2,6,72,256]{3,2,1,0:T(8,128)(2,1)S(1)} %pad_maximum_fusion.1), channel_id=1, source_target_pairs={{2,0},{3,1},{4,2},{5,3},{6,4},{7,5},{8,10},{9,11},{10,12},{11,13},... | collective-permute-start | bytes 1327112 | tf_op jit(solution)/shard_map/ppermute | solution.py:41
  6.2 12.6 %collective-permute-start.3 = (f32[1]{0:T(128)}, f32[1]{0:T(128)}, u32[]{:S(2)}, u32[]{:S(2)}) collective-permute-start(f32[1]{0:T(128)} %convert_element_type.89.scale_ref), channel_id=1, source_target_pairs={{0,8},{8,0},{16,24},{24,16},{1,9},{9,1},{17,25},{25,17},{2,10},{10... | collective-permute-start | bytes 20 | tf_op jit(solution)/shard_map/ppermute | solution.py:22
  20.2 8.3 %collective-permute-start.5 = (f16[16,64,768]{2,1,0:T(8,128)(2,1)S(1)}, f16[16,64,768]{2,1,0:T(8,128)(2,1)S(1)}, u32[]{:S(2)}, u32[]{:S(2)}) collective-permute-start(f16[16,64,768]{2,1,0:T(8,128)(2,1)S(1)} %convert_element_type.90), channel_id=1, source_target_pairs={{0,8},{8,0},{16,24},{24,16},{1,9},{9,1},{17,25},{25,17},{2,10},{10... | collective-permute-start | bytes 4718600 | tf_op jit(solution)/shard_map/ppermute | solution.py:22
  20.3 8.2 %collective-permute-start.4 = (bf16[2,6,72,256]{3,2,1,0:T(8,128)(2,1)S(1)}, bf16[2,6,72,256]{3,2,1,0:T(8,128)(2,1)S(1)}, u32[]{:S(2)}, u32[]{:S(2)}) collective-permute-start(bf16[2,6,72,256]{3,2,1,0:T(8,128)(2,1)S(1)} %pad_maximum_fusion.2), channel_id=1, source_target_pairs={{0,8},{8,0},{16,24},{24,16},{1,9},{9,1},{17,25},{25,17},{2,10},{10... | collective-permute-start | bytes 1327112 | tf_op jit(solution)/shard_map/ppermute | solution.py:22
  20.9 7.6 %collective-permute-start.6 = (f32[1]{0:T(128)}, f32[1]{0:T(128)}, u32[]{:S(2)}, u32[]{:S(2)}) collective-permute-start(f32[1]{0:T(128)} %add.69), channel_id=1, source_target_pairs={{0,16},{8,24},{16,0},{24,8},{1,17},{9,25},{17,1},{25,9},{2,18},{10... | collective-permute-start | bytes 20 | tf_op jit(solution)/shard_map/ppermute | solution.py:22
  28.5 5.6 %collective-permute-start.7 = (f16[16,64,768]{2,1,0:T(8,128)(2,1)S(1)}, f16[16,64,768]{2,1,0:T(8,128)(2,1)S(1)}, u32[]{:S(2)}, u32[]{:S(2)}) collective-permute-start(f16[16,64,768]{2,1,0:T(8,128)(2,1)S(1)} %convert_element_type.92), channel_id=1, source_target_pairs={{0,8},{8,0},{16,24},{24,16},{1,9},{9,1},{17,25},{25,17},{2,10},{10... | collective-permute-start | bytes 4718600 | tf_op jit(solution)/shard_map/ppermute | solution.py:22
  34.1 3.6 %collective-permute-start.8 = (f16[16,64,768]{2,1,0:T(8,128)(2,1)S(1)}, f16[16,64,768]{2,1,0:T(8,128)(2,1)S(1)}, u32[]{:S(2)}, u32[]{:S(2)}) collective-permute-start(f16[16,64,768]{2,1,0:T(8,128)(2,1)S(1)} %convert_element_type.97), channel_id=1, source_target_pairs={{0,8},{8,0},{16,24},{24,16},{1,9},{9,1},{17,25},{25,17},{2,10},{10... | collective-permute-start | bytes 4718600 | tf_op jit(solution)/shard_map/ppermute | solution.py:22
  35.4 12.1 %collective-permute-start.11 = (f16[8,64,768]{2,1,0:T(8,128)(2,1)S(1)}, f16[8,64,768]{2,1,0:T(8,128)(2,1)S(1)}, u32[]{:S(2)}, u32[]{:S(2)}) collective-permute-start(f16[8,64,768]{2,1,0:T(8,128)(2,1)S(1)} %get-tuple-element.127), channel_id=1, source_target_pairs={{0,16},{1,17},{2,18},{3,19},{4,20},{5,21},{6,22},{7,23},{8,9},{9,8... | collective-permute-start | bytes 2359304 | tf_op jit(solution)/shard_map/ppermute | solution.py:257
  36.0 20.4 %collective-permute-start.10 = (f16[8,64,768]{2,1,0:T(8,128)(2,1)S(1)}, f16[8,64,768]{2,1,0:T(8,128)(2,1)S(1)}, u32[]{:S(2)}, u32[]{:S(2)}) collective-permute-start(f16[8,64,768]{2,1,0:T(8,128)(2,1)S(1)} %get-tuple-element.128), channel_id=1, source_target_pairs={{0,2},{1,3},{2,0},{3,1},{4,6},{5,7},{6,4},{7,5},{8,10},{9,11},{10,... | collective-permute-start | bytes 2359304 | tf_op jit(solution)/shard_map/ppermute | solution.py:257
  38.3 20.1 %collective-permute-start.9 = (f16[8,64,768]{2,1,0:T(8,128)(2,1)S(1)}, f16[8,64,768]{2,1,0:T(8,128)(2,1)S(1)}, u32[]{:S(2)}, u32[]{:S(2)}) collective-permute-start(f16[8,64,768]{2,1,0:T(8,128)(2,1)S(1)} %slice_convert_fusion.2), channel_id=1, source_target_pairs={{0,16},{1,17},{2,18},{3,19},{4,20},{5,21},{6,22},{7,23},{8,9},{9,8... | collective-permute-start | bytes 2359304 | tf_op jit(solution)/shard_map/ppermute | solution.py:257
  47.8 11.8 %collective-permute-start.14 = (f16[4,64,768]{2,1,0:T(8,128)(2,1)S(1)}, f16[4,64,768]{2,1,0:T(8,128)(2,1)S(1)}, u32[]{:S(2)}, u32[]{:S(2)}) collective-permute-start(f16[4,64,768]{2,1,0:T(8,128)(2,1)S(1)} %slice_convert_fusion.5), channel_id=1, source_target_pairs={{0,1},{1,0},{2,3},{3,2},{4,5},{5,4},{6,7},{7,6},{8,10},{9,11},{10,... | collective-permute-start | bytes 1179656 | tf_op jit(solution)/shard_map/ppermute | solution.py:257
  56.7 11.7 %collective-permute-start.13 = (f16[4,64,768]{2,1,0:T(8,128)(2,1)S(1)}, f16[4,64,768]{2,1,0:T(8,128)(2,1)S(1)}, u32[]{:S(2)}, u32[]{:S(2)}) collective-permute-start(f16[4,64,768]{2,1,0:T(8,128)(2,1)S(1)} %slice_convert_fusion.4), channel_id=1, source_target_pairs={{0,16},{1,17},{2,18},{3,19},{4,20},{5,21},{6,22},{7,23},{8,24},{9,... | collective-permute-start | bytes 1179656 | tf_op jit(solution)/shard_map/ppermute | solution.py:257
  58.6 11.2 %collective-permute-start.12 = (f16[4,64,768]{2,1,0:T(8,128)(2,1)S(1)}, f16[4,64,768]{2,1,0:T(8,128)(2,1)S(1)}, u32[]{:S(2)}, u32[]{:S(2)}) collective-permute-start(f16[4,64,768]{2,1,0:T(8,128)(2,1)S(1)} %slice_convert_fusion.3), channel_id=1, source_target_pairs={{0,1},{1,0},{2,3},{3,2},{4,5},{5,4},{6,7},{7,6},{8,10},{9,11},{10,... | collective-permute-start | bytes 1179656 | tf_op jit(solution)/shard_map/ppermute | solution.py:257
  59.7 11.9 %collective-permute-start.17 = (f16[2,64,768]{2,1,0:T(8,128)(2,1)S(1)}, f16[2,64,768]{2,1,0:T(8,128)(2,1)S(1)}, u32[]{:S(2)}, u32[]{:S(2)}) collective-permute-start(f16[2,64,768]{2,1,0:T(8,128)(2,1)S(1)} %slice_convert_fusion.8), channel_id=1, source_target_pairs={{0,2},{1,3},{2,0},{3,1},{4,6},{5,7},{6,4},{7,5},{8,24},{9,25},{10,... | collective-permute-start | bytes 589832 | tf_op jit(solution)/shard_map/ppermute | solution.py:257
  68.5 5.7 %collective-permute-start.16 = (f16[2,64,768]{2,1,0:T(8,128)(2,1)S(1)}, f16[2,64,768]{2,1,0:T(8,128)(2,1)S(1)}, u32[]{:S(2)}, u32[]{:S(2)}) collective-permute-start(f16[2,64,768]{2,1,0:T(8,128)(2,1)S(1)} %slice_convert_fusion.7), channel_id=1, source_target_pairs={{0,1},{1,0},{2,3},{3,2},{4,5},{5,4},{6,7},{7,6},{8,9},{9,8},{10,11... | collective-permute-start | bytes 589832 | tf_op jit(solution)/shard_map/ppermute | solution.py:257
  69.9 5.7 %collective-permute-start.15 = (f16[2,64,768]{2,1,0:T(8,128)(2,1)S(1)}, f16[2,64,768]{2,1,0:T(8,128)(2,1)S(1)}, u32[]{:S(2)}, u32[]{:S(2)}) collective-permute-start(f16[2,64,768]{2,1,0:T(8,128)(2,1)S(1)} %slice_convert_fusion.6), channel_id=1, source_target_pairs={{0,2},{1,3},{2,0},{3,1},{4,6},{5,7},{6,4},{7,5},{8,24},{9,25},{10,... | collective-permute-start | bytes 589832 | tf_op jit(solution)/shard_map/ppermute | solution.py:257
  71.7 13.6 %collective-permute-start.19 = (f16[1,64,768]{2,1,0:T(8,128)(2,1)S(1)}, f16[1,64,768]{2,1,0:T(8,128)(2,1)S(1)}, u32[]{:S(2)}, u32[]{:S(2)}) collective-permute-start(f16[1,64,768]{2,1,0:T(8,128)(2,1)S(1)} %slice_convert_fusion.11), channel_id=1, source_target_pairs={{0,4},{1,5},{2,6},{3,7},{4,0},{5,1},{6,2},{7,3},{8,12},{9,13},{10,... | collective-permute-start | bytes 294920 | tf_op jit(solution)/shard_map/ppermute | solution.py:22
  75.8 10.9 %collective-permute-start.18 = (f16[1,64,1536]{2,1,0:T(8,128)(2,1)S(1)}, f16[1,64,1536]{2,1,0:T(8,128)(2,1)S(1)}, u32[]{:S(2)}, u32[]{:S(2)}) collective-permute-start(f16[1,64,1536]{2,1,0:T(8,128)(2,1)S(1)} %pad_maximum_fusion.3), channel_id=1, source_target_pairs={{0,4},{1,5},{2,6},{3,7},{4,0},{5,1},{6,2},{7,3},{8,12},{9,13},{10,... | collective-permute-start | bytes 589832 | tf_op jit(solution)/shard_map/ppermute | solution.py:22
